TPU v7x, 32 devices: a whole 2x2x4 slice. The times are simulated.
32 devices in a mesh: node: 8 (over z, core), rep: 4 (over y, x).
Axes of the slice: x: 2, y: 2, z: 4, core: 2. Of those that a mesh axis runs over, the one named last changes fastest.
Arguments:
- aggregated: bfloat16 [8192, 512], P(('node', 'rep')), may hold values from -6 to 6
- cotangent: bfloat16 [8192, 512], P(('node', 'rep')), may hold values from -6 to 6
- kernel_in: bfloat16 [512, 2048], P(None, 'rep'), may hold values from -0.25 to 0.25
- kernel_out: bfloat16 [2048, 512], P('rep'), may hold values from -0.125 to 0.125
- tile_values: bfloat16 [32, 4, 256, 256], P(('node', 'rep')), may hold values from -0.5 to 0.5
- tile_cols: int32 [32, 4], P(('node', 'rep')), may hold values from 0 to 2, as said below
- tile_count: int32 [32], P(('node', 'rep')), may hold values from 1 to 4, as said below
Outputs:
- grad_nodes: bfloat16 [8192, 512], P(('node', 'rep'))
- grad_in: float32 [512, 2048], P(None, 'rep')
- grad_out: float32 [2048, 512], P('rep')
Inputs may be any that keep to these rules, and one draw needn't show every extreme that they name: tile_cols 0, 1 and 2 name the block of the previous cycle position with the same rep index, the block itself and that of the next cycle position; slots at or past tile_count are ignored. `tile_count`: some block row has all 4 slots live.
All inputs are finite; a program needn't handle non-finite values.
Results may differ from a plain program's by a relative error of at most 0.024.
Values may be sent and summed in bfloat16 or wider, within the bound.
No kernel may reach another device: no remote copies, remote signals or barrier semaphores. Data moves between devices by JAX's collectives and lax.ppermute only.
A program may use at most 64 MiB of HBM per device.

v0:
```python
import math

import jax
import jax.numpy as jnp
from jax import lax
from jax.sharding import PartitionSpec as P


def with_halo(block, sides, width):
    for axis, dim in sides:
        count = lax.axis_size(axis)
        forward = [(i, i + 1) for i in range(count - 1)]
        forward.append((count - 1, 0))
        backward = [(target, source) for source, target in forward]
        low = lax.ppermute(
            lax.slice_in_dim(block, block.shape[dim] - width, None, axis=dim), axis, forward
        )
        high = lax.ppermute(lax.slice_in_dim(block, 0, width, axis=dim), axis, backward)
        block = jnp.concatenate([low, block, high], axis=dim)
    return block


def gelu_value(pre_act):
    inner = math.sqrt(2.0 / math.pi) * (pre_act + 0.044715 * pre_act * pre_act * pre_act)
    return 0.5 * pre_act * (1.0 + jnp.tanh(inner))


def gelu_slope(pre_act):
    inner = math.sqrt(2.0 / math.pi) * (pre_act + 0.044715 * pre_act * pre_act * pre_act)
    tanh_val = jnp.tanh(inner)
    return 0.5 * (1.0 + tanh_val) + 0.5 * pre_act * (1.0 - tanh_val * tanh_val) * math.sqrt(
        2.0 / math.pi
    ) * (1.0 + 3.0 * 0.044715 * pre_act * pre_act)


def contract_last(left, right):
    return lax.dot_general(
        left, right, (((1,), (1,)), ((), ())), preferred_element_type=jnp.float32
    )


def contract_first(left, right):
    return lax.dot_general(
        left, right, (((0,), (0,)), ((), ())), preferred_element_type=jnp.float32
    )


def local(aggregated, cotangent, kernel_in, kernel_out, tile_values, tile_cols, tile_count):
    row_count = aggregated.shape[0]
    group_size = lax.axis_size("rep")
    norm_factor = 1.0 / math.sqrt(row_count * lax.axis_size("node") * group_size)
    agg_piece = lax.all_gather(aggregated, "rep", axis=0, tiled=True)
    cot_piece = lax.all_gather(cotangent, "rep", axis=0, tiled=True)
    pre_act = jnp.dot(agg_piece, kernel_in, preferred_element_type=jnp.float32)
    act_out = gelu_value(pre_act).astype(jnp.bfloat16)
    grad_act = contract_last(cot_piece, kernel_out)
    grad_pre = (grad_act * gelu_slope(pre_act)).astype(jnp.bfloat16)
    sum_out = contract_first(act_out, cot_piece)
    sum_in = contract_first(agg_piece, grad_pre)
    sum_in, sum_out, hidden_buf = (sum_in, sum_out, grad_pre)
    grad_agg = lax.psum_scatter(
        contract_last(hidden_buf, kernel_in).astype(jnp.bfloat16),
        "rep",
        scatter_dimension=0,
        tiled=True,
    )
    total_in, total_out = lax.psum((sum_in, sum_out), "node")
    grad_in = total_in * norm_factor
    grad_out = total_out * norm_factor
    tiles = tile_values[0]
    slot_cols = tile_cols[0]
    slot_ids = jnp.arange(tiles.shape[0], dtype=jnp.int32)
    live = slot_ids < tile_count[0]
    terms = jnp.einsum("trc,rd->tcd", tiles, grad_agg, preferred_element_type=jnp.float32)
    targets = jnp.arange(3, dtype=jnp.int32)
    select = ((slot_cols[None, :] == targets[:, None]) & live[None, :]).astype(jnp.float32)
    by_target = jnp.einsum("kt,tcd->kcd", select, terms)
    outgoing = jnp.concatenate([by_target[0], by_target[2]], axis=0)
    padded = with_halo(outgoing.astype(jnp.bfloat16), (("node", 0),), row_count).astype(
        outgoing.dtype
    )
    from_left = padded[:row_count]
    from_right = padded[3 * row_count :]
    grad_nodes = (cotangent.astype(jnp.float32) + by_target[1] + from_left + from_right).astype(
        jnp.bfloat16
    )
    return (grad_nodes, grad_in, grad_out)


def solution(mesh):
    return jax.shard_map(
        local,
        mesh=mesh,
        in_specs=(
            P(("node", "rep"), None),
            P(("node", "rep"), None),
            P(None, "rep"),
            P("rep", None),
            P(("node", "rep"), None, None, None),
            P(("node", "rep"), None),
            P(("node", "rep")),
        ),
        out_specs=(P(("node", "rep"), None), P(None, "rep"), P("rep", None)),
        check_vma=False,
    )
```

profile of v0, /device:TPU:0, one launch (start us, length us, event | category | flops | bytes accessed | tf_op | source)
XLA Modules:
  0.0 186.5 jit_solution(17916311549348831739)
XLA Ops:
  7.2 0.0 copy-start
  7.2 0.0 all-gather.5.cloned.1.call-start
  7.2 0.7 all-gather.5.cloned.1.call-update
  7.9 0.0 all-gather.3.cloned.1.call-start
  8.0 0.7 all-gather.3.cloned.1.call-update
  8.7 0.0 reduce-scatter.2.cloned.1.call-start
  8.7 30.5 %all-gather.5.cloned.1.call-done = bf16[1024,512]{1,0:T(8,128)(2,1)} async-done(((bf16[256,512]{1,0:T(8,128)(2,1)}), bf16[1024,512]{1,0:T(8,128)(2,1)}) %all-gather.5.cloned.1.call-update) | async-done | bytes 1048592 | tf_op jit(solution)/shard_map/all_gather | solution.py:52
  39.2 1.9 %fusion.24 = f32[1024,512]{1,0:T(8,128)S(1)} fusion(bf16[1024,512]{1,0:T(8,128)(2,1)} %all-gather.5.cloned.1.call-done, bf16[512,512]{1,0:T(8,128)(2,1)S(1)} %copy-done), kind=kOutput, calls=%fused_computation.40 | convolution fusion | flops 536870912 | bytes 3670016 | tf_op jit(solution)/shard_map/dot_general | solution.py:54
  41.2 26.6 %all-gather.3.cloned.1.call-done = bf16[1024,512]{1,0:T(8,128)(2,1)} async-done(((bf16[256,512]{1,0:T(8,128)(2,1)}), bf16[1024,512]{1,0:T(8,128)(2,1)}) %all-gather.3.cloned.1.call-update) | async-done | bytes 1048592 | tf_op jit(solution)/shard_map/all_gather | solution.py:53
  67.7 2.9 %fusion.6 = bf16[1024,512]{1,0:T(8,128)(2,1)S(1)} fusion(f32[1024,512]{1,0:T(8,128)S(1)} %fusion.24, bf16[1024,512]{1,0:T(8,128)(2,1)} %all-gather.3.cloned.1.call-done, bf16[512,512]{1,0:T(8,128)(2,1)S(1)} %copy-done.5), kind=kOutput, calls=%fused_computation.8 | convolution fusion | flops 546832384 | bytes 4718592 | tf_op jit(solution)/shard_map/dot_general | solution.py:37
  70.7 0.0 copy-start.6
  70.7 1.0 copy-done.6
  71.6 1.7 convolution_convert_fusion
  73.4 0.0 reduce-scatter.2.cloned.1.call-update
  73.4 0.0 all-reduce.3.cloned.1.call-start
  73.4 3.3 %convolution_bitcast_fusion.1 = f32[512,512]{0,1:T(8,128)} fusion(bf16[1024,512]{1,0:T(8,128)(2,1)} %copy-done.6, bf16[1024,512]{1,0:T(8,128)(2,1)} %all-gather.5.cloned.1.call-done), kind=kOutput, calls=%fused_computation.12 | convolution fusion | flops 536870912 | bytes 3145728 | tf_op jit(solution)/shard_map/dot_general | solution.py:43
  76.8 2.0 %fusion.7 = f32[512,512]{0,1:T(8,128)} fusion(bf16[1024,512]{1,0:T(8,128)(2,1)S(1)} %copy-done.4, f32[1024,512]{1,0:T(8,128)S(1)} %fusion.24), kind=kOutput, calls=%fused_computation.13 | convolution fusion | flops 541589504 | bytes 4194304 | tf_op jit(solution)/shard_map/dot_general | solution.py:43
  78.8 0.0 all-reduce.3.cloned.1.call-update
  78.8 0.0 copy-start.3
  79.6 21.7 %reduce-scatter.2.cloned.1.call-done = bf16[256,512]{1,0:T(8,128)(2,1)} async-done(((bf16[1024,512]{1,0:T(8,128)(2,1)}), bf16[256,512]{1,0:T(8,128)(2,1)}) %reduce-scatter.2.cloned.1.call-update) | async-done | bytes 262160 | tf_op jit(solution)/shard_map/reduce_scatter | solution.py:61
  101.3 1.4 convolution_bitcast_fusion
  102.7 1.0 copy.20
  103.7 2.1 %fusion.23 = (bf16[3,256,512]{2,0,1:T(4,128)(2,1)S(1)}, f32[3,256,512]{2,0,1:T(4,128)}) fusion(bf16[4,256,512]{2,0,1:T(4,128)(2,1)S(1)} %copy.20, s32[4]{0:T(128)S(1)} %bitcast.42, pred[4]{0:T(512)(128)(4,1)S(1)} %iota_compare_fusion.1), kind=kOutput, calls=%fused_computation.39 | convolution fusion | flops 3538968 | bytes 3407892 | tf_op jit(solution)/shard_map/kt,tcd->kcd/dot_general | solution.py:77
  105.8 0.7 fusion.22
  106.6 2.8 %collective-permute-start.1 = (bf16[256,512]{1,0:T(8,128)(2,1)S(1)}, bf16[256,512]{1,0:T(8,128)(2,1)S(1)}, u32[]{:S(2)}, u32[]{:S(2)}) collective-permute-start(bf16[256,512]{1,0:T(8,128)(2,1)S(1)} %bitcast.40), channel_id=1, source_target_pairs={{4,0},{8,4},{12,8},{16,12},{20,16},{24,20},{28,24},{0,28},{5,1},{9... | collective-permute-start | bytes 786440 | tf_op jit(solution)/shard_map/ppermute | solution.py:18
  109.5 0.0 collective-permute-start
  109.5 62.1 %all-reduce.3.cloned.1.call-done = (f32[512,512]{0,1:T(8,128)}, f32[512,512]{0,1:T(8,128)}) async-done(((f32[512,512]{0,1:T(8,128)}, f32[512,512]{0,1:T(8,128)}), (f32[512,512]{0,1:T(8,128)}, f32[512,512]{0,1:T(8,128)})) %all-reduce.3.cloned.1.call-update) | async-done | bytes 2097168 | tf_op jit(solution)/shard_map/psum | solution.py:67
  171.6 1.8 broadcast_multiply_fusion
  173.3 1.3 copy.23
  174.7 1.3 copy.22
  176.0 2.1 %slice.24 = f32[1,256,512]{2,0,1:T(1,128)S(1)} slice(f32[3,256,512]{2,0,1:T(4,128)} %get-tuple-element.17), slice={[1:2], [0:256], [0:512]} | slice | bytes 1048576 | tf_op jit(solution)/shard_map/slice | solution.py:84
  178.1 1.8 fusion.9
  (15 shorter events, 0.1 us)
Async XLA Ops:
  7.2 32.1 %copy-start = (bf16[512,512]{1,0:T(8,128)(2,1)S(1)}, bf16[512,512]{1,0:T(8,128)(2,1)}, u32[]{:S(2)}) copy-start(bf16[512,512]{1,0:T(8,128)(2,1)} %param.9) | copy-start | bytes 1572868
  7.2 60.6 %copy-start.5 = (bf16[512,512]{1,0:T(8,128)(2,1)S(1)}, bf16[512,512]{1,0:T(8,128)(2,1)}, u32[]{:S(2)}) copy-start(bf16[512,512]{1,0:T(8,128)(2,1)} %param.10) | copy-start | bytes 1572868
  7.2 32.0 %all-gather.5.cloned.1.call-start = ((), (), s32[]{:S(2)}) async-start(), calls=%async_computation.2 | async-start | bytes 1310720 | tf_op jit(solution)/shard_map/all_gather | solution.py:52
  7.9 59.8 %all-gather.3.cloned.1.call-start = ((), (), s32[]{:S(2)}) async-start(), calls=%async_computation.1 | async-start | bytes 1310720 | tf_op jit(solution)/shard_map/all_gather | solution.py:53
  8.7 92.6 %reduce-scatter.2.cloned.1.call-start = ((), (), s32[]{:S(2)}) async-start(), calls=%async_computation.3 | async-start | bytes 1310720 | tf_op jit(solution)/shard_map/reduce_scatter | solution.py:61
  70.7 1.0 copy-start.6
  73.4 98.2 %all-reduce.3.cloned.1.call-start = ((), (), s32[]{:S(2)}) async-start(), calls=%async_computation.4 | async-start | bytes 4194304 | tf_op jit(solution)/shard_map/psum | solution.py:67
  73.4 3.4 %copy-start.4 = (bf16[1024,512]{1,0:T(8,128)(2,1)S(1)}, bf16[1024,512]{1,0:T(8,128)(2,1)}, u32[]{:S(2)}) copy-start(bf16[1024,512]{1,0:T(8,128)(2,1)} %all-gather.3.cloned.1.call-done) | copy-start | bytes 3145732
  78.8 22.4 %copy-start.2 = (bf16[1,4,256,256]{3,2,1,0:T(8,128)(2,1)S(1)}, bf16[1,4,256,256]{3,2,1,0:T(8,128)(2,1)}, u32[]{:S(2)}) copy-start(bf16[1,4,256,256]{3,2,1,0:T(8,128)(2,1)} %param.11) | copy-start | bytes 1572868
  78.8 24.9 %copy-start.3 = (s32[1,4]{1,0:T(1,128)S(1)}, s32[1,4]{1,0:T(1,128)}, u32[]{:S(2)}) copy-start(s32[1,4]{1,0:T(1,128)} %param.12) | copy-start | bytes 52
  106.6 71.5 %collective-permute-start.1 = (bf16[256,512]{1,0:T(8,128)(2,1)S(1)}, bf16[256,512]{1,0:T(8,128)(2,1)S(1)}, u32[]{:S(2)}, u32[]{:S(2)}) collective-permute-start(bf16[256,512]{1,0:T(8,128)(2,1)S(1)} %bitcast.40), channel_id=1, source_target_pairs={{4,0},{8,4},{12,8},{16,12},{20,16},{24,20},{28,24},{0,28},{5,1},{9... | collective-permute-start | bytes 786440 | tf_op jit(solution)/shard_map/ppermute | solution.py:18
  109.5 68.6 %collective-permute-start = (bf16[256,512]{1,0:T(8,128)(2,1)S(1)}, bf16[256,512]{1,0:T(8,128)(2,1)}, u32[]{:S(2)}, u32[]{:S(2)}) collective-permute-start(bf16[256,512]{1,0:T(8,128)(2,1)S(1)} %bitcast.38), channel_id=1, source_target_pairs={{0,4},{4,8},{8,12},{12,16},{16,20},{20,24},{24,28},{28,0},{1,5},{5... | collective-permute-start | bytes 786440 | tf_op jit(solution)/shard_map/ppermute | solution.py:15
  174.7 3.5 %copy-start.1 = (bf16[256,512]{1,0:T(8,128)(2,1)S(1)}, bf16[256,512]{1,0:T(8,128)(2,1)}, u32[]{:S(2)}) copy-start(bf16[256,512]{1,0:T(8,128)(2,1)} %param.8) | copy-start | bytes 786436
Sparse Core Ops, SparseCore 0:
  9.9 29.3 all-gather.4
  41.1 26.6 all-gather.2
  73.5 27.7 reduce-scatter.1
  104.2 67.2 all-reduce.2
where the time goes:
time: 187 us; the launch traced here: 186 us
  waiting for transfers between devices  142 us (76%)
  matrix products  15.5 us (8%)
  between operations  14.6 us (8%)
  local copies, waits for them, and re-layouts  7.56 us (4%)
  other arithmetic  3.6 us (2%)
  starting transfers between devices  2.98 us (2%)
    psum x1, waiting for transfers between devices, local(): total_in, total_out = lax.psum((sum_in, sum_out), 'node')  62.1 us
    all_gather x1, waiting for transfers between devices, local(): agg_piece = lax.all_gather(aggregated, 'rep', axis=0, tiled=True)  30.5 us
    all_gather x1, waiting for transfers between devices, local(): cot_piece = lax.all_gather(cotangent, 'rep', axis=0, tiled=True)  26.6 us
    reduce_scatter x1, waiting for transfers between devices, local(): lax.psum_scatter(contract_last(hidden_buf, kernel_in).astype(jnp.bfloat16...  21.7 us
    dot_general x2, matrix products, contract_first(): lax.dot_general(left, right, (((0,), (0,)), ((), ())), preferred_element_...  5.38 us
    dot_general x2, matrix products, contract_last(): lax.dot_general(left, right, (((1,), (1,)), ((), ())), preferred_element_...  4.65 us
  transfers between devices with their start and end apart: 6, of which 4 were waited for; matrix products, arithmetic and copies ran while one was open for 10% of the time, Pallas kernels for 0%

commit v1 on v0

v1 whole, which is shorter than its diff:
```python
import math

import jax
import jax.numpy as jnp
from jax import lax
from jax.sharding import PartitionSpec as P

BF16 = jnp.bfloat16
F32 = jnp.float32


def gelu_both(pre_act):
    root = math.sqrt(2.0 / math.pi)
    inner = root * (pre_act + 0.044715 * pre_act * pre_act * pre_act)
    tanh_val = jnp.tanh(inner)
    value = 0.5 * pre_act * (1.0 + tanh_val)
    slope = 0.5 * (1.0 + tanh_val) + 0.5 * pre_act * (1.0 - tanh_val * tanh_val) * root * (
        1.0 + 3.0 * 0.044715 * pre_act * pre_act
    )
    return value, slope


def contract_last(left, right):
    return lax.dot_general(left, right, (((1,), (1,)), ((), ())), preferred_element_type=F32)


def contract_first(left, right):
    return lax.dot_general(left, right, (((0,), (0,)), ((), ())), preferred_element_type=F32)


def swap(block, axis, mask):
    count = lax.axis_size(axis)
    return lax.ppermute(block, axis, [(i, i ^ mask) for i in range(count)])


def shift(block, axis, step):
    count = lax.axis_size(axis)
    return lax.ppermute(block, axis, [(i, (i + step) % count) for i in range(count)])


def over_groups(piece):
    groups = lax.axis_size("node") // 4
    if groups == 2:
        return piece.astype(F32) + swap(piece, "node", 4).astype(F32)
    pieces = jnp.stack([piece] + [shift(piece, "node", 4 * s) for s in range(1, groups)])
    group = lax.axis_index("node") // 4
    ordered = jnp.roll(pieces[::-1], group + 1, axis=0)
    total = jnp.zeros(piece.shape, F32)
    for s in range(groups):
        total = total + ordered[s].astype(F32)
    return total


def local(aggregated, cotangent, kernel_in, kernel_out, tile_values, tile_cols, tile_count):
    rows = aggregated.shape[0]
    reps = lax.axis_size("rep")
    norm_factor = 1.0 / math.sqrt(rows * lax.axis_size("node") * reps)
    quarter = kernel_out.shape[0] // 4
    me = lax.axis_index("node") % 4

    agg_z = swap(aggregated, "node", 2)
    cot_z = swap(cotangent, "node", 2)
    kin = lax.dynamic_slice_in_dim(kernel_in, me * quarter, quarter, axis=1)
    kout = lax.dynamic_slice_in_dim(kernel_out, me * quarter, quarter, axis=0)
    kins = [kin] + [swap(kin, "rep", s) for s in range(1, reps)]
    kouts = [kout] + [swap(kout, "rep", s) for s in range(1, reps)]
    agg_c = swap(aggregated, "node", 1)
    cot_c = swap(cotangent, "node", 1)
    agg_zc = swap(agg_z, "node", 1)
    cot_zc = swap(cot_z, "node", 1)
    agg = jnp.concatenate([aggregated, agg_c, agg_z, agg_zc], axis=0)
    cot = jnp.concatenate([cotangent, cot_c, cot_z, cot_zc], axis=0)
    w_in = jnp.concatenate(kins, axis=1)
    w_out = jnp.concatenate(kouts, axis=0)

    pre_act = jnp.dot(agg, w_in, preferred_element_type=F32)
    value, slope = gelu_both(pre_act)
    act_out = value.astype(BF16)
    part_out = contract_first(act_out, cot).astype(BF16)
    grad_act = contract_last(cot, w_out)
    grad_pre = (grad_act * slope).astype(BF16)
    part_in = contract_first(agg, grad_pre).astype(BF16)

    def to_owner(pieces):
        total = pieces[0].astype(F32)
        for s in range(1, reps):
            total = total + swap(pieces[s], "rep", s).astype(F32)
        return total.astype(BF16)

    def gathered(mine, axis):
        z_piece = swap(mine, "node", 2)
        pieces = [mine, swap(mine, "node", 1), z_piece, swap(z_piece, "node", 1)]
        shape = list(mine.shape)
        shape[axis] *= 4
        out = jnp.zeros(shape, F32)
        for j in range(4):
            out = lax.dynamic_update_slice_in_dim(
                out, pieces[j].astype(F32) * norm_factor, (me ^ j) * quarter, axis=axis
            )
        return out

    out_piece = over_groups(
        to_owner([part_out[s * quarter : (s + 1) * quarter] for s in range(reps)])
    ).astype(BF16)
    in_piece = over_groups(
        to_owner([part_in[:, s * quarter : (s + 1) * quarter] for s in range(reps)])
    ).astype(BF16)
    grad_out = gathered(out_piece, 0)
    grad_in = gathered(in_piece, 1)

    part_agg = contract_last(grad_pre, w_in).astype(BF16).reshape(4, rows, -1)
    got_own, got_z = swap(part_agg[1], "node", 1), swap(part_agg[3], "node", 1)
    own = part_agg[0].astype(F32) + got_own.astype(F32)
    other = (part_agg[2].astype(F32) + got_z.astype(F32)).astype(BF16)
    grad_agg = (own + swap(other, "node", 2).astype(F32)).astype(BF16)

    tiles = tile_values[0]
    slot_cols = tile_cols[0]
    live = jnp.arange(tiles.shape[0], dtype=jnp.int32) < tile_count[0]
    terms = jnp.einsum("trc,rd->tcd", tiles, grad_agg, preferred_element_type=F32)

    def toward(target):
        total = jnp.zeros(terms.shape[1:], F32)
        for slot in range(tiles.shape[0]):
            take = live[slot] & (slot_cols[slot] == target)
            total = total + jnp.where(take, terms[slot], 0.0)
        return total

    from_next = shift(toward(0).astype(BF16), "node", -1)
    from_prev = shift(toward(2).astype(BF16), "node", 1)
    grad_nodes = (
        cotangent.astype(F32) + toward(1) + from_next.astype(F32) + from_prev.astype(F32)
    ).astype(BF16)
    return (grad_nodes, grad_in, grad_out)


def solution(mesh):
    return jax.shard_map(
        local,
        mesh=mesh,
        in_specs=(
            P(("node", "rep"), None),
            P(("node", "rep"), None),
            P(None, "rep"),
            P("rep", None),
            P(("node", "rep"), None, None, None),
            P(("node", "rep"), None),
            P(("node", "rep")),
        ),
        out_specs=(P(("node", "rep"), None), P(None, "rep"), P("rep", None)),
        check_vma=False,
    )
```

time: 187 us -> 93 us (0.50)
  waiting for transfers between devices: 142 us -> 28.4 us
  starting transfers between devices: 2.98 us -> 28.3 us
  matrix products: 15.5 us -> 7.16 us
  local copies, waits for them, and re-layouts: 7.56 us -> 11.1 us
  other arithmetic: 3.6 us -> 1.02 us
  between operations: 14.6 us -> 16.5 us
    psum x1 -> x0, waiting for transfers between devices: 62.1 us -> none  [local(): total_in, total_out = lax.psum((sum_in, sum_out), 'node')]
    all_gather x2 -> x0, waiting for transfers between devices: 57.1 us -> none  [the longest x1 30.5 us: local(): agg_piece = lax.all_gather(aggregated, 'rep', axis=0, tiled=True)]
    ppermute x2 -> x31, waiting for transfers between devices: 0.01 us -> 28.4 us  [the longest x29 20.6 us: swap(): return lax.ppermute(block, axis, [(i, i ^ mask) for i in range(count)])]
    ppermute x2 -> x31, starting transfers between devices: 2.83 us -> 28.3 us  [the longest x29 26.4 us: swap(): return lax.ppermute(block, axis, [(i, i ^ mask) for i in range(count)])]
    reduce_scatter x1 -> x0, waiting for transfers between devices: 21.7 us -> none  [local(): lax.psum_scatter(contract_last(hidden_buf, kernel_in).astype(jnp.bfloat16...]
    dot_general x2, matrix products: 5.38 us -> 1.67 us  [contract_first(): lax.dot_general(left, right, (((0,), (0,)), ((), ())), preferred_element_...]
    dot_general x3 -> x2, matrix products: 5.43 us -> 2.41 us  [the longest x1 1.93 us: local(): pre_act = jnp.dot(agg, w_in, preferred_element_type=F32)]
    unnamed x18 -> x16, local copies, waits for them, and re-layouts: 3.69 us -> 6.07 us
  transfers between devices with their start and end apart: 6 -> 31, of which waited for: 4 -> 10; matrix products, arithmetic and copies ran while one was open for 10% -> 20% of each run, Pallas kernels for 0% -> 0%
where the time goes in v1:
time: 93 us; the launch traced here: 92.5 us
  waiting for transfers between devices  28.4 us (31%)
  starting transfers between devices  28.3 us (30%)
  between operations  16.5 us (18%)
  local copies, waits for them, and re-layouts  11.1 us (12%)
  matrix products  7.16 us (8%)
  other arithmetic  1.02 us (1%)
    ppermute x29, starting transfers between devices, swap(): return lax.ppermute(block, axis, [(i, i ^ mask) for i in range(count)])  26.4 us
    ppermute x29, waiting for transfers between devices, swap(): return lax.ppermute(block, axis, [(i, i ^ mask) for i in range(count)])  20.6 us
    ppermute x2, waiting for transfers between devices, shift(): lax.ppermute(block, axis, [(i, (i + step) % count) for i in range(count)])  7.79 us
    unnamed x16, local copies, waits for them, and re-layouts  6.07 us
    dot_general x2, matrix products, contract_last(): lax.dot_general(left, right, (((1,), (1,)), ((), ())), preferred_element_...  3.08 us
    slice x2, local copies, waits for them, and re-layouts, toward(): take = live[slot] & (slot_cols[slot] == target)  2.08 us
    dot_general x1, matrix products, local(): pre_act = jnp.dot(agg, w_in, preferred_element_type=F32)  1.93 us
    ppermute x2, starting transfers between devices, shift(): lax.ppermute(block, axis, [(i, (i + step) % count) for i in range(count)])  1.89 us
  transfers between devices with their start and end apart: 31, of which 10 were waited for; matrix products, arithmetic and copies ran while one was open for 20% of the time, Pallas kernels for 0%

profile of v1, /device:TPU:0, one launch (start us, length us, event | category | flops | bytes accessed | tf_op | source)
XLA Modules:
  0.0 92.5 jit_solution(10658809825221252204)
XLA Ops:
  0.6 3.1 %collective-permute-start.7 = (bf16[256,512]{1,0:T(8,128)(2,1)}, bf16[256,512]{1,0:T(8,128)(2,1)S(1)}, u32[]{:S(2)}, u32[]{:S(2)}) collective-permute-start(bf16[256,512]{1,0:T(8,128)(2,1)} %param.7), channel_id=1, source_target_pairs={{0,8},{4,12},{8,0},{12,4},{16,24},{20,28},{24,16},{28,20},{1,9},{5... | collective-permute-start | bytes 786440 | tf_op jit(solution)/shard_map/ppermute | solution.py:33
  4.2 0.9 constant_dynamic-slice_fusion
  5.2 1.8 %collective-permute-start.10 = (bf16[512,128]{1,0:T(8,128)(2,1)S(1)}, bf16[512,128]{1,0:T(8,128)(2,1)S(1)}, u32[]{:S(2)}, u32[]{:S(2)}) collective-permute-start(bf16[512,128]{1,0:T(8,128)(2,1)S(1)} %constant_dynamic-slice_fusion), channel_id=1, source_target_pairs={{0,2},{1,3},{2,0},{3,1},{4,6},{5,7},{6,4},{7,5},{8,10},{9,11},{10,... | collective-permute-start | bytes 393224 | tf_op jit(solution)/shard_map/ppermute | solution.py:33
  6.9 1.7 %constant_dynamic-update-slice_fusion.7 = bf16[1024,512]{1,0:T(8,128)(2,1)} fusion(bf16[256,512]{1,0:T(8,128)(2,1)} %param.7), kind=kLoop, calls=%fused_computation.58 | loop fusion | bytes 524288
  10.8 1.0 %constant_dynamic-update-slice_fusion.3 = bf16[1024,512]{1,0:T(8,128)(2,1)S(1)} fusion(bf16[256,512]{1,0:T(8,128)(2,1)} %param.8), kind=kLoop, calls=%fused_computation.54 | loop fusion | bytes 524288
  11.8 1.5 %fusion.37 = (s32[1,1]{1,0:T(1,128)}, s32[1,1]{1,0:T(1,128)}, s32[1,1]{1,0:T(1,128)}, s32[1,1]{1,0:T(1,128)}) fusion(s32[1,4]{1,0:T(1,128)} %param.12), kind=kLoop, calls=%fused_computation.72 | loop fusion | bytes 32 | tf_op jit(solution)/shard_map/slice | solution.py:125
  20.6 1.1 %copy.10 = bf16[256,512]{0,1:T(8,128)(2,1)S(1)} copy(bf16[256,512]{1,0:T(8,128)(2,1)} %param.8) | data formatting | bytes 524288 | tf_op args[1]
  29.2 1.5 %collective-permute-start.11 = (bf16[512,128]{1,0:T(8,128)(2,1)S(1)}, bf16[512,128]{1,0:T(8,128)(2,1)S(1)}, u32[]{:S(2)}, u32[]{:S(2)}) collective-permute-start(bf16[512,128]{1,0:T(8,128)(2,1)S(1)} %constant_dynamic-slice_fusion), channel_id=1, source_target_pairs={{0,3},{1,2},{2,1},{3,0},{4,7},{5,6},{6,5},{7,4},{8,11},{9,10},{10,... | collective-permute-start | bytes 393224 | tf_op jit(solution)/shard_map/ppermute | solution.py:33
  32.8 1.7 %collective-permute-start.3 = (bf16[128,512]{1,0:T(8,128)(2,1)S(1)}, bf16[128,512]{1,0:T(8,128)(2,1)S(1)}, u32[]{:S(2)}, u32[]{:S(2)}) collective-permute-start(bf16[128,512]{1,0:T(8,128)(2,1)S(1)} %constant_dynamic-slice_fusion.1), channel_id=1, source_target_pairs={{0,1},{1,0},{2,3},{3,2},{4,5},{5,4},{6,7},{7,6},{8,9},{9,8},{10,11... | collective-permute-start | bytes 393224 | tf_op jit(solution)/shard_map/ppermute | solution.py:33
  35.3 1.5 %collective-permute-start.4 = (bf16[128,512]{1,0:T(8,128)(2,1)S(1)}, bf16[128,512]{1,0:T(8,128)(2,1)S(1)}, u32[]{:S(2)}, u32[]{:S(2)}) collective-permute-start(bf16[128,512]{1,0:T(8,128)(2,1)S(1)} %constant_dynamic-slice_fusion.1), channel_id=1, source_target_pairs={{0,2},{1,3},{2,0},{3,1},{4,6},{5,7},{6,4},{7,5},{8,10},{9,11},{10,... | collective-permute-start | bytes 393224 | tf_op jit(solution)/shard_map/ppermute | solution.py:33
  37.3 1.2 %collective-permute-done.9 = bf16[512,128]{1,0:T(8,128)(2,1)S(1)} collective-permute-done((bf16[512,128]{1,0:T(8,128)(2,1)S(1)}, bf16[512,128]{1,0:T(8,128)(2,1)S(1)}, u32[]{:S(2)}, u32[]{:S(2)}) %collective-permute-start.9) | collective-permute-done | bytes 131104 | tf_op jit(solution)/shard_map/ppermute | solution.py:33
  38.5 1.9 %fusion.26 = f32[1024,512]{1,0:T(8,128)S(1)} fusion(bf16[1024,512]{1,0:T(8,128)(2,1)} %constant_dynamic-update-slice_fusion.4, bf16[512,128]{1,0:T(8,128)(2,1)S(1)} %collective-permute-done.11, bf16[512,128]{1,0:T(8,128)(2,1)S(1)} %collective-permute-done.10, bf16[512,128]{1,0:T(8,128)(2,1)S(1)} %collective-permute-done.9, ...), kind=kOutput, calls=%fused_computation.50 | convolution fusion | flops 538968064 | bytes 3670016 | tf_op jit(solution)/shard_map/dot_general | solution.py:76
  40.4 0.9 %convolution_convert_fusion.1 = bf16[512,512]{1,0:T(8,128)(2,1)S(1)} fusion(bf16[1024,512]{1,0:T(8,128)(2,1)S(1)} %constant_dynamic-update-slice_fusion, f32[1024,512]{1,0:T(8,128)S(1)} %fusion.26), kind=kOutput, calls=%fused_computation.12 | convolution fusion | flops 541851648 | bytes 3670016 | tf_op jit(solution)/shard_map/dot_general | solution.py:28
  41.4 1.0 %collective-permute-start.24 = (bf16[128,512]{1,0:T(8,128)(2,1)S(1)}, bf16[128,512]{1,0:T(8,128)(2,1)S(1)}, u32[]{:S(2)}, u32[]{:S(2)}) collective-permute-start(bf16[128,512]{1,0:T(8,128)(2,1)S(1)} %get-tuple-element.14), channel_id=1, source_target_pairs={{0,1},{1,0},{2,3},{3,2},{4,5},{5,4},{6,7},{7,6},{8,9},{9,8},{10,11... | collective-permute-start | bytes 393224 | tf_op jit(solution)/shard_map/ppermute | solution.py:33
  42.4 1.3 %collective-permute-start.25 = (bf16[128,512]{1,0:T(8,128)(2,1)S(1)}, bf16[128,512]{1,0:T(8,128)(2,1)S(1)}, u32[]{:S(2)}, u32[]{:S(2)}) collective-permute-start(bf16[128,512]{1,0:T(8,128)(2,1)S(1)} %get-tuple-element.16), channel_id=1, source_target_pairs={{0,2},{1,3},{2,0},{3,1},{4,6},{5,7},{6,4},{7,5},{8,10},{9,11},{10,... | collective-permute-start | bytes 393224 | tf_op jit(solution)/shard_map/ppermute | solution.py:33
  43.7 1.3 %collective-permute-start.26 = (bf16[128,512]{1,0:T(8,128)(2,1)S(1)}, bf16[128,512]{1,0:T(8,128)(2,1)S(1)}, u32[]{:S(2)}, u32[]{:S(2)}) collective-permute-start(bf16[128,512]{1,0:T(8,128)(2,1)S(1)} %get-tuple-element.15), channel_id=1, source_target_pairs={{0,3},{1,2},{2,1},{3,0},{4,7},{5,6},{6,5},{7,4},{8,11},{9,10},{10,... | collective-permute-start | bytes 393224 | tf_op jit(solution)/shard_map/ppermute | solution.py:33
  45.0 2.3 %fusion.6 = bf16[1024,512]{1,0:T(8,128)(2,1)S(1)} fusion(f32[1024,512]{1,0:T(8,128)S(1)} %fusion.26, bf16[1024,512]{1,0:T(8,128)(2,1)S(1)} %constant_dynamic-update-slice_fusion, bf16[128,512]{1,0:T(8,128)(2,1)S(1)} %collective-permute-done.5, bf16[128,512]{1,0:T(8,128)(2,1)S(1)} %collective-permute-done.4, bf16[128,512]{1,0:T(8,128)(2,1)S(1)} %collective-permute-done.3, ...), kind=kOutput, calls=%fused_computation.8 | convolution fusion | flops 548929536 | bytes 4718592 | tf_op jit(solution)/shard_map/dot_general | solution.py:24
  48.1 1.0 %collective-permute-start.17 = (bf16[512,128]{1,0:T(8,128)(2,1)S(1)}, bf16[512,128]{1,0:T(8,128)(2,1)S(1)}, u32[]{:S(2)}, u32[]{:S(2)}) collective-permute-start(bf16[512,128]{1,0:T(8,128)(2,1)S(1)} %get-tuple-element.17), channel_id=1, source_target_pairs={{0,1},{1,0},{2,3},{3,2},{4,5},{5,4},{6,7},{7,6},{8,9},{9,8},{10,11... | collective-permute-start | bytes 393224 | tf_op jit(solution)/shard_map/ppermute | solution.py:33
  49.1 1.3 %collective-permute-start.18 = (bf16[512,128]{1,0:T(8,128)(2,1)S(1)}, bf16[512,128]{1,0:T(8,128)(2,1)S(1)}, u32[]{:S(2)}, u32[]{:S(2)}) collective-permute-start(bf16[512,128]{1,0:T(8,128)(2,1)S(1)} %get-tuple-element.19), channel_id=1, source_target_pairs={{0,2},{1,3},{2,0},{3,1},{4,6},{5,7},{6,4},{7,5},{8,10},{9,11},{10,... | collective-permute-start | bytes 393224 | tf_op jit(solution)/shard_map/ppermute | solution.py:33
  51.2 1.3 %collective-permute-start.19 = (bf16[512,128]{1,0:T(8,128)(2,1)S(1)}, bf16[512,128]{1,0:T(8,128)(2,1)S(1)}, u32[]{:S(2)}, u32[]{:S(2)}) collective-permute-start(bf16[512,128]{1,0:T(8,128)(2,1)S(1)} %get-tuple-element.18), channel_id=1, source_target_pairs={{0,3},{1,2},{2,1},{3,0},{4,7},{5,6},{6,5},{7,4},{8,11},{9,10},{10,... | collective-permute-start | bytes 393224 | tf_op jit(solution)/shard_map/ppermute | solution.py:33
  53.3 2.6 %collective-permute-start.27 = (bf16[128,512]{1,0:T(8,128)(2,1)S(1)}, bf16[128,512]{1,0:T(8,128)(2,1)S(1)}, u32[]{:S(2)}, u32[]{:S(2)}) collective-permute-start(bf16[128,512]{1,0:T(8,128)(2,1)S(1)} %add_convert_fusion.5), channel_id=1, source_target_pairs={{0,16},{4,20},{8,24},{12,28},{16,0},{20,4},{24,8},{28,12},{1,17},{... | collective-permute-start | bytes 393224 | tf_op jit(solution)/shard_map/ppermute | solution.py:33
  55.9 1.2 %collective-permute-done.19 = bf16[512,128]{1,0:T(8,128)(2,1)S(1)} collective-permute-done((bf16[512,128]{1,0:T(8,128)(2,1)S(1)}, bf16[512,128]{1,0:T(8,128)(2,1)S(1)}, u32[]{:S(2)}, u32[]{:S(2)}) %collective-permute-start.19) | collective-permute-done | bytes 131104 | tf_op jit(solution)/shard_map/ppermute | solution.py:33
  57.2 2.7 %collective-permute-start.20 = (bf16[512,128]{1,0:T(8,128)(2,1)S(1)}, bf16[512,128]{1,0:T(8,128)(2,1)S(1)}, u32[]{:S(2)}, u32[]{:S(2)}) collective-permute-start(bf16[512,128]{1,0:T(8,128)(2,1)S(1)} %add_convert_fusion.7), channel_id=1, source_target_pairs={{0,16},{4,20},{8,24},{12,28},{16,0},{20,4},{24,8},{28,12},{1,17},{... | collective-permute-start | bytes 393224 | tf_op jit(solution)/shard_map/ppermute | solution.py:33
  59.9 6.3 %collective-permute-done.27 = bf16[128,512]{1,0:T(8,128)(2,1)S(1)} collective-permute-done((bf16[128,512]{1,0:T(8,128)(2,1)S(1)}, bf16[128,512]{1,0:T(8,128)(2,1)S(1)}, u32[]{:S(2)}, u32[]{:S(2)}) %collective-permute-start.27) | collective-permute-done | bytes 131104 | tf_op jit(solution)/shard_map/ppermute | solution.py:33
  66.6 1.5 %collective-permute-done.20 = bf16[512,128]{1,0:T(8,128)(2,1)S(1)} collective-permute-done((bf16[512,128]{1,0:T(8,128)(2,1)S(1)}, bf16[512,128]{1,0:T(8,128)(2,1)S(1)}, u32[]{:S(2)}, u32[]{:S(2)}) %collective-permute-start.20) | collective-permute-done | bytes 131104 | tf_op jit(solution)/shard_map/ppermute | solution.py:33
  69.0 1.4 %collective-permute-start.14 = (bf16[256,512]{1,0:T(8,128)(2,1)S(1)}, bf16[256,512]{1,0:T(8,128)(2,1)S(1)}, u32[]{:S(2)}, u32[]{:S(2)}) collective-permute-start(bf16[256,512]{1,0:T(8,128)(2,1)S(1)} %add_convert_fusion.3), channel_id=1, source_target_pairs={{0,8},{4,12},{8,0},{12,4},{16,24},{20,28},{24,16},{28,20},{1,9},{5... | collective-permute-start | bytes 786440 | tf_op jit(solution)/shard_map/ppermute | solution.py:33
  70.4 2.4 %collective-permute-done.29 = bf16[128,512]{1,0:T(8,128)(2,1)S(1)} collective-permute-done((bf16[128,512]{1,0:T(8,128)(2,1)S(1)}, bf16[128,512]{1,0:T(8,128)(2,1)S(1)}, u32[]{:S(2)}, u32[]{:S(2)}) %collective-permute-start.29) | collective-permute-done | bytes 131104 | tf_op jit(solution)/shard_map/ppermute | solution.py:33
  72.8 2.8 %collective-permute-done.22 = bf16[512,128]{1,0:T(8,128)(2,1)S(1)} collective-permute-done((bf16[512,128]{1,0:T(8,128)(2,1)S(1)}, bf16[512,128]{1,0:T(8,128)(2,1)S(1)}, u32[]{:S(2)}, u32[]{:S(2)}) %collective-permute-start.22) | collective-permute-done | bytes 131104 | tf_op jit(solution)/shard_map/ppermute | solution.py:33
  75.8 5.0 %collective-permute-done.14 = bf16[256,512]{1,0:T(8,128)(2,1)S(1)} collective-permute-done((bf16[256,512]{1,0:T(8,128)(2,1)S(1)}, bf16[256,512]{1,0:T(8,128)(2,1)S(1)}, u32[]{:S(2)}, u32[]{:S(2)}) %collective-permute-start.14) | collective-permute-done | bytes 262176 | tf_op jit(solution)/shard_map/ppermute | solution.py:33
  81.6 1.9 %collective-permute-start.15 = (bf16[256,512]{0,1:T(8,128)(2,1)S(1)}, bf16[256,512]{0,1:T(8,128)(2,1)S(1)}, u32[]{:S(2)}, u32[]{:S(2)}) collective-permute-start(bf16[256,512]{0,1:T(8,128)(2,1)S(1)} %get-tuple-element.10), channel_id=1, source_target_pairs={{0,28},{4,0},{8,4},{12,8},{16,12},{20,16},{24,20},{28,24},{1,29},{... | collective-permute-start | bytes 786440 | tf_op jit(solution)/shard_map/ppermute | solution.py:38
  83.6 5.5 %collective-permute-done.15 = bf16[256,512]{0,1:T(8,128)(2,1)S(1)} collective-permute-done((bf16[256,512]{0,1:T(8,128)(2,1)S(1)}, bf16[256,512]{0,1:T(8,128)(2,1)S(1)}, u32[]{:S(2)}, u32[]{:S(2)}) %collective-permute-start.15) | collective-permute-done | bytes 262176 | tf_op jit(solution)/shard_map/ppermute | solution.py:38
  89.1 2.3 %collective-permute-done.16 = bf16[256,512]{0,1:T(8,128)(2,1)S(1)} collective-permute-done((bf16[256,512]{0,1:T(8,128)(2,1)S(1)}, bf16[256,512]{0,1:T(8,128)(2,1)S(1)}, u32[]{:S(2)}, u32[]{:S(2)}) %collective-permute-start.16) | collective-permute-done | bytes 262176 | tf_op jit(solution)/shard_map/ppermute | solution.py:38
  (77 shorter events, 11.2 us)
Async XLA Ops:
  0.6 80.2 %copy-start = (bf16[1,4,256,256]{3,2,1,0:T(8,128)(2,1)S(1)}, bf16[1,4,256,256]{3,2,1,0:T(8,128)(2,1)}, u32[]{:S(2)}) copy-start(bf16[1,4,256,256]{3,2,1,0:T(8,128)(2,1)} %param.11) | copy-start | bytes 1572868
  0.6 28.6 %collective-permute-start.7 = (bf16[256,512]{1,0:T(8,128)(2,1)}, bf16[256,512]{1,0:T(8,128)(2,1)S(1)}, u32[]{:S(2)}, u32[]{:S(2)}) collective-permute-start(bf16[256,512]{1,0:T(8,128)(2,1)} %param.7), channel_id=1, source_target_pairs={{0,8},{4,12},{8,0},{12,4},{16,24},{20,28},{24,16},{28,20},{1,9},{5... | collective-permute-start | bytes 786440 | tf_op jit(solution)/shard_map/ppermute | solution.py:33
  3.7 27.0 %collective-permute-start.6 = (bf16[256,512]{1,0:T(8,128)(2,1)}, bf16[256,512]{1,0:T(8,128)(2,1)S(1)}, u32[]{:S(2)}, u32[]{:S(2)}) collective-permute-start(bf16[256,512]{1,0:T(8,128)(2,1)} %param.7), channel_id=1, source_target_pairs={{0,4},{4,0},{8,12},{12,8},{16,20},{20,16},{24,28},{28,24},{1,5},{5... | collective-permute-start | bytes 786440 | tf_op jit(solution)/shard_map/ppermute | solution.py:33
  3.7 28.4 %collective-permute-start.1 = (bf16[256,512]{1,0:T(8,128)(2,1)}, bf16[256,512]{1,0:T(8,128)(2,1)S(1)}, u32[]{:S(2)}, u32[]{:S(2)}) collective-permute-start(bf16[256,512]{1,0:T(8,128)(2,1)} %param.8), channel_id=1, source_target_pairs={{0,8},{4,12},{8,0},{12,4},{16,24},{20,28},{24,16},{28,20},{1,9},{5... | collective-permute-start | bytes 786440 | tf_op jit(solution)/shard_map/ppermute | solution.py:33
  3.9 28.6 %collective-permute-start = (bf16[256,512]{1,0:T(8,128)(2,1)}, bf16[256,512]{1,0:T(8,128)(2,1)S(1)}, u32[]{:S(2)}, u32[]{:S(2)}) collective-permute-start(bf16[256,512]{1,0:T(8,128)(2,1)} %param.8), channel_id=1, source_target_pairs={{0,4},{4,0},{8,12},{12,8},{16,20},{20,16},{24,28},{28,24},{1,5},{5... | collective-permute-start | bytes 786440 | tf_op jit(solution)/shard_map/ppermute | solution.py:33
  5.2 31.7 %collective-permute-start.10 = (bf16[512,128]{1,0:T(8,128)(2,1)S(1)}, bf16[512,128]{1,0:T(8,128)(2,1)S(1)}, u32[]{:S(2)}, u32[]{:S(2)}) collective-permute-start(bf16[512,128]{1,0:T(8,128)(2,1)S(1)} %constant_dynamic-slice_fusion), channel_id=1, source_target_pairs={{0,2},{1,3},{2,0},{3,1},{4,6},{5,7},{6,4},{7,5},{8,10},{9,11},{10,... | collective-permute-start | bytes 393224 | tf_op jit(solution)/shard_map/ppermute | solution.py:33
  29.2 8.1 %collective-permute-start.11 = (bf16[512,128]{1,0:T(8,128)(2,1)S(1)}, bf16[512,128]{1,0:T(8,128)(2,1)S(1)}, u32[]{:S(2)}, u32[]{:S(2)}) collective-permute-start(bf16[512,128]{1,0:T(8,128)(2,1)S(1)} %constant_dynamic-slice_fusion), channel_id=1, source_target_pairs={{0,3},{1,2},{2,1},{3,0},{4,7},{5,6},{6,5},{7,4},{8,11},{9,10},{10,... | collective-permute-start | bytes 393224 | tf_op jit(solution)/shard_map/ppermute | solution.py:33
  30.7 2.1 %collective-permute-start.8 = (bf16[256,512]{1,0:T(8,128)(2,1)S(1)}, bf16[256,512]{1,0:T(8,128)(2,1)S(1)}, u32[]{:S(2)}, u32[]{:S(2)}) collective-permute-start(bf16[256,512]{1,0:T(8,128)(2,1)S(1)} %collective-permute-done.7), channel_id=1, source_target_pairs={{0,4},{4,0},{8,12},{12,8},{16,20},{20,16},{24,28},{28,24},{1,5},{5... | collective-permute-start | bytes 786440 | tf_op jit(solution)/shard_map/ppermute | solution.py:33
  32.2 6.3 %collective-permute-start.9 = (bf16[512,128]{1,0:T(8,128)(2,1)S(1)}, bf16[512,128]{1,0:T(8,128)(2,1)S(1)}, u32[]{:S(2)}, u32[]{:S(2)}) collective-permute-start(bf16[512,128]{1,0:T(8,128)(2,1)S(1)} %constant_dynamic-slice_fusion), channel_id=1, source_target_pairs={{0,1},{1,0},{2,3},{3,2},{4,5},{5,4},{6,7},{7,6},{8,9},{9,8},{10,11... | collective-permute-start | bytes 393224 | tf_op jit(solution)/shard_map/ppermute | solution.py:33
  32.5 2.7 %collective-permute-start.2 = (bf16[256,512]{1,0:T(8,128)(2,1)S(1)}, bf16[256,512]{1,0:T(8,128)(2,1)S(1)}, u32[]{:S(2)}, u32[]{:S(2)}) collective-permute-start(bf16[256,512]{1,0:T(8,128)(2,1)S(1)} %collective-permute-done.1), channel_id=1, source_target_pairs={{0,4},{4,0},{8,12},{12,8},{16,20},{20,16},{24,28},{28,24},{1,5},{5... | collective-permute-start | bytes 786440 | tf_op jit(solution)/shard_map/ppermute | solution.py:33
  32.8 10.9 %collective-permute-start.3 = (bf16[128,512]{1,0:T(8,128)(2,1)S(1)}, bf16[128,512]{1,0:T(8,128)(2,1)S(1)}, u32[]{:S(2)}, u32[]{:S(2)}) collective-permute-start(bf16[128,512]{1,0:T(8,128)(2,1)S(1)} %constant_dynamic-slice_fusion.1), channel_id=1, source_target_pairs={{0,1},{1,0},{2,3},{3,2},{4,5},{5,4},{6,7},{7,6},{8,9},{9,8},{10,11... | collective-permute-start | bytes 393224 | tf_op jit(solution)/shard_map/ppermute | solution.py:33
  35.3 9.7 %collective-permute-start.4 = (bf16[128,512]{1,0:T(8,128)(2,1)S(1)}, bf16[128,512]{1,0:T(8,128)(2,1)S(1)}, u32[]{:S(2)}, u32[]{:S(2)}) collective-permute-start(bf16[128,512]{1,0:T(8,128)(2,1)S(1)} %constant_dynamic-slice_fusion.1), channel_id=1, source_target_pairs={{0,2},{1,3},{2,0},{3,1},{4,6},{5,7},{6,4},{7,5},{8,10},{9,11},{10,... | collective-permute-start | bytes 393224 | tf_op jit(solution)/shard_map/ppermute | solution.py:33
  36.8 8.1 %collective-permute-start.5 = (bf16[128,512]{1,0:T(8,128)(2,1)S(1)}, bf16[128,512]{1,0:T(8,128)(2,1)S(1)}, u32[]{:S(2)}, u32[]{:S(2)}) collective-permute-start(bf16[128,512]{1,0:T(8,128)(2,1)S(1)} %constant_dynamic-slice_fusion.1), channel_id=1, source_target_pairs={{0,3},{1,2},{2,1},{3,0},{4,7},{5,6},{6,5},{7,4},{8,11},{9,10},{10,... | collective-permute-start | bytes 393224 | tf_op jit(solution)/shard_map/ppermute | solution.py:33
  41.4 9.8 %collective-permute-start.24 = (bf16[128,512]{1,0:T(8,128)(2,1)S(1)}, bf16[128,512]{1,0:T(8,128)(2,1)S(1)}, u32[]{:S(2)}, u32[]{:S(2)}) collective-permute-start(bf16[128,512]{1,0:T(8,128)(2,1)S(1)} %get-tuple-element.14), channel_id=1, source_target_pairs={{0,1},{1,0},{2,3},{3,2},{4,5},{5,4},{6,7},{7,6},{8,9},{9,8},{10,11... | collective-permute-start | bytes 393224 | tf_op jit(solution)/shard_map/ppermute | solution.py:33
  42.4 10.2 %collective-permute-start.25 = (bf16[128,512]{1,0:T(8,128)(2,1)S(1)}, bf16[128,512]{1,0:T(8,128)(2,1)S(1)}, u32[]{:S(2)}, u32[]{:S(2)}) collective-permute-start(bf16[128,512]{1,0:T(8,128)(2,1)S(1)} %get-tuple-element.16), channel_id=1, source_target_pairs={{0,2},{1,3},{2,0},{3,1},{4,6},{5,7},{6,4},{7,5},{8,10},{9,11},{10,... | collective-permute-start | bytes 393224 | tf_op jit(solution)/shard_map/ppermute | solution.py:33
  43.7 8.9 %collective-permute-start.26 = (bf16[128,512]{1,0:T(8,128)(2,1)S(1)}, bf16[128,512]{1,0:T(8,128)(2,1)S(1)}, u32[]{:S(2)}, u32[]{:S(2)}) collective-permute-start(bf16[128,512]{1,0:T(8,128)(2,1)S(1)} %get-tuple-element.15), channel_id=1, source_target_pairs={{0,3},{1,2},{2,1},{3,0},{4,7},{5,6},{6,5},{7,4},{8,11},{9,10},{10,... | collective-permute-start | bytes 393224 | tf_op jit(solution)/shard_map/ppermute | solution.py:33
  48.1 5.2 %collective-permute-start.17 = (bf16[512,128]{1,0:T(8,128)(2,1)S(1)}, bf16[512,128]{1,0:T(8,128)(2,1)S(1)}, u32[]{:S(2)}, u32[]{:S(2)}) collective-permute-start(bf16[512,128]{1,0:T(8,128)(2,1)S(1)} %get-tuple-element.17), channel_id=1, source_target_pairs={{0,1},{1,0},{2,3},{3,2},{4,5},{5,4},{6,7},{7,6},{8,9},{9,8},{10,11... | collective-permute-start | bytes 393224 | tf_op jit(solution)/shard_map/ppermute | solution.py:33
  49.1 6.8 %collective-permute-start.18 = (bf16[512,128]{1,0:T(8,128)(2,1)S(1)}, bf16[512,128]{1,0:T(8,128)(2,1)S(1)}, u32[]{:S(2)}, u32[]{:S(2)}) collective-permute-start(bf16[512,128]{1,0:T(8,128)(2,1)S(1)} %get-tuple-element.19), channel_id=1, source_target_pairs={{0,2},{1,3},{2,0},{3,1},{4,6},{5,7},{6,4},{7,5},{8,10},{9,11},{10,... | collective-permute-start | bytes 393224 | tf_op jit(solution)/shard_map/ppermute | solution.py:33
  51.2 5.9 %collective-permute-start.19 = (bf16[512,128]{1,0:T(8,128)(2,1)S(1)}, bf16[512,128]{1,0:T(8,128)(2,1)S(1)}, u32[]{:S(2)}, u32[]{:S(2)}) collective-permute-start(bf16[512,128]{1,0:T(8,128)(2,1)S(1)} %get-tuple-element.18), channel_id=1, source_target_pairs={{0,3},{1,2},{2,1},{3,0},{4,7},{5,6},{6,5},{7,4},{8,11},{9,10},{10,... | collective-permute-start | bytes 393224 | tf_op jit(solution)/shard_map/ppermute | solution.py:33
  52.6 16.4 %collective-permute-start.13 = (bf16[256,512]{1,0:T(8,128)(2,1)S(1)}, bf16[256,512]{1,0:T(8,128)(2,1)S(1)}, u32[]{:S(2)}, u32[]{:S(2)}) collective-permute-start(bf16[256,512]{1,0:T(8,128)(2,1)S(1)} %get-tuple-element.13), channel_id=1, source_target_pairs={{0,4},{4,0},{8,12},{12,8},{16,20},{20,16},{24,28},{28,24},{1,5},{5... | collective-permute-start | bytes 786440 | tf_op jit(solution)/shard_map/ppermute | solution.py:33
  52.6 23.2 %collective-permute-start.12 = (bf16[256,512]{1,0:T(8,128)(2,1)S(1)}, bf16[256,512]{1,0:T(8,128)(2,1)S(1)}, u32[]{:S(2)}, u32[]{:S(2)}) collective-permute-start(bf16[256,512]{1,0:T(8,128)(2,1)S(1)} %get-tuple-element.12), channel_id=1, source_target_pairs={{0,4},{4,0},{8,12},{12,8},{16,20},{20,16},{24,28},{28,24},{1,5},{5... | collective-permute-start | bytes 786440 | tf_op jit(solution)/shard_map/ppermute | solution.py:33
  53.3 12.9 %collective-permute-start.27 = (bf16[128,512]{1,0:T(8,128)(2,1)S(1)}, bf16[128,512]{1,0:T(8,128)(2,1)S(1)}, u32[]{:S(2)}, u32[]{:S(2)}) collective-permute-start(bf16[128,512]{1,0:T(8,128)(2,1)S(1)} %add_convert_fusion.5), channel_id=1, source_target_pairs={{0,16},{4,20},{8,24},{12,28},{16,0},{20,4},{24,8},{28,12},{1,17},{... | collective-permute-start | bytes 393224 | tf_op jit(solution)/shard_map/ppermute | solution.py:33
  57.2 10.8 %collective-permute-start.20 = (bf16[512,128]{1,0:T(8,128)(2,1)S(1)}, bf16[512,128]{1,0:T(8,128)(2,1)S(1)}, u32[]{:S(2)}, u32[]{:S(2)}) collective-permute-start(bf16[512,128]{1,0:T(8,128)(2,1)S(1)} %add_convert_fusion.7), channel_id=1, source_target_pairs={{0,16},{4,20},{8,24},{12,28},{16,0},{20,4},{24,8},{28,12},{1,17},{... | collective-permute-start | bytes 393224 | tf_op jit(solution)/shard_map/ppermute | solution.py:33
  66.4 4.0 %collective-permute-start.28 = (bf16[128,512]{1,0:T(8,128)(2,1)S(1)}, bf16[128,512]{1,0:T(8,128)(2,1)S(1)}, u32[]{:S(2)}, u32[]{:S(2)}) collective-permute-start(bf16[128,512]{1,0:T(8,128)(2,1)S(1)} %get-tuple-element.7), channel_id=1, source_target_pairs={{0,4},{4,0},{8,12},{12,8},{16,20},{20,16},{24,28},{28,24},{1,5},{5... | collective-permute-start | bytes 393224 | tf_op jit(solution)/shard_map/ppermute | solution.py:33
  66.5 6.4 %collective-permute-start.29 = (bf16[128,512]{1,0:T(8,128)(2,1)S(1)}, bf16[128,512]{1,0:T(8,128)(2,1)S(1)}, u32[]{:S(2)}, u32[]{:S(2)}) collective-permute-start(bf16[128,512]{1,0:T(8,128)(2,1)S(1)} %get-tuple-element.7), channel_id=1, source_target_pairs={{0,8},{4,12},{8,0},{12,4},{16,24},{20,28},{24,16},{28,20},{1,9},{5... | collective-permute-start | bytes 393224 | tf_op jit(solution)/shard_map/ppermute | solution.py:33
  68.2 7.5 %collective-permute-start.22 = (bf16[512,128]{1,0:T(8,128)(2,1)S(1)}, bf16[512,128]{1,0:T(8,128)(2,1)S(1)}, u32[]{:S(2)}, u32[]{:S(2)}) collective-permute-start(bf16[512,128]{1,0:T(8,128)(2,1)S(1)} %get-tuple-element.9), channel_id=1, source_target_pairs={{0,8},{4,12},{8,0},{12,4},{16,24},{20,28},{24,16},{28,20},{1,9},{5... | collective-permute-start | bytes 393224 | tf_op jit(solution)/shard_map/ppermute | solution.py:33
  69.0 11.8 %collective-permute-start.14 = (bf16[256,512]{1,0:T(8,128)(2,1)S(1)}, bf16[256,512]{1,0:T(8,128)(2,1)S(1)}, u32[]{:S(2)}, u32[]{:S(2)}) collective-permute-start(bf16[256,512]{1,0:T(8,128)(2,1)S(1)} %add_convert_fusion.3), channel_id=1, source_target_pairs={{0,8},{4,12},{8,0},{12,4},{16,24},{20,28},{24,16},{28,20},{1,9},{5... | collective-permute-start | bytes 786440 | tf_op jit(solution)/shard_map/ppermute | solution.py:33
  70.4 5.3 %collective-permute-start.21 = (bf16[512,128]{1,0:T(8,128)(2,1)S(1)}, bf16[512,128]{1,0:T(8,128)(2,1)S(1)}, u32[]{:S(2)}, u32[]{:S(2)}) collective-permute-start(bf16[512,128]{1,0:T(8,128)(2,1)S(1)} %get-tuple-element.9), channel_id=1, source_target_pairs={{0,4},{4,0},{8,12},{12,8},{16,20},{20,16},{24,28},{28,24},{1,5},{5... | collective-permute-start | bytes 393224 | tf_op jit(solution)/shard_map/ppermute | solution.py:33
  72.8 10.6 %collective-permute-start.30 = (bf16[128,512]{1,0:T(8,128)(2,1)S(1)}, bf16[128,512]{1,0:T(8,128)(2,1)S(1)}, u32[]{:S(2)}, u32[]{:S(2)}) collective-permute-start(bf16[128,512]{1,0:T(8,128)(2,1)S(1)} %collective-permute-done.29), channel_id=1, source_target_pairs={{0,4},{4,0},{8,12},{12,8},{16,20},{20,16},{24,28},{28,24},{1,5},{5... | collective-permute-start | bytes 393224 | tf_op jit(solution)/shard_map/ppermute | solution.py:33
  75.7 7.9 %collective-permute-start.23 = (bf16[512,128]{1,0:T(8,128)(2,1)S(1)}, bf16[512,128]{1,0:T(8,128)(2,1)S(1)}, u32[]{:S(2)}, u32[]{:S(2)}) collective-permute-start(bf16[512,128]{1,0:T(8,128)(2,1)S(1)} %collective-permute-done.22), channel_id=1, source_target_pairs={{0,4},{4,0},{8,12},{12,8},{16,20},{20,16},{24,28},{28,24},{1,5},{5... | collective-permute-start | bytes 393224 | tf_op jit(solution)/shard_map/ppermute | solution.py:33
  81.6 7.5 %collective-permute-start.15 = (bf16[256,512]{0,1:T(8,128)(2,1)S(1)}, bf16[256,512]{0,1:T(8,128)(2,1)S(1)}, u32[]{:S(2)}, u32[]{:S(2)}) collective-permute-start(bf16[256,512]{0,1:T(8,128)(2,1)S(1)} %get-tuple-element.10), channel_id=1, source_target_pairs={{0,28},{4,0},{8,4},{12,8},{16,12},{20,16},{24,20},{28,24},{1,29},{... | collective-permute-start | bytes 786440 | tf_op jit(solution)/shard_map/ppermute | solution.py:38
  83.5 7.9 %collective-permute-start.16 = (bf16[256,512]{0,1:T(8,128)(2,1)S(1)}, bf16[256,512]{0,1:T(8,128)(2,1)S(1)}, u32[]{:S(2)}, u32[]{:S(2)}) collective-permute-start(bf16[256,512]{0,1:T(8,128)(2,1)S(1)} %get-tuple-element.11), channel_id=1, source_target_pairs={{0,4},{4,8},{8,12},{12,16},{16,20},{20,24},{24,28},{28,0},{1,5},{5... | collective-permute-start | bytes 786440 | tf_op jit(solution)/shard_map/ppermute | solution.py:38
  (3 other events, 21.5 us)

commit v2 on v1

v2 whole, which is shorter than its diff:
```python
import functools
import math

import jax
import jax.numpy as jnp
from jax import lax
from jax.experimental import pallas as pl
from jax.experimental.pallas import tpu as pltpu
from jax.sharding import PartitionSpec as P

BF16 = jnp.bfloat16
F32 = jnp.float32
VMEM = pl.BlockSpec(memory_space=pltpu.VMEM)
SMEM = pl.BlockSpec(memory_space=pltpu.SMEM)
ANY = pl.BlockSpec(memory_space=pl.ANY)


def gelu_both(pre_act):
    root = math.sqrt(2.0 / math.pi)
    square = pre_act * pre_act
    tanh_val = jnp.tanh(root * (pre_act + 0.044715 * square * pre_act))
    half = 0.5 + 0.5 * tanh_val
    value = pre_act * half
    slope = half + 0.5 * pre_act * (1.0 - tanh_val * tanh_val) * (
        root + (root * 3.0 * 0.044715) * square
    )
    return value, slope


def product(left, right, left_dim, right_dim):
    return lax.dot_general(
        left, right, (((left_dim,), (right_dim,)), ((), ())), preferred_element_type=F32
    )


def swap(block, axis, mask):
    count = lax.axis_size(axis)
    return lax.ppermute(block, axis, [(i, i ^ mask) for i in range(count)])


def shift(block, axis, step):
    count = lax.axis_size(axis)
    return lax.ppermute(block, axis, [(i, (i + step) % count) for i in range(count)])


def call(kernel, outs, args, specs=None, scratch=(), flops=0, nbytes=0):
    single = not isinstance(outs, (list, tuple))
    return pl.pallas_call(
        kernel,
        out_shape=outs,
        in_specs=specs or [VMEM] * len(args),
        out_specs=VMEM if single else [VMEM] * len(outs),
        scratch_shapes=list(scratch),
        compiler_params=pltpu.CompilerParams(vmem_limit_bytes=40 * 1024 * 1024),
        cost_estimate=pl.CostEstimate(flops=flops, bytes_accessed=nbytes, transcendentals=0),
    )(*args)


def place():
    return lax.rem(lax.axis_index("node"), 4)


def pack_kernel(quarter, kin_ref, kout_ref, out_ref, kin_part, sems):
    first = pl.multiple_of(place() * quarter, quarter)
    take_in = pltpu.make_async_copy(kin_ref.at[:, pl.ds(first, quarter)], kin_part, sems.at[0])
    take_out = pltpu.make_async_copy(
        kout_ref.at[pl.ds(first, quarter)], out_ref.at[pl.ds(quarter, quarter)], sems.at[1]
    )
    take_in.start()
    take_out.start()
    take_in.wait()
    out_ref[:quarter] = kin_part[...].T
    take_out.wait()


def pack(kernel_in, kernel_out, quarter):
    width = kernel_out.shape[1]
    if quarter % 128:
        kin = lax.dynamic_slice_in_dim(kernel_in, place() * quarter, quarter, axis=1)
        kout = lax.dynamic_slice_in_dim(kernel_out, place() * quarter, quarter, axis=0)
        return jnp.concatenate([kin.T, kout], axis=0)
    return call(
        functools.partial(pack_kernel, quarter),
        jax.ShapeDtypeStruct((2 * quarter, width), BF16),
        (kernel_in, kernel_out),
        [ANY, ANY],
        [pltpu.VMEM((width, quarter), BF16), pltpu.SemaphoreType.DMA((2,))],
        nbytes=4 * quarter * width * 2,
    )


def forward_kernel(reps, quarter, *refs):
    aggs, cots, weights = refs[:4], refs[4:8], refs[8 : 8 + reps]
    parts, slope_ref = refs[8 + reps : 8 + 2 * reps], refs[8 + 2 * reps]
    w_in = jnp.concatenate([w[:quarter] for w in weights], axis=0)
    total = None
    for j in range(4):
        value, slope = gelu_both(product(w_in, aggs[j][...], 1, 1))
        slope_ref[j] = slope.astype(BF16)
        term = product(value.astype(BF16), cots[j][...], 1, 0)
        total = term if total is None else total + term
    for s in range(reps):
        parts[s][...] = total[s * quarter : (s + 1) * quarter].astype(BF16)


def backward_kernel(reps, quarter, *refs):
    aggs, cots, weights = refs[:4], refs[4:8], refs[8 : 8 + reps]
    slope_ref = refs[8 + reps]
    parts, keep_ref, send_ref = refs[9 + reps : 9 + 2 * reps], refs[9 + 2 * reps], refs[10 + 2 * reps]
    w_in = jnp.concatenate([w[:quarter] for w in weights], axis=0)
    w_out = jnp.concatenate([w[quarter:] for w in weights], axis=0)
    total = None
    for j in range(4):
        grad_act = product(w_out, cots[j][...], 1, 1)
        grad_pre = (grad_act * slope_ref[j].astype(F32)).astype(BF16)
        term = product(grad_pre, aggs[j][...], 1, 0)
        total = term if total is None else total + term
        rows = product(grad_pre, w_in, 0, 0).astype(BF16)
        (send_ref if j % 2 else keep_ref)[j // 2] = rows
    for s in range(reps):
        parts[s][...] = total[s * quarter : (s + 1) * quarter].astype(BF16)


def tiles_kernel(keep_ref, got_ref, last_ref, tiles_ref, cols_ref, count_ref, cot_ref,
                 low_ref, high_ref, own_ref, sums):
    grad_agg = (
        keep_ref[0].astype(F32) + got_ref[0].astype(F32) + last_ref[...].astype(F32)
    ).astype(BF16)
    sums[0] = jnp.zeros_like(sums[0])
    sums[1] = cot_ref[...].astype(F32)
    sums[2] = jnp.zeros_like(sums[2])
    for slot in range(tiles_ref.shape[1]):

        @pl.when(slot < count_ref[0])
        def _():
            target = cols_ref[0, slot]
            sums[target] += product(tiles_ref[0, slot], grad_agg, 0, 0)

    low_ref[...] = sums[0].astype(BF16)
    high_ref[...] = sums[2].astype(BF16)
    own_ref[...] = sums[1]


def assemble_kernel(axis, quarter, factor, *refs):
    out_ref = refs[4]
    me = place()
    for j in range(4):
        block = refs[j][...].astype(F32) * factor
        for spot in range(4):

            @pl.when(me == spot ^ j)
            def _(block=block, spot=spot):
                where = pl.ds(spot * quarter, quarter)
                if axis == 0:
                    out_ref[where, :] = block
                else:
                    out_ref[:, where] = block


def over_groups(piece):
    groups = lax.axis_size("node") // 4
    if groups == 2:
        return piece.astype(F32) + swap(piece, "node", 4).astype(F32)
    pieces = jnp.stack([piece] + [shift(piece, "node", 4 * s) for s in range(1, groups)])
    group = lax.axis_index("node") // 4
    ordered = jnp.roll(pieces[::-1], group + 1, axis=0)
    total = jnp.zeros(piece.shape, F32)
    for s in range(groups):
        total = total + ordered[s].astype(F32)
    return total


def local(aggregated, cotangent, kernel_in, kernel_out, tile_values, tile_cols, tile_count):
    rows, width = aggregated.shape
    reps = lax.axis_size("rep")
    factor = 1.0 / math.sqrt(rows * lax.axis_size("node") * reps)
    quarter = kernel_out.shape[0] // 4
    hidden = quarter * reps

    agg_z = swap(aggregated, "node", 2)
    cot_z = swap(cotangent, "node", 2)
    packed = pack(kernel_in, kernel_out, quarter)
    weights = [packed] + [swap(packed, "rep", s) for s in range(1, reps)]
    aggs = [aggregated, swap(aggregated, "node", 1), agg_z, swap(agg_z, "node", 1)]
    cots = [cotangent, swap(cotangent, "node", 1), cot_z, swap(cot_z, "node", 1)]

    piece = jax.ShapeDtypeStruct((quarter, width), BF16)
    pair = jax.ShapeDtypeStruct((2, rows, width), BF16)
    work = 2 * 4 * rows * width * hidden
    *part_out, slope = call(
        functools.partial(forward_kernel, reps, quarter),
        [piece] * reps + [jax.ShapeDtypeStruct((4, hidden, rows), BF16)],
        (*aggs, *cots, *weights),
        flops=2 * work,
        nbytes=10 * rows * width * 2,
    )
    *part_in, keep, send = call(
        functools.partial(backward_kernel, reps, quarter),
        [piece] * reps + [pair, pair],
        (*aggs, *cots, *weights, slope),
        flops=3 * work,
        nbytes=10 * rows * width * 2,
    )

    def to_owner(pieces):
        total = pieces[0].astype(F32)
        for s in range(1, reps):
            total = total + swap(pieces[s], "rep", s).astype(F32)
        return total

    def gathered(mine, axis):
        z_piece = swap(mine, "node", 2)
        pieces = (mine, swap(mine, "node", 1), z_piece, swap(z_piece, "node", 1))
        shape = (4 * quarter, width) if axis == 0 else (width, 4 * quarter)
        return call(
            functools.partial(assemble_kernel, axis, quarter, factor),
            jax.ShapeDtypeStruct(shape, F32),
            pieces,
            nbytes=6 * 4 * quarter * width,
        )

    grad_out = gathered(over_groups(to_owner(part_out).astype(BF16)).astype(BF16), 0)
    grad_in = gathered(over_groups(to_owner(part_in).T.astype(BF16)).astype(BF16), 1)

    got = swap(send, "node", 1)
    other = (keep[1].astype(F32) + got[1].astype(F32)).astype(BF16)
    last = swap(other, "node", 2)
    block = jax.ShapeDtypeStruct((rows, width), BF16)
    low, high, own = call(
        tiles_kernel,
        [block, block, jax.ShapeDtypeStruct((rows, width), F32)],
        (keep, got, last, tile_values, tile_cols, tile_count, cotangent),
        [VMEM] * 4 + [SMEM] * 2 + [VMEM],
        [pltpu.VMEM((3, rows, width), F32)],
        flops=2 * 4 * rows * rows * width,
        nbytes=8 * rows * width * 2,
    )
    from_next = shift(low, "node", -1)
    from_prev = shift(high, "node", 1)
    grad_nodes = (own + from_next.astype(F32) + from_prev.astype(F32)).astype(BF16)
    return (grad_nodes, grad_in, grad_out)


def solution(mesh):
    return jax.shard_map(
        local,
        mesh=mesh,
        in_specs=(
            P(("node", "rep"), None),
            P(("node", "rep"), None),
            P(None, "rep"),
            P("rep", None),
            P(("node", "rep"), None, None, None),
            P(("node", "rep"), None),
            P(("node", "rep")),
        ),
        out_specs=(P(("node", "rep"), None), P(None, "rep"), P("rep", None)),
        check_vma=False,
    )
```

time: 93 us -> 68.3 us (0.73)
  between operations: 16.5 us -> 1.44 us
  Pallas kernels: 0 us -> 9.32 us
  local copies, waits for them, and re-layouts: 11.1 us -> 2.57 us
  matrix products: 7.16 us -> 0 us
  waiting for transfers between devices: 28.4 us -> 23.9 us
  starting transfers between devices: 28.3 us -> 29.5 us
    pallas_call x0 -> x6, Pallas kernels: none -> 9.32 us  [call(): pl.pallas_call(kernel, out_shape=outs, in_specs=specs or [VMEM] * len(arg...]
    dot_general x6 -> x0, matrix products: 7.16 us -> none  [the longest x2 3.08 us: contract_last(): lax.dot_general(left, right, (((1,), (1,)), ((), ())), preferred_element_...]
    ppermute x2, waiting for transfers between devices: 7.79 us -> 2.57 us  [shift(): lax.ppermute(block, axis, [(i, (i + step) % count) for i in range(count)])]
    unnamed x16 -> x12, local copies, waits for them, and re-layouts: 6.07 us -> 2.1 us
    slice x5 -> x0, local copies, waits for them, and re-layouts: 2.22 us -> none  [the longest x2 2.08 us: toward(): take = live[slot] & (slot_cols[slot] == target)]
    dynamic_slice x2 -> x0, local copies, waits for them, and re-layouts: 1.83 us -> none  [the longest x1 0.91 us: local(): kin = lax.dynamic_slice_in_dim(kernel_in, me * quarter, quarter, axis=1)]
    ppermute x2, starting transfers between devices: 1.89 us -> 3.59 us  [shift(): lax.ppermute(block, axis, [(i, (i + step) % count) for i in range(count)])]
    ppermute x29 -> x25, waiting for transfers between devices: 20.6 us -> 21.4 us  [swap(): return lax.ppermute(block, axis, [(i, i ^ mask) for i in range(count)])]
  transfers between devices with their start and end apart: 31 -> 27, of which waited for: 10 -> 10; matrix products, arithmetic and copies ran while one was open for 20% -> 1% of each run, Pallas kernels for 0% -> 7%
where the time goes in v2:
time: 68.3 us; the launch traced here: 67.8 us
  starting transfers between devices  29.5 us (43%)
  waiting for transfers between devices  23.9 us (35%)
  Pallas kernels  9.32 us (14%)
  local copies, waits for them, and re-layouts  2.57 us (4%)
  between operations  1.44 us (2%)
  other arithmetic  1.09 us (2%)
    ppermute x25, starting transfers between devices, swap(): return lax.ppermute(block, axis, [(i, i ^ mask) for i in range(count)])  25.9 us
    ppermute x25, waiting for transfers between devices, swap(): return lax.ppermute(block, axis, [(i, i ^ mask) for i in range(count)])  21.4 us
    pallas_call x6, Pallas kernels, call(): pl.pallas_call(kernel, out_shape=outs, in_specs=specs or [VMEM] * len(arg...  9.32 us
    ppermute x2, starting transfers between devices, shift(): lax.ppermute(block, axis, [(i, (i + step) % count) for i in range(count)])  3.59 us
    ppermute x2, waiting for transfers between devices, shift(): lax.ppermute(block, axis, [(i, (i + step) % count) for i in range(count)])  2.57 us
    unnamed x12, local copies, waits for them, and re-layouts  2.1 us
  transfers between devices with their start and end apart: 27, of which 10 were waited for; matrix products, arithmetic and copies ran while one was open for 1% of the time, Pallas kernels for 7%

profile of v2, /device:TPU:0, one launch (start us, length us, event | category | flops | bytes accessed | tf_op | source)
XLA Modules:
  0.0 67.8 jit_solution(8078246340548327436)
XLA Ops:
  1.1 2.6 %collective-permute-start.1 = (bf16[256,512]{1,0:T(8,128)(2,1)}, bf16[256,512]{1,0:T(8,128)(2,1)S(1)}, u32[]{:S(2)}, u32[]{:S(2)}) collective-permute-start(bf16[256,512]{1,0:T(8,128)(2,1)} %refs_0_.3), channel_id=1, source_target_pairs={{0,8},{4,12},{8,0},{12,4},{16,24},{20,28},{24,16},{28,20},{1,9},{5... | collective-permute-start | bytes 786440 | tf_op jit(solution)/shard_map/ppermute | solution.py:38
  4.2 1.0 %copy-done = bf16[512,512]{1,0:T(8,128)(2,1)S(1)} copy-done((bf16[512,512]{1,0:T(8,128)(2,1)S(1)}, bf16[512,512]{1,0:T(8,128)(2,1)}, u32[]{:S(2)}) %copy-start) | copy-done | bytes 524312
  5.3 1.0 %copy-done.1 = bf16[512,512]{1,0:T(8,128)(2,1)S(1)} copy-done((bf16[512,512]{1,0:T(8,128)(2,1)S(1)}, bf16[512,512]{1,0:T(8,128)(2,1)}, u32[]{:S(2)}) %copy-start.1) | copy-done | bytes 524312
  6.6 1.7 %collective-permute-start.6 = (bf16[256,512]{1,0:T(8,128)(2,1)S(1)}, bf16[256,512]{1,0:T(8,128)(2,1)S(1)}, u32[]{:S(2)}, u32[]{:S(2)}) collective-permute-start(bf16[256,512]{1,0:T(8,128)(2,1)S(1)} %shard_map.94.refs_8_), channel_id=1, source_target_pairs={{0,1},{1,0},{2,3},{3,2},{4,5},{5,4},{6,7},{7,6},{8,9},{9,8},{10,11... | collective-permute-start | bytes 786440 | tf_op jit(solution)/shard_map/ppermute | solution.py:38
  8.4 1.5 %collective-permute-start.7 = (bf16[256,512]{1,0:T(8,128)(2,1)S(1)}, bf16[256,512]{1,0:T(8,128)(2,1)S(1)}, u32[]{:S(2)}, u32[]{:S(2)}) collective-permute-start(bf16[256,512]{1,0:T(8,128)(2,1)S(1)} %shard_map.94.refs_8_), channel_id=1, source_target_pairs={{0,2},{1,3},{2,0},{3,1},{4,6},{5,7},{6,4},{7,5},{8,10},{9,11},{10,... | collective-permute-start | bytes 786440 | tf_op jit(solution)/shard_map/ppermute | solution.py:38
  9.9 1.3 %collective-permute-done.1.refs_2_ = bf16[256,512]{1,0:T(8,128)(2,1)S(1)} collective-permute-done((bf16[256,512]{1,0:T(8,128)(2,1)}, bf16[256,512]{1,0:T(8,128)(2,1)S(1)}, u32[]{:S(2)}, u32[]{:S(2)}) %collective-permute-start.1) | collective-permute-done | bytes 262176 | tf_op jit(solution)/shard_map/ppermute | solution.py:38
  11.2 2.8 %collective-permute-start.8 = (bf16[256,512]{1,0:T(8,128)(2,1)S(1)}, bf16[256,512]{1,0:T(8,128)(2,1)S(1)}, u32[]{:S(2)}, u32[]{:S(2)}) collective-permute-start(bf16[256,512]{1,0:T(8,128)(2,1)S(1)} %shard_map.94.refs_8_), channel_id=1, source_target_pairs={{0,3},{1,2},{2,1},{3,0},{4,7},{5,6},{6,5},{7,4},{8,11},{9,10},{10,... | collective-permute-start | bytes 786440 | tf_op jit(solution)/shard_map/ppermute | solution.py:38
  14.0 2.5 %collective-permute-done.4.refs_6_ = bf16[256,512]{1,0:T(8,128)(2,1)S(1)} collective-permute-done((bf16[256,512]{1,0:T(8,128)(2,1)}, bf16[256,512]{1,0:T(8,128)(2,1)S(1)}, u32[]{:S(2)}, u32[]{:S(2)}) %collective-permute-start.4) | collective-permute-done | bytes 262176 | tf_op jit(solution)/shard_map/ppermute | solution.py:38
  16.5 5.4 %collective-permute-done.7.refs_10_ = bf16[256,512]{1,0:T(8,128)(2,1)S(1)} collective-permute-done((bf16[256,512]{1,0:T(8,128)(2,1)S(1)}, bf16[256,512]{1,0:T(8,128)(2,1)S(1)}, u32[]{:S(2)}, u32[]{:S(2)}) %collective-permute-start.7) | collective-permute-done | bytes 262176 | tf_op jit(solution)/shard_map/ppermute | solution.py:38
  22.0 2.2 %shard_map.95 = (bf16[128,512]{1,0:T(8,128)(2,1)S(1)}, bf16[128,512]{1,0:T(8,128)(2,1)S(1)}, bf16[128,512]{1,0:T(8,128)(2,1)S(1)}, bf16[128,512]{1,0:T(8,128)(2,1)S(1)}, bf16[4,512,256]{2,1,0:T(8,128)(2,1)S(1)}) custom-call(bf16[256,512]{1,0:T(8,128)(2,1)S(1)} %copy-done.5, bf16[256,512]{1,0:T(8,128)(2,1)S(1)} %collective-permute-done.refs_1_, ...), custom_call_target="tpu_custom_call" | custom-call | flops 1073741824 | bytes 2621440 | tf_op jit(solution)/shard_map/pallas_call | solution.py:48
  24.2 2.6 %shard_map.96 = (bf16[128,512]{1,0:T(8,128)(2,1)S(1)}, bf16[128,512]{1,0:T(8,128)(2,1)S(1)}, bf16[128,512]{1,0:T(8,128)(2,1)S(1)}, bf16[128,512]{1,0:T(8,128)(2,...) custom-call(bf16[256,512]{1,0:T(8,128)(2,1)S(1)} %copy-done.5, ...), custom_call_target="tpu_custom_call" | custom-call | flops 1610612736 | bytes 2621440 | tf_op jit(solution)/shard_map/pallas_call | solution.py:48
  27.0 1.6 %collective-permute-start.15 = (bf16[128,512]{0,1:T(8,128)(2,1)S(1)}, bf16[128,512]{0,1:T(8,128)(2,1)S(1)}, u32[]{:S(2)}, u32[]{:S(2)}) collective-permute-start(bf16[128,512]{0,1:T(8,128)(2,1)S(1)} %copy.13), channel_id=1, source_target_pairs={{0,3},{1,2},{2,1},{3,0},{4,7},{5,6},{6,5},{7,4},{8,11},{9,10},{10,... | collective-permute-start | bytes 393224 | tf_op jit(solution)/shard_map/ppermute | solution.py:38
  28.6 1.3 %collective-permute-start.14 = (bf16[128,512]{0,1:T(8,128)(2,1)S(1)}, bf16[128,512]{0,1:T(8,128)(2,1)S(1)}, u32[]{:S(2)}, u32[]{:S(2)}) collective-permute-start(bf16[128,512]{0,1:T(8,128)(2,1)S(1)} %copy.12), channel_id=1, source_target_pairs={{0,2},{1,3},{2,0},{3,1},{4,6},{5,7},{6,4},{7,5},{8,10},{9,11},{10,... | collective-permute-start | bytes 393224 | tf_op jit(solution)/shard_map/ppermute | solution.py:38
  30.0 0.9 %collective-permute-start.13 = (bf16[128,512]{0,1:T(8,128)(2,1)S(1)}, bf16[128,512]{0,1:T(8,128)(2,1)S(1)}, u32[]{:S(2)}, u32[]{:S(2)}) collective-permute-start(bf16[128,512]{0,1:T(8,128)(2,1)S(1)} %copy.11), channel_id=1, source_target_pairs={{0,1},{1,0},{2,3},{3,2},{4,5},{5,4},{6,7},{7,6},{8,9},{9,8},{10,11... | collective-permute-start | bytes 393224 | tf_op jit(solution)/shard_map/ppermute | solution.py:38
  31.7 1.6 %collective-permute-start.22 = (bf16[128,512]{1,0:T(8,128)(2,1)S(1)}, bf16[128,512]{1,0:T(8,128)(2,1)S(1)}, u32[]{:S(2)}, u32[]{:S(2)}) collective-permute-start(bf16[128,512]{1,0:T(8,128)(2,1)S(1)} %get-tuple-element.30), channel_id=1, source_target_pairs={{0,3},{1,2},{2,1},{3,0},{4,7},{5,6},{6,5},{7,4},{8,11},{9,10},{10,... | collective-permute-start | bytes 393224 | tf_op jit(solution)/shard_map/ppermute | solution.py:38
  33.2 0.9 %collective-permute-done.15 = bf16[128,512]{0,1:T(8,128)(2,1)S(1)} collective-permute-done((bf16[128,512]{0,1:T(8,128)(2,1)S(1)}, bf16[128,512]{0,1:T(8,128)(2,1)S(1)}, u32[]{:S(2)}, u32[]{:S(2)}) %collective-permute-start.15) | collective-permute-done | bytes 131104 | tf_op jit(solution)/shard_map/ppermute | solution.py:38
  34.2 1.6 %collective-permute-start.21 = (bf16[128,512]{1,0:T(8,128)(2,1)S(1)}, bf16[128,512]{1,0:T(8,128)(2,1)S(1)}, u32[]{:S(2)}, u32[]{:S(2)}) collective-permute-start(bf16[128,512]{1,0:T(8,128)(2,1)S(1)} %get-tuple-element.29), channel_id=1, source_target_pairs={{0,2},{1,3},{2,0},{3,1},{4,6},{5,7},{6,4},{7,5},{8,10},{9,11},{10,... | collective-permute-start | bytes 393224 | tf_op jit(solution)/shard_map/ppermute | solution.py:38
  35.7 0.9 %collective-permute-start.20 = (bf16[128,512]{1,0:T(8,128)(2,1)S(1)}, bf16[128,512]{1,0:T(8,128)(2,1)S(1)}, u32[]{:S(2)}, u32[]{:S(2)}) collective-permute-start(bf16[128,512]{1,0:T(8,128)(2,1)S(1)} %get-tuple-element.28), channel_id=1, source_target_pairs={{0,1},{1,0},{2,3},{3,2},{4,5},{5,4},{6,7},{7,6},{8,9},{9,8},{10,11... | collective-permute-start | bytes 393224 | tf_op jit(solution)/shard_map/ppermute | solution.py:38
  36.7 2.4 %collective-permute-start.16 = (bf16[512,128]{1,0:T(8,128)(2,1)S(1)}, bf16[512,128]{1,0:T(8,128)(2,1)S(1)}, u32[]{:S(2)}, u32[]{:S(2)}) collective-permute-start(bf16[512,128]{1,0:T(8,128)(2,1)S(1)} %fusion.1), channel_id=1, source_target_pairs={{0,16},{4,20},{8,24},{12,28},{16,0},{20,4},{24,8},{28,12},{1,17},{... | collective-permute-start | bytes 393224 | tf_op jit(solution)/shard_map/ppermute | solution.py:38
  39.0 2.3 %collective-permute-done.21 = bf16[128,512]{1,0:T(8,128)(2,1)S(1)} collective-permute-done((bf16[128,512]{1,0:T(8,128)(2,1)S(1)}, bf16[128,512]{1,0:T(8,128)(2,1)S(1)}, u32[]{:S(2)}, u32[]{:S(2)}) %collective-permute-start.21) | collective-permute-done | bytes 131104 | tf_op jit(solution)/shard_map/ppermute | solution.py:38
  41.5 2.7 %collective-permute-start.23 = (bf16[128,512]{1,0:T(8,128)(2,1)S(1)}, bf16[128,512]{1,0:T(8,128)(2,1)S(1)}, u32[]{:S(2)}, u32[]{:S(2)}) collective-permute-start(bf16[128,512]{1,0:T(8,128)(2,1)S(1)} %add_convert_fusion.3), channel_id=1, source_target_pairs={{0,16},{4,20},{8,24},{12,28},{16,0},{20,4},{24,8},{28,12},{1,17},{... | collective-permute-start | bytes 393224 | tf_op jit(solution)/shard_map/ppermute | solution.py:38
  44.3 1.6 %collective-permute-start.10 = (bf16[256,512]{1,0:T(8,128)(2,1)S(1)}, bf16[256,512]{1,0:T(8,128)(2,1)S(1)}, u32[]{:S(2)}, u32[]{:S(2)}) collective-permute-start(bf16[256,512]{1,0:T(8,128)(2,1)S(1)} %fusion), channel_id=1, source_target_pairs={{0,8},{4,12},{8,0},{12,4},{16,24},{20,28},{24,16},{28,20},{1,9},{5... | collective-permute-start | bytes 786440 | tf_op jit(solution)/shard_map/ppermute | solution.py:38
  46.6 4.2 %collective-permute-done.23 = bf16[128,512]{1,0:T(8,128)(2,1)S(1)} collective-permute-done((bf16[128,512]{1,0:T(8,128)(2,1)S(1)}, bf16[128,512]{1,0:T(8,128)(2,1)S(1)}, u32[]{:S(2)}, u32[]{:S(2)}) %collective-permute-start.23) | collective-permute-done | bytes 131104 | tf_op jit(solution)/shard_map/ppermute | solution.py:38
  50.8 0.7 %collective-permute-start.25 = (bf16[128,512]{1,0:T(8,128)(2,1)S(1)}, bf16[128,512]{1,0:T(8,128)(2,1)S(1)}, u32[]{:S(2)}, u32[]{:S(2)}) collective-permute-start(bf16[128,512]{1,0:T(8,128)(2,1)S(1)} %add_convert_fusion.2.refs_0_), channel_id=1, source_target_pairs={{0,8},{4,12},{8,0},{12,4},{16,24},{20,28},{24,16},{28,20},{1,9},{5... | collective-permute-start | bytes 393224 | tf_op jit(solution)/shard_map/ppermute | solution.py:38
  51.5 3.8 %collective-permute-done.10.last_ref = bf16[256,512]{1,0:T(8,128)(2,1)S(1)} collective-permute-done((bf16[256,512]{1,0:T(8,128)(2,1)S(1)}, bf16[256,512]{1,0:T(8,128)(2,1)S(1)}, u32[]{:S(2)}, u32[]{:S(2)}) %collective-permute-start.10) | collective-permute-done | bytes 262176 | tf_op jit(solution)/shard_map/ppermute | solution.py:38
  55.3 1.9 %shard_map.97 = (bf16[256,512]{1,0:T(8,128)(2,1)S(1)}, bf16[256,512]{1,0:T(8,128)(2,1)S(1)}, f32[256,512]{1,0:T(8,128)S(1)}) custom-call(bf16[2,256,512]{2,1,0:T(8,128)(2,1)S(1)} %get-tuple-element.18.keep_ref, bf16[2,256,512]{2,1,0:T(8,128)(2,1)S(1)} %collective-permute-done.9.got_ref, bf16[256,512]{1,0:T(8,128)(2,1)S(1)} %collective-permute-done.10.last_ref, ...), custom_call_target="tpu_custom_call" | custom-call | flops 268435456 | bytes 2097152 | tf_op jit(solution)/shard_map/pallas_call | solution.py:48
  57.2 3.5 %collective-permute-start.11 = (bf16[256,512]{1,0:T(8,128)(2,1)S(1)}, bf16[256,512]{1,0:T(8,128)(2,1)S(1)}, u32[]{:S(2)}, u32[]{:S(2)}) collective-permute-start(bf16[256,512]{1,0:T(8,128)(2,1)S(1)} %get-tuple-element.21), channel_id=1, source_target_pairs={{0,28},{4,0},{8,4},{12,8},{16,12},{20,16},{24,20},{28,24},{1,29},{... | collective-permute-start | bytes 786440 | tf_op jit(solution)/shard_map/ppermute | solution.py:43
  61.3 0.8 %collective-permute-done.19.refs_3_ = bf16[512,128]{1,0:T(8,128)(2,1)S(1)} collective-permute-done((bf16[512,128]{1,0:T(8,128)(2,1)S(1)}, bf16[512,128]{1,0:T(8,128)(2,1)S(1)}, u32[]{:S(2)}, u32[]{:S(2)}) %collective-permute-start.19) | collective-permute-done | bytes 131104 | tf_op jit(solution)/shard_map/ppermute | solution.py:38
  62.1 1.2 %shard_map.98 = f32[512,512]{1,0:T(8,128)} custom-call(bf16[512,128]{1,0:T(8,128)(2,1)S(1)} %add_convert_fusion.4.refs_0_, bf16[512,128]{1,0:T(8,128)(2,1)S(1)} %collective-permute-done.17.refs_1_, bf16[512,128]{1,0:T(8,128)(2,1)S(1)} %collective-permute-done.18.refs_2_, bf16[512,128]{1,0:T(8,128)(2,1)S(1)} %collective-permute-done.19.refs_3_), custom_call_target="tpu_custom_call" | custom-call | bytes 1572864 | tf_op jit(solution)/shard_map/pallas_call | solution.py:48
  63.3 1.1 %shard_map.99 = f32[512,512]{1,0:T(8,128)} custom-call(bf16[128,512]{1,0:T(8,128)(2,1)S(1)} %add_convert_fusion.2.refs_0_, bf16[128,512]{1,0:T(8,128)(2,1)S(1)} %collective-permute-done.24.refs_1_, bf16[128,512]{1,0:T(8,128)(2,1)S(1)} %collective-permute-done.25.refs_2_, bf16[128,512]{1,0:T(8,128)(2,1)S(1)} %collective-permute-done.26.refs_3_), custom_call_target="tpu_custom_call" | custom-call | bytes 1572864 | tf_op jit(solution)/shard_map/pallas_call | solution.py:48
  64.4 2.6 %collective-permute-done.12 = bf16[256,512]{1,0:T(8,128)(2,1)S(1)} collective-permute-done((bf16[256,512]{1,0:T(8,128)(2,1)S(1)}, bf16[256,512]{1,0:T(8,128)(2,1)S(1)}, u32[]{:S(2)}, u32[]{:S(2)}) %collective-permute-start.12) | collective-permute-done | bytes 262176 | tf_op jit(solution)/shard_map/ppermute | solution.py:43
  67.0 0.8 %add_convert_fusion = bf16[256,512]{1,0:T(8,128)(2,1)} fusion(bf16[256,512]{1,0:T(8,128)(2,1)S(1)} %collective-permute-done.12, f32[256,512]{1,0:T(8,128)S(1)} %get-tuple-element.20, bf16[256,512]{1,0:T(8,128)(2,1)S(1)} %collective-permute-done.11), kind=kLoop, calls=%fused_computation | loop fusion | flops 655360 | bytes 1310720 | tf_op jit(solution)/shard_map/convert_element_type | solution.py:240
  (50 shorter events, 3.4 us)
Async XLA Ops:
  0.6 7.7 %collective-permute-start = (bf16[256,512]{1,0:T(8,128)(2,1)}, bf16[256,512]{1,0:T(8,128)(2,1)S(1)}, u32[]{:S(2)}, u32[]{:S(2)}) collective-permute-start(bf16[256,512]{1,0:T(8,128)(2,1)} %refs_0_.3), channel_id=1, source_target_pairs={{0,4},{4,0},{8,12},{12,8},{16,20},{20,16},{24,28},{28,24},{1,5},{5... | collective-permute-start | bytes 786440 | tf_op jit(solution)/shard_map/ppermute | solution.py:38
  1.1 10.0 %collective-permute-start.1 = (bf16[256,512]{1,0:T(8,128)(2,1)}, bf16[256,512]{1,0:T(8,128)(2,1)S(1)}, u32[]{:S(2)}, u32[]{:S(2)}) collective-permute-start(bf16[256,512]{1,0:T(8,128)(2,1)} %refs_0_.3), channel_id=1, source_target_pairs={{0,8},{4,12},{8,0},{12,4},{16,24},{20,28},{24,16},{28,20},{1,9},{5... | collective-permute-start | bytes 786440 | tf_op jit(solution)/shard_map/ppermute | solution.py:38
  3.8 10.2 %collective-permute-start.3 = (bf16[256,512]{1,0:T(8,128)(2,1)}, bf16[256,512]{1,0:T(8,128)(2,1)S(1)}, u32[]{:S(2)}, u32[]{:S(2)}) collective-permute-start(bf16[256,512]{1,0:T(8,128)(2,1)} %cot_ref.1), channel_id=1, source_target_pairs={{0,4},{4,0},{8,12},{12,8},{16,20},{20,16},{24,28},{28,24},{1,5},{5... | collective-permute-start | bytes 786440 | tf_op jit(solution)/shard_map/ppermute | solution.py:38
  4.0 12.6 %collective-permute-start.4 = (bf16[256,512]{1,0:T(8,128)(2,1)}, bf16[256,512]{1,0:T(8,128)(2,1)S(1)}, u32[]{:S(2)}, u32[]{:S(2)}) collective-permute-start(bf16[256,512]{1,0:T(8,128)(2,1)} %cot_ref.1), channel_id=1, source_target_pairs={{0,8},{4,12},{8,0},{12,4},{16,24},{20,28},{24,16},{28,20},{1,9},{5... | collective-permute-start | bytes 786440 | tf_op jit(solution)/shard_map/ppermute | solution.py:38
  4.2 1.0 %copy-start = (bf16[512,512]{1,0:T(8,128)(2,1)S(1)}, bf16[512,512]{1,0:T(8,128)(2,1)}, u32[]{:S(2)}) copy-start(bf16[512,512]{1,0:T(8,128)(2,1)} %kin_ref.1) | copy-start | bytes 1572868
  6.3 15.7 %copy-start.3 = (bf16[256,512]{1,0:T(8,128)(2,1)S(1)}, bf16[256,512]{1,0:T(8,128)(2,1)}, u32[]{:S(2)}) copy-start(bf16[256,512]{1,0:T(8,128)(2,1)} %cot_ref.1) | copy-start | bytes 786436
  6.3 15.7 %copy-start.5 = (bf16[256,512]{1,0:T(8,128)(2,1)S(1)}, bf16[256,512]{1,0:T(8,128)(2,1)}, u32[]{:S(2)}) copy-start(bf16[256,512]{1,0:T(8,128)(2,1)} %refs_0_.3) | copy-start | bytes 786436
  6.6 9.9 %collective-permute-start.6 = (bf16[256,512]{1,0:T(8,128)(2,1)S(1)}, bf16[256,512]{1,0:T(8,128)(2,1)S(1)}, u32[]{:S(2)}, u32[]{:S(2)}) collective-permute-start(bf16[256,512]{1,0:T(8,128)(2,1)S(1)} %shard_map.94.refs_8_), channel_id=1, source_target_pairs={{0,1},{1,0},{2,3},{3,2},{4,5},{5,4},{6,7},{7,6},{8,9},{9,8},{10,11... | collective-permute-start | bytes 786440 | tf_op jit(solution)/shard_map/ppermute | solution.py:38
  8.4 13.6 %collective-permute-start.7 = (bf16[256,512]{1,0:T(8,128)(2,1)S(1)}, bf16[256,512]{1,0:T(8,128)(2,1)S(1)}, u32[]{:S(2)}, u32[]{:S(2)}) collective-permute-start(bf16[256,512]{1,0:T(8,128)(2,1)S(1)} %shard_map.94.refs_8_), channel_id=1, source_target_pairs={{0,2},{1,3},{2,0},{3,1},{4,6},{5,7},{6,4},{7,5},{8,10},{9,11},{10,... | collective-permute-start | bytes 786440 | tf_op jit(solution)/shard_map/ppermute | solution.py:38
  11.2 10.8 %collective-permute-start.8 = (bf16[256,512]{1,0:T(8,128)(2,1)S(1)}, bf16[256,512]{1,0:T(8,128)(2,1)S(1)}, u32[]{:S(2)}, u32[]{:S(2)}) collective-permute-start(bf16[256,512]{1,0:T(8,128)(2,1)S(1)} %shard_map.94.refs_8_), channel_id=1, source_target_pairs={{0,3},{1,2},{2,1},{3,0},{4,7},{5,6},{6,5},{7,4},{8,11},{9,10},{10,... | collective-permute-start | bytes 786440 | tf_op jit(solution)/shard_map/ppermute | solution.py:38
  14.0 8.0 %collective-permute-start.2 = (bf16[256,512]{1,0:T(8,128)(2,1)S(1)}, bf16[256,512]{1,0:T(8,128)(2,1)S(1)}, u32[]{:S(2)}, u32[]{:S(2)}) collective-permute-start(bf16[256,512]{1,0:T(8,128)(2,1)S(1)} %collective-permute-done.1.refs_2_), channel_id=1, source_target_pairs={{0,4},{4,0},{8,12},{12,8},{16,20},{20,16},{24,28},{28,24},{1,5},{5... | collective-permute-start | bytes 786440 | tf_op jit(solution)/shard_map/ppermute | solution.py:38
  16.5 5.5 %collective-permute-start.5 = (bf16[256,512]{1,0:T(8,128)(2,1)S(1)}, bf16[256,512]{1,0:T(8,128)(2,1)S(1)}, u32[]{:S(2)}, u32[]{:S(2)}) collective-permute-start(bf16[256,512]{1,0:T(8,128)(2,1)S(1)} %collective-permute-done.4.refs_6_), channel_id=1, source_target_pairs={{0,4},{4,0},{8,12},{12,8},{16,20},{20,16},{24,28},{28,24},{1,5},{5... | collective-permute-start | bytes 786440 | tf_op jit(solution)/shard_map/ppermute | solution.py:38
  27.0 7.2 %collective-permute-start.15 = (bf16[128,512]{0,1:T(8,128)(2,1)S(1)}, bf16[128,512]{0,1:T(8,128)(2,1)S(1)}, u32[]{:S(2)}, u32[]{:S(2)}) collective-permute-start(bf16[128,512]{0,1:T(8,128)(2,1)S(1)} %copy.13), channel_id=1, source_target_pairs={{0,3},{1,2},{2,1},{3,0},{4,7},{5,6},{6,5},{7,4},{8,11},{9,10},{10,... | collective-permute-start | bytes 393224 | tf_op jit(solution)/shard_map/ppermute | solution.py:38
  28.6 7.1 %collective-permute-start.14 = (bf16[128,512]{0,1:T(8,128)(2,1)S(1)}, bf16[128,512]{0,1:T(8,128)(2,1)S(1)}, u32[]{:S(2)}, u32[]{:S(2)}) collective-permute-start(bf16[128,512]{0,1:T(8,128)(2,1)S(1)} %copy.12), channel_id=1, source_target_pairs={{0,2},{1,3},{2,0},{3,1},{4,6},{5,7},{6,4},{7,5},{8,10},{9,11},{10,... | collective-permute-start | bytes 393224 | tf_op jit(solution)/shard_map/ppermute | solution.py:38
  30.0 6.6 %collective-permute-start.13 = (bf16[128,512]{0,1:T(8,128)(2,1)S(1)}, bf16[128,512]{0,1:T(8,128)(2,1)S(1)}, u32[]{:S(2)}, u32[]{:S(2)}) collective-permute-start(bf16[128,512]{0,1:T(8,128)(2,1)S(1)} %copy.11), channel_id=1, source_target_pairs={{0,1},{1,0},{2,3},{3,2},{4,5},{5,4},{6,7},{7,6},{8,9},{9,8},{10,11... | collective-permute-start | bytes 393224 | tf_op jit(solution)/shard_map/ppermute | solution.py:38
  30.9 13.3 %collective-permute-start.9 = (bf16[2,256,512]{2,1,0:T(8,128)(2,1)S(1)}, bf16[2,256,512]{2,1,0:T(8,128)(2,1)S(1)}, u32[]{:S(2)}, u32[]{:S(2)}) collective-permute-start(bf16[2,256,512]{2,1,0:T(8,128)(2,1)S(1)} %get-tuple-element.19), channel_id=1, source_target_pairs={{0,4},{4,0},{8,12},{12,8},{16,20},{20,16},{24,28},{28,24},{1,5},{5... | collective-permute-start | bytes 1572872 | tf_op jit(solution)/shard_map/ppermute | solution.py:38
  31.7 7.4 %collective-permute-start.22 = (bf16[128,512]{1,0:T(8,128)(2,1)S(1)}, bf16[128,512]{1,0:T(8,128)(2,1)S(1)}, u32[]{:S(2)}, u32[]{:S(2)}) collective-permute-start(bf16[128,512]{1,0:T(8,128)(2,1)S(1)} %get-tuple-element.30), channel_id=1, source_target_pairs={{0,3},{1,2},{2,1},{3,0},{4,7},{5,6},{6,5},{7,4},{8,11},{9,10},{10,... | collective-permute-start | bytes 393224 | tf_op jit(solution)/shard_map/ppermute | solution.py:38
  34.2 7.2 %collective-permute-start.21 = (bf16[128,512]{1,0:T(8,128)(2,1)S(1)}, bf16[128,512]{1,0:T(8,128)(2,1)S(1)}, u32[]{:S(2)}, u32[]{:S(2)}) collective-permute-start(bf16[128,512]{1,0:T(8,128)(2,1)S(1)} %get-tuple-element.29), channel_id=1, source_target_pairs={{0,2},{1,3},{2,0},{3,1},{4,6},{5,7},{6,4},{7,5},{8,10},{9,11},{10,... | collective-permute-start | bytes 393224 | tf_op jit(solution)/shard_map/ppermute | solution.py:38
  35.7 5.7 %collective-permute-start.20 = (bf16[128,512]{1,0:T(8,128)(2,1)S(1)}, bf16[128,512]{1,0:T(8,128)(2,1)S(1)}, u32[]{:S(2)}, u32[]{:S(2)}) collective-permute-start(bf16[128,512]{1,0:T(8,128)(2,1)S(1)} %get-tuple-element.28), channel_id=1, source_target_pairs={{0,1},{1,0},{2,3},{3,2},{4,5},{5,4},{6,7},{7,6},{8,9},{9,8},{10,11... | collective-permute-start | bytes 393224 | tf_op jit(solution)/shard_map/ppermute | solution.py:38
  36.7 9.3 %collective-permute-start.16 = (bf16[512,128]{1,0:T(8,128)(2,1)S(1)}, bf16[512,128]{1,0:T(8,128)(2,1)S(1)}, u32[]{:S(2)}, u32[]{:S(2)}) collective-permute-start(bf16[512,128]{1,0:T(8,128)(2,1)S(1)} %fusion.1), channel_id=1, source_target_pairs={{0,16},{4,20},{8,24},{12,28},{16,0},{20,4},{24,8},{28,12},{1,17},{... | collective-permute-start | bytes 393224 | tf_op jit(solution)/shard_map/ppermute | solution.py:38
  41.5 9.2 %collective-permute-start.23 = (bf16[128,512]{1,0:T(8,128)(2,1)S(1)}, bf16[128,512]{1,0:T(8,128)(2,1)S(1)}, u32[]{:S(2)}, u32[]{:S(2)}) collective-permute-start(bf16[128,512]{1,0:T(8,128)(2,1)S(1)} %add_convert_fusion.3), channel_id=1, source_target_pairs={{0,16},{4,20},{8,24},{12,28},{16,0},{20,4},{24,8},{28,12},{1,17},{... | collective-permute-start | bytes 393224 | tf_op jit(solution)/shard_map/ppermute | solution.py:38
  44.3 11.0 %copy-start.2 = (bf16[1,4,256,256]{3,2,1,0:T(8,128)(2,1)S(1)}, bf16[1,4,256,256]{3,2,1,0:T(8,128)(2,1)}, u32[]{:S(2)}) copy-start(bf16[1,4,256,256]{3,2,1,0:T(8,128)(2,1)} %tiles_ref.1) | copy-start | bytes 1572868
  44.3 11.0 %collective-permute-start.10 = (bf16[256,512]{1,0:T(8,128)(2,1)S(1)}, bf16[256,512]{1,0:T(8,128)(2,1)S(1)}, u32[]{:S(2)}, u32[]{:S(2)}) collective-permute-start(bf16[256,512]{1,0:T(8,128)(2,1)S(1)} %fusion), channel_id=1, source_target_pairs={{0,8},{4,12},{8,0},{12,4},{16,24},{20,28},{24,16},{28,20},{1,9},{5... | collective-permute-start | bytes 786440 | tf_op jit(solution)/shard_map/ppermute | solution.py:38
  46.0 9.3 %copy-start.4 = (s32[1,4]{1,0:T(1,128)S(1)}, s32[1,4]{1,0:T(1,128)}, u32[]{:S(2)}) copy-start(s32[1,4]{1,0:T(1,128)} %cols_ref.1) | copy-start | bytes 52
  46.0 14.8 %collective-permute-start.17 = (bf16[512,128]{1,0:T(8,128)(2,1)S(1)}, bf16[512,128]{1,0:T(8,128)(2,1)S(1)}, u32[]{:S(2)}, u32[]{:S(2)}) collective-permute-start(bf16[512,128]{1,0:T(8,128)(2,1)S(1)} %add_convert_fusion.4.refs_0_), channel_id=1, source_target_pairs={{0,4},{4,0},{8,12},{12,8},{16,20},{20,16},{24,28},{28,24},{1,5},{5... | collective-permute-start | bytes 393224 | tf_op jit(solution)/shard_map/ppermute | solution.py:38
  46.1 14.7 %collective-permute-start.18 = (bf16[512,128]{1,0:T(8,128)(2,1)S(1)}, bf16[512,128]{1,0:T(8,128)(2,1)S(1)}, u32[]{:S(2)}, u32[]{:S(2)}) collective-permute-start(bf16[512,128]{1,0:T(8,128)(2,1)S(1)} %add_convert_fusion.4.refs_0_), channel_id=1, source_target_pairs={{0,8},{4,12},{8,0},{12,4},{16,24},{20,28},{24,16},{28,20},{1,9},{5... | collective-permute-start | bytes 393224 | tf_op jit(solution)/shard_map/ppermute | solution.py:38
  50.8 10.5 %collective-permute-start.25 = (bf16[128,512]{1,0:T(8,128)(2,1)S(1)}, bf16[128,512]{1,0:T(8,128)(2,1)S(1)}, u32[]{:S(2)}, u32[]{:S(2)}) collective-permute-start(bf16[128,512]{1,0:T(8,128)(2,1)S(1)} %add_convert_fusion.2.refs_0_), channel_id=1, source_target_pairs={{0,8},{4,12},{8,0},{12,4},{16,24},{20,28},{24,16},{28,20},{1,9},{5... | collective-permute-start | bytes 393224 | tf_op jit(solution)/shard_map/ppermute | solution.py:38
  57.2 9.8 %collective-permute-start.12 = (bf16[256,512]{1,0:T(8,128)(2,1)S(1)}, bf16[256,512]{1,0:T(8,128)(2,1)S(1)}, u32[]{:S(2)}, u32[]{:S(2)}) collective-permute-start(bf16[256,512]{1,0:T(8,128)(2,1)S(1)} %get-tuple-element.22), channel_id=1, source_target_pairs={{0,4},{4,8},{8,12},{12,16},{16,20},{20,24},{24,28},{28,0},{1,5},{5... | collective-permute-start | bytes 786440 | tf_op jit(solution)/shard_map/ppermute | solution.py:43
  57.2 9.8 %collective-permute-start.11 = (bf16[256,512]{1,0:T(8,128)(2,1)S(1)}, bf16[256,512]{1,0:T(8,128)(2,1)S(1)}, u32[]{:S(2)}, u32[]{:S(2)}) collective-permute-start(bf16[256,512]{1,0:T(8,128)(2,1)S(1)} %get-tuple-element.21), channel_id=1, source_target_pairs={{0,28},{4,0},{8,4},{12,8},{16,12},{20,16},{24,20},{28,24},{1,29},{... | collective-permute-start | bytes 786440 | tf_op jit(solution)/shard_map/ppermute | solution.py:43
  60.8 1.3 %collective-permute-start.19 = (bf16[512,128]{1,0:T(8,128)(2,1)S(1)}, bf16[512,128]{1,0:T(8,128)(2,1)S(1)}, u32[]{:S(2)}, u32[]{:S(2)}) collective-permute-start(bf16[512,128]{1,0:T(8,128)(2,1)S(1)} %collective-permute-done.18.refs_2_), channel_id=1, source_target_pairs={{0,4},{4,0},{8,12},{12,8},{16,20},{20,16},{24,28},{28,24},{1,5},{5... | collective-permute-start | bytes 393224 | tf_op jit(solution)/shard_map/ppermute | solution.py:38
  60.8 2.5 %collective-permute-start.24 = (bf16[128,512]{1,0:T(8,128)(2,1)S(1)}, bf16[128,512]{1,0:T(8,128)(2,1)S(1)}, u32[]{:S(2)}, u32[]{:S(2)}) collective-permute-start(bf16[128,512]{1,0:T(8,128)(2,1)S(1)} %add_convert_fusion.2.refs_0_), channel_id=1, source_target_pairs={{0,4},{4,0},{8,12},{12,8},{16,20},{20,16},{24,28},{28,24},{1,5},{5... | collective-permute-start | bytes 393224 | tf_op jit(solution)/shard_map/ppermute | solution.py:38
  61.3 2.0 %collective-permute-start.26 = (bf16[128,512]{1,0:T(8,128)(2,1)S(1)}, bf16[128,512]{1,0:T(8,128)(2,1)S(1)}, u32[]{:S(2)}, u32[]{:S(2)}) collective-permute-start(bf16[128,512]{1,0:T(8,128)(2,1)S(1)} %collective-permute-done.25.refs_2_), channel_id=1, source_target_pairs={{0,4},{4,0},{8,12},{12,8},{16,20},{20,16},{24,28},{28,24},{1,5},{5... | collective-permute-start | bytes 393224 | tf_op jit(solution)/shard_map/ppermute | solution.py:38
  (1 other events, 1.0 us)

commit v3 on v1

v3 whole, which is shorter than its diff:
```python
import functools
import math

import jax
import jax.numpy as jnp
from jax import lax
from jax.experimental import pallas as pl
from jax.experimental.pallas import tpu as pltpu
from jax.sharding import PartitionSpec as P

BF16 = jnp.bfloat16
F32 = jnp.float32
VMEM = pl.BlockSpec(memory_space=pltpu.VMEM)
SMEM = pl.BlockSpec(memory_space=pltpu.SMEM)
COST = {'in': 0.1, 'place_out': 0.1, 'out': 8, 'middle': 8, 'sum_out': 25, 'add_out': 1, 'add_in': 3, 'forward': 1, 'sum_in': 25, 'place_in': 1, 'tiles': 0.1, 'other': 0.1, 'gate_cot': 1, 'lift': 9, 'own': 3, 'split_out': 25}
ORDER = ['gate_agg', 'need_ykin', 'gate_cot', 'forward', 'tiny', 'out', 'in', 'own', 'split_out', 'middle', 'other', 'sum_out', 'tiles', 'sum_in', 'final', 'add_out', 'place_out', 'add_in', 'place_in']
ANY = pl.BlockSpec(memory_space=pl.ANY)


def gelu_both(pre_act):
    root = math.sqrt(2.0 / math.pi)
    square = pre_act * pre_act
    half = 0.5 + 0.5 * jnp.tanh(pre_act * (root + (root * 0.044715) * square))
    value = pre_act * half
    slope = half + (value - value * half) * (2.0 * root + (6.0 * root * 0.044715) * square)
    return value, slope


def product(left, right, left_dim, right_dim):
    return lax.dot_general(
        left, right, (((left_dim,), (right_dim,)), ((), ())), preferred_element_type=F32
    )


def swap(block, axis, mask):
    count = lax.axis_size(axis)
    return lax.ppermute(block, axis, [(i, i ^ mask) for i in range(count)])


def shift(block, axis, step):
    count = lax.axis_size(axis)
    return lax.ppermute(block, axis, [(i, (i + step) % count) for i in range(count)])


def call(name, kernel, outs, args, after=(), specs=None, scratch=()):
    single = not isinstance(outs, (list, tuple))
    return pl.pallas_call(
        kernel,
        out_shape=outs,
        in_specs=(specs or [VMEM] * len(args)) + [ANY] * len(after),
        out_specs=VMEM if single else [VMEM] * len(outs),
        scratch_shapes=list(scratch),
        compiler_params=pltpu.CompilerParams(vmem_limit_bytes=40 * 1024 * 1024),
        cost_estimate=pl.CostEstimate(
            flops=int(1e9 * COST.get(name, 0.1)), bytes_accessed=0, transcendentals=0
        ),
        name=name,
    )(*args, *after)


def core():
    return lax.rem(lax.axis_index("node"), 2)


def joined(refs, turn=False):
    blocks = [ref[...].T if turn else ref[...] for ref in refs]
    return blocks[0] if len(blocks) == 1 else jnp.concatenate(blocks, axis=0)


def both_kernel(own_ref, far_ref, *refs):
    refs[-1][0] = own_ref[...]
    refs[-1][1] = far_ref[...]


def blocks(own_ref, far_ref, other_ref):
    return own_ref, other_ref.at[0], far_ref, other_ref.at[1]


def forward_kernel(pieces, *refs):
    aggs, weights, (act_ref, slope_ref) = blocks(*refs[:3]), refs[3 : 3 + pieces], refs[-2:]
    w_in = joined(weights, True)
    for j in range(4):
        value, slope = gelu_both(product(w_in, aggs[j][...], 1, 1))
        act_ref[j] = value.astype(BF16)
        slope_ref[j] = slope.astype(BF16)


def odd_z():
    return lax.rem(lax.axis_index("node"), 4) >= 2


def out_term(act_ref, rows, cots):
    total = product(act_ref[0, rows], cots[0][...], 1, 0)
    for j in range(1, 4):
        total = total + product(act_ref[j, rows], cots[j][...], 1, 0)
    return total


def out_kernel(pieces, *refs):
    act_ref, outs = refs[0], refs[-pieces:]
    half = outs[0].shape[0]
    total = out_term(act_ref, slice(half, None), blocks(*refs[1:4]))
    for i, ref in enumerate(outs):
        ref[...] = total[i * half : (i + 1) * half].astype(BF16)


def in_kernel(pieces, *refs):
    slope_ref, aggs, cots = refs[0], blocks(*refs[1:4]), blocks(*refs[4:7])
    weights = refs[7 : 7 + pieces]
    grad_ref, keep_ref, send_ref = refs[-3:]
    w_out = joined(weights)
    total = None
    for j in range(4):
        grad_act = product(w_out, cots[j][...], 1, 1)
        grad_pre = (grad_act * slope_ref[j].astype(F32)).astype(BF16)
        grad_ref[j] = grad_pre
        term = product(grad_pre, aggs[j][...], 1, 0)
        total = term if j == 0 else total + term
    quarter = keep_ref.shape[0] // pieces
    odd = odd_z()
    for i in range(pieces):
        low = total[2 * i * quarter : (2 * i + 1) * quarter]
        high = total[(2 * i + 1) * quarter : (2 * i + 2) * quarter]
        rows = slice(i * quarter, (i + 1) * quarter)
        keep_ref[rows] = jnp.where(odd, high, low)
        send_ref[rows] = jnp.where(odd, low, high).astype(BF16)


def own_kernel(pieces, *refs):
    act_ref, cots, grad_ref = refs[0], blocks(*refs[1:4]), refs[4]
    weights = refs[5 : 5 + pieces]
    out_ref, keep_ref, send_ref = refs[-3:]
    out_ref[...] = out_term(act_ref, slice(0, out_ref.shape[0]), cots)
    w_in = joined(weights, True)
    for j in range(4):
        rows = product(grad_ref[j], w_in, 0, 0)
        (send_ref if j % 2 else keep_ref)[j // 2] = rows.astype(BF16)


def middle_kernel(pieces, *refs):
    keep_ref, got_ref, outs = refs[0], refs[1], refs[-pieces:]
    quarter = outs[0].shape[0]
    for i, ref in enumerate(outs):
        rows = slice(i * quarter, (i + 1) * quarter)
        ref[...] = (keep_ref[rows] + got_ref[rows].astype(F32)).astype(ref.dtype)


def add_rows_kernel(keep_ref, got_ref, *refs):
    refs[-1][...] = (keep_ref[1].astype(F32) + got_ref[1].astype(F32)).astype(BF16)


def split_kernel(count, *refs):
    total = refs[0][...].astype(F32)
    for other in refs[1:count]:
        total = total + other[...].astype(F32)
    keep_ref, send_ref = refs[-2:]
    quarter = keep_ref.shape[0]
    odd = odd_z()
    keep_ref[...] = jnp.where(odd, total[quarter:], total[:quarter])
    send_ref[...] = jnp.where(odd, total[:quarter], total[quarter:]).astype(BF16)


def sum_kernel(count, *refs):
    total = refs[0][...].astype(F32)
    for other in refs[1:count]:
        total = total + other[...].astype(F32)
    refs[-1][...] = total.astype(refs[-1].dtype)


def add(name, parts, after=()):
    return call(
        name,
        functools.partial(sum_kernel, len(parts)),
        jax.ShapeDtypeStruct(parts[0].shape, BF16),
        parts,
        after,
    )


def tiles_kernel(keep_ref, got_ref, last_ref, tiles_ref, cols_ref, count_ref, cot_ref, *refs):
    low_ref, high_ref, own_ref, sums = refs[-4:]
    grad_agg = (
        keep_ref[0].astype(F32) + got_ref[0].astype(F32) + last_ref[...].astype(F32)
    ).astype(BF16)
    sums[0] = jnp.zeros_like(sums[0])
    sums[1] = cot_ref[...].astype(F32)
    sums[2] = jnp.zeros_like(sums[2])
    for slot in range(tiles_ref.shape[1]):

        @pl.when(slot < count_ref[0])
        def _():
            target = cols_ref[0, slot]
            sums[target] += product(tiles_ref[0, slot], grad_agg, 0, 0)

    low_ref[...] = sums[0].astype(BF16)
    high_ref[...] = sums[2].astype(BF16)
    own_ref[...] = sums[1]


def assemble_kernel(turn, factor, *refs):
    out_ref = refs[-1]
    quarter = refs[0].shape[0]
    me = lax.rem(lax.axis_index("node"), 4)
    for j in range(4):
        block = refs[j][...].astype(F32) * factor
        block = block.T if turn else block
        for device in range(4):

            @pl.when(me == device)
            def _(block=block, owner=device ^ j):
                first = (owner % 2 * 2 + owner // 2) * quarter
                if turn:
                    out_ref[:, first : first + quarter] = block
                else:
                    out_ref[first : first + quarter, :] = block


def over_groups(piece):
    groups = lax.axis_size("node") // 4
    pieces = jnp.stack([piece] + [shift(piece, "node", 4 * s) for s in range(1, groups)])
    group = lax.axis_index("node") // 4
    ordered = jnp.roll(pieces[::-1], group + 1, axis=0)
    total = jnp.zeros(piece.shape, F32)
    for s in range(groups):
        total = total + ordered[s].astype(F32)
    return total.astype(BF16)


def local(aggregated, cotangent, kernel_in, kernel_out, tile_values, tile_cols, tile_count):
    rows, width = aggregated.shape
    reps = lax.axis_size("rep")
    groups = lax.axis_size("node") // 4
    factor = 1.0 / math.sqrt(rows * lax.axis_size("node") * reps)
    half = kernel_out.shape[0] // 2
    quarter = half // 2
    shards = range(2, reps, 2)
    pieces = 1 + len(shards)
    far = pieces - 1

    def shape(*dims, dtype=BF16):
        return jax.ShapeDtypeStruct(dims, dtype)

    hidden = shape(4, pieces * half, rows)
    agg_x = swap(aggregated, "rep", 1)
    cot_x = swap(cotangent, "rep", 1)
    win = lax.dynamic_slice_in_dim(kernel_in, core() * half, half, axis=1)
    wout = lax.dynamic_slice_in_dim(kernel_out, core() * half, half, axis=0)
    wins = [swap(win, "rep", s) for s in shards]
    wouts = [swap(wout, "rep", s) for s in shards]
    v = {}
    token = []

    def aggs():
        return aggregated, agg_x, v['agg_c']

    def cots():
        return cotangent, cot_x, v['cot_c']

    def after(first):
        out = (token[0],)
        return out

    def run(name, kernel, outs, args, **kw):
        got = call(name, kernel, outs, args, tuple(token), **kw)
        token[:] = [got[0] if isinstance(got, (list, tuple)) else got]
        return got

    def total(name, parts):
        got = add(name, parts, tuple(token))
        token[:] = [got]
        return got

    def place(name, mine, z_piece, turn):
        turned = v.get('turn_' + name, z_piece)
        sources = (mine, swap(mine, "node", 1), z_piece, swap(turned, "node", 1))
        return call("place_" + name, functools.partial(assemble_kernel, turn, factor),
                    shape(*((width, 2 * half) if turn else (2 * half, width)), dtype=F32), sources)

    for step in ORDER:
        if step == 'gate_agg':
            v['agg_c'] = swap(run("gate_agg", both_kernel, shape(2, rows, width), (aggregated, agg_x)), "node", 1)
        elif step == 'gate_cot':
            v['cot_c'] = swap(run("gate_cot", both_kernel, shape(2, rows, width), (cotangent, cot_x)), "node", 1)
        elif step == 'forward':
            v['act'], v['slope'] = run("forward", functools.partial(forward_kernel, pieces), [hidden] * 2, (*aggs(), win, *wins))
        elif step == 'out':
            part_out = run("out", functools.partial(out_kernel, far), [shape(half, width)] * far, (v['act'], *cots()))
            v['got_out'] = [swap(part, "rep", s) for part, s in zip(part_out, shards)]
        elif step == 'in':
            v['grad_pre'], v['keep_in'], give = run("in", functools.partial(in_kernel, pieces),
                [hidden, shape(pieces * quarter, width, dtype=F32), shape(pieces * quarter, width)],
                (v['slope'], *aggs(), *cots(), wout, *wouts))
            v['zgot_in'] = swap(give, "node", 2)
        elif step == 'middle':
            v['mine_in'], *gives = run("middle", functools.partial(middle_kernel, pieces),
                [shape(quarter, width, dtype=F32)] + [shape(quarter, width)] * far, (v['keep_in'], v['zgot_in']))
            v['ygot_in'] = [swap(give, "rep", s) for give, s in zip(gives, shards)]
        elif step == 'own':
            v['own_out'], v['keep'], send = run("own", functools.partial(own_kernel, pieces),
                [shape(half, width, dtype=F32)] + [shape(2, rows, width)] * 2,
                (v['act'], *cots(), v['grad_pre'], win, *wins))
            v['got'] = swap(send, "node", 1)
        elif step == 'split_out':
            v['mine_out'], give = run("split_out", functools.partial(split_kernel, pieces),
                [shape(quarter, width, dtype=F32), shape(quarter, width)], (v['own_out'], *v['got_out']))
            v['ygot_out'] = [swap(give, "node", 2)]
        elif step == 'other':
            v['other'] = run("other", add_rows_kernel, shape(rows, width), (v['keep'], v['got']))
            v['last'] = swap(v['other'], "rep", 1)
        elif step == 'tiles':
            low, high, v['own'] = run("tiles", tiles_kernel, [shape(rows, width)] * 2 + [shape(rows, width, dtype=F32)],
                (v['keep'], v['got'], v['last'], tile_values, tile_cols, tile_count, cotangent),
                specs=[VMEM] * 4 + [SMEM] * 2 + [VMEM], scratch=[pltpu.VMEM((3, rows, width), F32)])
            v['next'] = shift(low, "node", -1)
            v['prev'] = shift(high, "node", 1)
        elif step in ('sum_out', 'sum_in'):
            n = step[4:]
            v['t_' + n] = total("sum_" + n, (v['mine_' + n], *v['ygot_' + n]))
            if groups == 2:
                v['cgot_' + n] = swap(v['t_' + n], "node", 4)
        elif step in ('add_out', 'add_in'):
            n = step[4:]
            if groups == 2:
                v['sum_' + n] = total("add_" + n, (v['t_' + n], v['cgot_' + n]))
            else:
                v['sum_' + n] = over_groups(v['t_' + n])
            v['z_' + n] = swap(v['sum_' + n], "node", 2)
        elif step in ('turn_out', 'turn_in'):
            n = step[5:]
            v[step] = total(step, (v['z_' + n],))
        elif step in ('place_out', 'place_in'):
            n = step[6:]
            v['grad_' + n] = place(n, v['sum_' + n], v['z_' + n], n == 'in')
        elif step == 'halo':
            token += [v['next'], v['prev']]
        elif step == 'tiny':
            token += [swap(add("lift", (w[:16],)), "node", 1) for w in wouts[:1]]
        elif step == 'need_ykin':
            token += wins
        elif step == 'need_ykout':
            token += wouts
        elif step == 'need_last':
            token += [v['last']]
        elif step == 'need_zout':
            token += [v['z_out']]
        elif step == 'final':
            v['nodes'] = (v['own'] + v['next'].astype(F32) + v['prev'].astype(F32)).astype(BF16)
    return (v['nodes'], v['grad_in'], v['grad_out'])


def solution(mesh):
    return jax.shard_map(
        local,
        mesh=mesh,
        in_specs=(
            P(("node", "rep"), None),
            P(("node", "rep"), None),
            P(None, "rep"),
            P("rep", None),
            P(("node", "rep"), None, None, None),
            P(("node", "rep"), None),
            P(("node", "rep")),
        ),
        out_specs=(P(("node", "rep"), None), P(None, "rep"), P("rep", None)),
        check_vma=False,
    )
```

time: 93 us -> 62.8 us (0.68)
  between operations: 16.5 us -> 1.49 us
  Pallas kernels: 0 us -> 9.36 us
  local copies, waits for them, and re-layouts: 11.1 us -> 2.04 us
  starting transfers between devices: 28.3 us -> 21.1 us
  matrix products: 7.16 us -> 0 us
    pallas_call x0 -> x17, Pallas kernels: none -> 9.36 us  [call(): pl.pallas_call(kernel, out_shape=outs, in_specs=(specs or [VMEM] * len(ar...]
    ppermute x2, waiting for transfers between devices: 7.79 us -> 0.01 us  [shift(): lax.ppermute(block, axis, [(i, (i + step) % count) for i in range(count)])]
    ppermute x29 -> x21, waiting for transfers between devices: 20.6 us -> 27.8 us  [swap(): return lax.ppermute(block, axis, [(i, i ^ mask) for i in range(count)])]
    dot_general x6 -> x0, matrix products: 7.16 us -> none  [the longest x2 3.08 us: contract_last(): lax.dot_general(left, right, (((1,), (1,)), ((), ())), preferred_element_...]
    ppermute x29 -> x21, starting transfers between devices: 26.4 us -> 20.8 us  [swap(): return lax.ppermute(block, axis, [(i, i ^ mask) for i in range(count)])]
    unnamed x16 -> x10, local copies, waits for them, and re-layouts: 6.07 us -> 1.05 us
    slice x5 -> x1, local copies, waits for them, and re-layouts: 2.22 us -> 0.01 us  [local(): token += [swap(add('lift', (w[:16],)), 'node', 1) for w in wouts[:1]]]
    ppermute x2, starting transfers between devices: 1.89 us -> 0.23 us  [shift(): lax.ppermute(block, axis, [(i, (i + step) % count) for i in range(count)])]
  transfers between devices with their start and end apart: 31 -> 23, of which waited for: 10 -> 8; matrix products, arithmetic and copies ran while one was open for 20% -> 3% of each run, Pallas kernels for 0% -> 12%
where the time goes in v3:
time: 62.8 us; the launch traced here: 62.6 us
  waiting for transfers between devices  27.9 us (44%)
  starting transfers between devices  21.1 us (34%)
  Pallas kernels  9.36 us (15%)
  local copies, waits for them, and re-layouts  2.04 us (3%)
  between operations  1.49 us (2%)
  other arithmetic  0.81 us (1%)
    ppermute x21, waiting for transfers between devices, swap(): return lax.ppermute(block, axis, [(i, i ^ mask) for i in range(count)])  27.8 us
    ppermute x21, starting transfers between devices, swap(): return lax.ppermute(block, axis, [(i, i ^ mask) for i in range(count)])  20.8 us
    pallas_call x17, Pallas kernels, call(): pl.pallas_call(kernel, out_shape=outs, in_specs=(specs or [VMEM] * len(ar...  9.36 us
  transfers between devices with their start and end apart: 23, of which 8 were waited for; matrix products, arithmetic and copies ran while one was open for 3% of the time, Pallas kernels for 12%

profile of v3, /device:TPU:0, one launch (start us, length us, event | category | flops | bytes accessed | tf_op | source)
XLA Modules:
  0.0 62.6 jit_solution(9150369473064210964)
XLA Ops:
  0.7 1.0 %copy-done = bf16[512,512]{1,0:T(8,128)(2,1)S(1)} copy-done((bf16[512,512]{1,0:T(8,128)(2,1)S(1)}, bf16[512,512]{1,0:T(8,128)(2,1)}, u32[]{:S(2)}) %copy-start) | copy-done | bytes 524312
  1.7 3.0 %collective-permute-start.2 = (bf16[512,256]{1,0:T(8,128)(2,1)S(1)}, bf16[512,256]{1,0:T(8,128)(2,1)S(1)}, u32[]{:S(2)}, u32[]{:S(2)}) collective-permute-start(bf16[512,256]{1,0:T(8,128)(2,1)S(1)} %constant_dynamic-slice_fusion.1.refs_3_.refs_5_), channel_id=1, source_target_pairs={{0,2},{1,3},{2,0},{3,1},{4,6},{5,7},{6,4},{7,5},{8,10},{9,11},{10,... | collective-permute-start | bytes 786440 | tf_op jit(solution)/shard_map/ppermute | solution.py:37
  4.7 1.5 %collective-permute-start = (bf16[256,512]{1,0:T(8,128)(2,1)S(1)}, bf16[256,512]{1,0:T(8,128)(2,1)S(1)}, u32[]{:S(2)}, u32[]{:S(2)}) collective-permute-start(bf16[256,512]{1,0:T(8,128)(2,1)S(1)} %copy-done.1), channel_id=1, source_target_pairs={{0,1},{1,0},{2,3},{3,2},{4,5},{5,4},{6,7},{7,6},{8,9},{9,8},{10,11... | collective-permute-start | bytes 786440 | tf_op jit(solution)/shard_map/ppermute | solution.py:37
  6.2 0.5 collective-permute-start.3
  6.8 1.0 %constant_dynamic-slice_fusion.refs_7_ = bf16[256,512]{1,0:T(8,128)(2,1)S(1)} fusion(bf16[512,512]{1,0:T(8,128)(2,1)} %param.10, s32[]{:T(128)S(6)} %select_n.4), kind=kLoop, calls=%fused_computation.1 | loop fusion | bytes 524292 | tf_op jit(solution)/shard_map/dynamic_slice | solution.py:247
  7.7 0.9 %collective-permute-start.5 = (bf16[256,512]{1,0:T(8,128)(2,1)S(1)}, bf16[256,512]{1,0:T(8,128)(2,1)S(1)}, u32[]{:S(2)}, u32[]{:S(2)}) collective-permute-start(bf16[256,512]{1,0:T(8,128)(2,1)S(1)} %constant_dynamic-slice_fusion.refs_7_), channel_id=1, source_target_pairs={{0,2},{1,3},{2,0},{3,1},{4,6},{5,7},{6,4},{7,5},{8,10},{9,11},{10,... | collective-permute-start | bytes 786440 | tf_op jit(solution)/shard_map/ppermute | solution.py:37
  9.3 4.7 %collective-permute-done.far_ref.refs_1_.refs_2_ = bf16[256,512]{1,0:T(8,128)(2,1)S(1)} collective-permute-done((bf16[256,512]{1,0:T(8,128)(2,1)S(1)}, bf16[256,512]{1,0:T(8,128)(2,1)S(1)}, u32[]{:S(2)}, u32[]{:S(2)}) %collective-permute-start) | collective-permute-done | bytes 262176 | tf_op jit(solution)/shard_map/ppermute | solution.py:37
  14.1 4.0 %collective-permute-done.3.far_ref.refs_2_.refs_5_ = bf16[256,512]{1,0:T(8,128)(2,1)S(1)} collective-permute-done((bf16[256,512]{1,0:T(8,128)(2,1)S(1)}, bf16[256,512]{1,0:T(8,128)(2,1)S(1)}, u32[]{:S(2)}, u32[]{:S(2)}) %collective-permute-start.3) | collective-permute-done | bytes 262176 | tf_op jit(solution)/shard_map/ppermute | solution.py:37
  18.3 0.5 collective-permute-start.6
  18.8 1.4 %forward.1 = (bf16[4,512,256]{2,1,0:T(8,128)(2,1)S(1)}, bf16[4,512,256]{2,1,0:T(8,128)(2,1)S(1)}) custom-call(bf16[256,512]{1,0:T(8,128)(2,1)S(1)} %copy-done.1, bf16[256,512]{1,0:T(8,128)(2,1)S(1)} %collective-permute-done.far_ref.refs_1_.refs_2_, bf16[2,256,512]{2,1,0:T(8,128)(2,1)S(1)} %collective-permute-done.1.refs_2_.refs_3_, ...), custom_call_target="tpu_custom_call" | custom-call | flops 1000000000 | tf_op jit(solution)/shard_map/forward/pallas_call | solution.py:47
  20.7 1.2 %collective-permute-start.9 = (bf16[256,512]{1,0:T(8,128)(2,1)S(1)}, bf16[256,512]{1,0:T(8,128)(2,1)S(1)}, u32[]{:S(2)}, u32[]{:S(2)}) collective-permute-start(bf16[256,512]{1,0:T(8,128)(2,1)S(1)} %out.1.refs_9_), channel_id=1, source_target_pairs={{0,2},{1,3},{2,0},{3,1},{4,6},{5,7},{6,4},{7,5},{8,10},{9,11},{10,... | collective-permute-start | bytes 786440 | tf_op jit(solution)/shard_map/ppermute | solution.py:37
  21.9 1.5 %in.1 = (bf16[4,512,256]{2,1,0:T(8,128)(2,1)S(1)}, f32[256,512]{1,0:T(8,128)S(1)}, bf16[256,512]{1,0:T(8,128)(2,1)S(1)}) custom-call(bf16[4,512,256]{2,1,0:T(8,128)(2,1)S(1)} %get-tuple-element.19.refs_0_, bf16[256,512]{1,0:T(8,128)(2,1)S(1)} %copy-done.1, bf16[256,512]{1,0:T(8,128)(2,1)S(1)} %collective-permute-done.far_ref.refs_1_.refs_2_, ...), custom_call_target="tpu_custom_call" | custom-call | flops 100000000 | tf_op jit(solution)/shard_map/in/pallas_call | solution.py:47
  23.5 1.7 %collective-permute-start.8 = (bf16[256,512]{1,0:T(8,128)(2,1)S(1)}, bf16[256,512]{1,0:T(8,128)(2,1)S(1)}, u32[]{:S(2)}, u32[]{:S(2)}) collective-permute-start(bf16[256,512]{1,0:T(8,128)(2,1)S(1)} %get-tuple-element.24), channel_id=1, source_target_pairs={{0,8},{4,12},{8,0},{12,4},{16,24},{20,28},{24,16},{28,20},{1,9},{5... | collective-permute-start | bytes 786440 | tf_op jit(solution)/shard_map/ppermute | solution.py:37
  25.1 1.0 %own.1 = (f32[256,512]{1,0:T(8,128)S(1)}, bf16[2,256,512]{2,1,0:T(8,128)(2,1)S(1)}, bf16[2,256,512]{2,1,0:T(8,128)(2,1)S(1)}) custom-call(bf16[4,512,256]{2,1,0:T(8,128)(2,1)S(1)} %get-tuple-element.18.refs_0_.refs_4_, bf16[256,512]{1,0:T(8,128)(2,1)S(1)} %copy-done.2, bf16[256,512]{1,0:T(8,128)(2,1)S(1)} %collective-permute-done.3.far_ref.refs_2_.refs_5_, ...), custom_call_target="tpu_custom_call" | custom-call | flops 3000000000 | tf_op jit(solution)/shard_map/own/pallas_call | solution.py:47
  26.2 2.8 %collective-permute-done.9.refs_1_ = bf16[256,512]{1,0:T(8,128)(2,1)S(1)} collective-permute-done((bf16[256,512]{1,0:T(8,128)(2,1)S(1)}, bf16[256,512]{1,0:T(8,128)(2,1)S(1)}, u32[]{:S(2)}, u32[]{:S(2)}) %collective-permute-start.9) | collective-permute-done | bytes 262176 | tf_op jit(solution)/shard_map/ppermute | solution.py:37
  29.1 1.6 %collective-permute-start.11 = (bf16[128,512]{1,0:T(8,128)(2,1)S(1)}, bf16[128,512]{1,0:T(8,128)(2,1)S(1)}, u32[]{:S(2)}, u32[]{:S(2)}) collective-permute-start(bf16[128,512]{1,0:T(8,128)(2,1)S(1)} %get-tuple-element.28), channel_id=1, source_target_pairs={{0,8},{4,12},{8,0},{12,4},{16,24},{20,28},{24,16},{28,20},{1,9},{5... | collective-permute-start | bytes 393224 | tf_op jit(solution)/shard_map/ppermute | solution.py:37
  30.8 1.2 %collective-permute-done.8.refs_1_ = bf16[256,512]{1,0:T(8,128)(2,1)S(1)} collective-permute-done((bf16[256,512]{1,0:T(8,128)(2,1)S(1)}, bf16[256,512]{1,0:T(8,128)(2,1)S(1)}, u32[]{:S(2)}, u32[]{:S(2)}) %collective-permute-start.8) | collective-permute-done | bytes 262176 | tf_op jit(solution)/shard_map/ppermute | solution.py:37
  32.1 0.7 %collective-permute-start.14 = (bf16[128,512]{1,0:T(8,128)(2,1)S(1)}, bf16[128,512]{1,0:T(8,128)(2,1)S(1)}, u32[]{:S(2)}, u32[]{:S(2)}) collective-permute-start(bf16[128,512]{1,0:T(8,128)(2,1)S(1)} %get-tuple-element.32), channel_id=1, source_target_pairs={{0,2},{1,3},{2,0},{3,1},{4,6},{5,7},{6,4},{7,5},{8,10},{9,11},{10,... | collective-permute-start | bytes 393224 | tf_op jit(solution)/shard_map/ppermute | solution.py:37
  32.8 1.6 %collective-permute-start.10 = (bf16[256,512]{1,0:T(8,128)(2,1)S(1)}, bf16[256,512]{1,0:T(8,128)(2,1)S(1)}, u32[]{:S(2)}, u32[]{:S(2)}) collective-permute-start(bf16[256,512]{1,0:T(8,128)(2,1)S(1)} %other.1.refs_2_), channel_id=1, source_target_pairs={{0,1},{1,0},{2,3},{3,2},{4,5},{5,4},{6,7},{7,6},{8,9},{9,8},{10,11... | collective-permute-start | bytes 786440 | tf_op jit(solution)/shard_map/ppermute | solution.py:37
  34.5 2.6 %collective-permute-start.16 = (bf16[128,512]{1,0:T(8,128)(2,1)S(1)}, bf16[128,512]{1,0:T(8,128)(2,1)S(1)}, u32[]{:S(2)}, u32[]{:S(2)}) collective-permute-start(bf16[128,512]{1,0:T(8,128)(2,1)S(1)} %sum_out.1.refs_0_), channel_id=1, source_target_pairs={{0,16},{4,20},{8,24},{12,28},{16,0},{20,4},{24,8},{28,12},{1,17},{... | collective-permute-start | bytes 393224 | tf_op jit(solution)/shard_map/ppermute | solution.py:37
  37.1 2.4 %collective-permute-done.10.last_ref = bf16[256,512]{1,0:T(8,128)(2,1)S(1)} collective-permute-done((bf16[256,512]{1,0:T(8,128)(2,1)S(1)}, bf16[256,512]{1,0:T(8,128)(2,1)S(1)}, u32[]{:S(2)}, u32[]{:S(2)}) %collective-permute-start.10) | collective-permute-done | bytes 262176 | tf_op jit(solution)/shard_map/ppermute | solution.py:37
  39.5 1.9 %tiles.1 = (bf16[256,512]{1,0:T(8,128)(2,1)S(1)}, bf16[256,512]{1,0:T(8,128)(2,1)S(1)}, f32[256,512]{1,0:T(8,128)S(1)}) custom-call(bf16[2,256,512]{2,1,0:T(8,128)(2,1)S(1)} %get-tuple-element.21.keep_ref, bf16[2,256,512]{2,1,0:T(8,128)(2,1)S(1)} %collective-permute-done.7.got_ref, bf16[256,512]{1,0:T(8,128)(2,1)S(1)} %collective-permute-done.10.last_ref, ...), custom_call_target="tpu_custom_call" | custom-call | flops 100000000 | tf_op jit(solution)/shard_map/tiles/pallas_call | solution.py:47
  41.4 2.7 %collective-permute-start.15 = (bf16[128,512]{1,0:T(8,128)(2,1)S(1)}, bf16[128,512]{1,0:T(8,128)(2,1)S(1)}, u32[]{:S(2)}, u32[]{:S(2)}) collective-permute-start(bf16[128,512]{1,0:T(8,128)(2,1)S(1)} %sum_in.1.refs_2_.refs_0_), channel_id=1, source_target_pairs={{0,16},{4,20},{8,24},{12,28},{16,0},{20,4},{24,8},{28,12},{1,17},{... | collective-permute-start | bytes 393224 | tf_op jit(solution)/shard_map/ppermute | solution.py:37
  44.1 0.9 %collective-permute-start.21 = (bf16[128,512]{1,0:T(8,128)(2,1)S(1)}, bf16[128,512]{1,0:T(8,128)(2,1)S(1)}, u32[]{:S(2)}, u32[]{:S(2)}) collective-permute-start(bf16[128,512]{1,0:T(8,128)(2,1)S(1)} %add_out.1.refs_2_.refs_0_), channel_id=1, source_target_pairs={{0,8},{4,12},{8,0},{12,4},{16,24},{20,28},{24,16},{28,20},{1,9},{5... | collective-permute-start | bytes 393224 | tf_op jit(solution)/shard_map/ppermute | solution.py:37
  45.3 3.5 %collective-permute-done.15.refs_1_ = bf16[128,512]{1,0:T(8,128)(2,1)S(1)} collective-permute-done((bf16[128,512]{1,0:T(8,128)(2,1)S(1)}, bf16[128,512]{1,0:T(8,128)(2,1)S(1)}, u32[]{:S(2)}, u32[]{:S(2)}) %collective-permute-start.15) | collective-permute-done | bytes 131104 | tf_op jit(solution)/shard_map/ppermute | solution.py:37
  48.8 0.6 collective-permute-start.18
  49.4 7.8 %collective-permute-done.21.refs_2_ = bf16[128,512]{1,0:T(8,128)(2,1)S(1)} collective-permute-done((bf16[128,512]{1,0:T(8,128)(2,1)S(1)}, bf16[128,512]{1,0:T(8,128)(2,1)S(1)}, u32[]{:S(2)}, u32[]{:S(2)}) %collective-permute-start.21) | collective-permute-done | bytes 131104 | tf_op jit(solution)/shard_map/ppermute | solution.py:37
  57.2 1.4 %collective-permute-done.18.refs_2_ = bf16[128,512]{1,0:T(8,128)(2,1)S(1)} collective-permute-done((bf16[128,512]{1,0:T(8,128)(2,1)S(1)}, bf16[128,512]{1,0:T(8,128)(2,1)S(1)}, u32[]{:S(2)}, u32[]{:S(2)}) %collective-permute-start.18) | collective-permute-done | bytes 131104 | tf_op jit(solution)/shard_map/ppermute | solution.py:37
  58.6 0.5 collective-permute-start.19
  59.1 0.8 %add_convert_fusion = bf16[256,512]{1,0:T(8,128)(2,1)} fusion(bf16[256,512]{1,0:T(8,128)(2,1)S(1)} %collective-permute-done.13, f32[256,512]{1,0:T(8,128)S(1)} %get-tuple-element.29, bf16[256,512]{1,0:T(8,128)(2,1)S(1)} %collective-permute-done.12), kind=kLoop, calls=%fused_computation | loop fusion | flops 655360 | bytes 1310720 | tf_op jit(solution)/shard_map/convert_element_type | solution.py:347
  59.9 1.1 %place_out.1 = f32[512,512]{1,0:T(8,128)} custom-call(bf16[128,512]{1,0:T(8,128)(2,1)S(1)} %add_out.1.refs_2_.refs_0_, bf16[128,512]{1,0:T(8,128)(2,1)S(1)} %collective-permute-done.20.refs_1_, bf16[128,512]{1,0:T(8,128)(2,1)S(1)} %collective-permute-done.21.refs_2_, bf16[128,512]{1,0:T(8,128)(2,1)S(1)} %collective-permute-done.22.refs_3_), custom_call_target="tpu_custom_call" | custom-call | flops 100000000 | tf_op jit(solution)/shard_map/place_out/pallas_call | solution.py:47
  61.1 1.5 %place_in.1 = f32[512,512]{1,0:T(8,128)} custom-call(bf16[128,512]{1,0:T(8,128)(2,1)S(1)} %add_in.1.refs_0_, bf16[128,512]{1,0:T(8,128)(2,1)S(1)} %collective-permute-done.17.refs_1_, bf16[128,512]{1,0:T(8,128)(2,1)S(1)} %collective-permute-done.18.refs_2_, bf16[128,512]{1,0:T(8,128)(2,1)S(1)} %collective-permute-done.19.refs_3_), custom_call_target="tpu_custom_call" | custom-call | flops 1000000000 | tf_op jit(solution)/shard_map/place_in/pallas_call | solution.py:47
  (45 shorter events, 1.4 us)
Async XLA Ops:
  0.6 1.0 %copy-start = (bf16[512,512]{1,0:T(8,128)(2,1)S(1)}, bf16[512,512]{1,0:T(8,128)(2,1)}, u32[]{:S(2)}) copy-start(bf16[512,512]{1,0:T(8,128)(2,1)} %param.9) | copy-start | bytes 1572868
  1.7 3.1 %copy-start.1 = (bf16[256,512]{1,0:T(8,128)(2,1)S(1)}, bf16[256,512]{1,0:T(8,128)(2,1)}, u32[]{:S(2)}) copy-start(bf16[256,512]{1,0:T(8,128)(2,1)} %refs_1_.4) | copy-start | bytes 786436
  1.7 4.6 %copy-start.2 = (bf16[256,512]{1,0:T(8,128)(2,1)S(1)}, bf16[256,512]{1,0:T(8,128)(2,1)}, u32[]{:S(2)}) copy-start(bf16[256,512]{1,0:T(8,128)(2,1)} %cot_ref.1) | copy-start | bytes 786436
  1.7 12.4 %collective-permute-start.2 = (bf16[512,256]{1,0:T(8,128)(2,1)S(1)}, bf16[512,256]{1,0:T(8,128)(2,1)S(1)}, u32[]{:S(2)}, u32[]{:S(2)}) collective-permute-start(bf16[512,256]{1,0:T(8,128)(2,1)S(1)} %constant_dynamic-slice_fusion.1.refs_3_.refs_5_), channel_id=1, source_target_pairs={{0,2},{1,3},{2,0},{3,1},{4,6},{5,7},{6,4},{7,5},{8,10},{9,11},{10,... | collective-permute-start | bytes 786440 | tf_op jit(solution)/shard_map/ppermute | solution.py:37
  4.7 9.2 %collective-permute-start = (bf16[256,512]{1,0:T(8,128)(2,1)S(1)}, bf16[256,512]{1,0:T(8,128)(2,1)S(1)}, u32[]{:S(2)}, u32[]{:S(2)}) collective-permute-start(bf16[256,512]{1,0:T(8,128)(2,1)S(1)} %copy-done.1), channel_id=1, source_target_pairs={{0,1},{1,0},{2,3},{3,2},{4,5},{5,4},{6,7},{7,6},{8,9},{9,8},{10,11... | collective-permute-start | bytes 786440 | tf_op jit(solution)/shard_map/ppermute | solution.py:37
  6.2 11.9 %collective-permute-start.3 = (bf16[256,512]{1,0:T(8,128)(2,1)S(1)}, bf16[256,512]{1,0:T(8,128)(2,1)S(1)}, u32[]{:S(2)}, u32[]{:S(2)}) collective-permute-start(bf16[256,512]{1,0:T(8,128)(2,1)S(1)} %copy-done.2), channel_id=1, source_target_pairs={{0,1},{1,0},{2,3},{3,2},{4,5},{5,4},{6,7},{7,6},{8,9},{9,8},{10,11... | collective-permute-start | bytes 786440 | tf_op jit(solution)/shard_map/ppermute | solution.py:37
  7.7 10.5 %collective-permute-start.5 = (bf16[256,512]{1,0:T(8,128)(2,1)S(1)}, bf16[256,512]{1,0:T(8,128)(2,1)S(1)}, u32[]{:S(2)}, u32[]{:S(2)}) collective-permute-start(bf16[256,512]{1,0:T(8,128)(2,1)S(1)} %constant_dynamic-slice_fusion.refs_7_), channel_id=1, source_target_pairs={{0,2},{1,3},{2,0},{3,1},{4,6},{5,7},{6,4},{7,5},{8,10},{9,11},{10,... | collective-permute-start | bytes 786440 | tf_op jit(solution)/shard_map/ppermute | solution.py:37
  14.0 4.8 %collective-permute-start.1 = (bf16[2,256,512]{2,1,0:T(8,128)(2,1)S(1)}, bf16[2,256,512]{2,1,0:T(8,128)(2,1)S(1)}, u32[]{:S(2)}, u32[]{:S(2)}) collective-permute-start(bf16[2,256,512]{2,1,0:T(8,128)(2,1)S(1)} %gate_agg.1.refs_0_), channel_id=1, source_target_pairs={{0,4},{4,0},{8,12},{12,8},{16,20},{20,16},{24,28},{28,24},{1,5},{5... | collective-permute-start | bytes 1572872 | tf_op jit(solution)/shard_map/ppermute | solution.py:37
  18.2 2.1 %collective-permute-start.4 = (bf16[2,256,512]{2,1,0:T(8,128)(2,1)S(1)}, bf16[2,256,512]{2,1,0:T(8,128)(2,1)S(1)}, u32[]{:S(2)}, u32[]{:S(2)}) collective-permute-start(bf16[2,256,512]{2,1,0:T(8,128)(2,1)S(1)} %gate_cot.1.refs_5_), channel_id=1, source_target_pairs={{0,4},{4,0},{8,12},{12,8},{16,20},{20,16},{24,28},{28,24},{1,5},{5... | collective-permute-start | bytes 1572872 | tf_op jit(solution)/shard_map/ppermute | solution.py:37
  18.3 2.0 %collective-permute-start.6 = (bf16[16,512]{1,0:T(8,128)(2,1)S(1)}, bf16[16,512]{1,0:T(8,128)(2,1)S(1)}, u32[]{:S(2)}, u32[]{:S(2)}) collective-permute-start(bf16[16,512]{1,0:T(8,128)(2,1)S(1)} %lift.1), channel_id=1, source_target_pairs={{0,4},{4,0},{8,12},{12,8},{16,20},{20,16},{24,28},{28,24},{1,5},{5... | collective-permute-start | bytes 49160 | tf_op jit(solution)/shard_map/ppermute | solution.py:37
  20.7 8.3 %collective-permute-start.9 = (bf16[256,512]{1,0:T(8,128)(2,1)S(1)}, bf16[256,512]{1,0:T(8,128)(2,1)S(1)}, u32[]{:S(2)}, u32[]{:S(2)}) collective-permute-start(bf16[256,512]{1,0:T(8,128)(2,1)S(1)} %out.1.refs_9_), channel_id=1, source_target_pairs={{0,2},{1,3},{2,0},{3,1},{4,6},{5,7},{6,4},{7,5},{8,10},{9,11},{10,... | collective-permute-start | bytes 786440 | tf_op jit(solution)/shard_map/ppermute | solution.py:37
  23.5 8.5 %collective-permute-start.8 = (bf16[256,512]{1,0:T(8,128)(2,1)S(1)}, bf16[256,512]{1,0:T(8,128)(2,1)S(1)}, u32[]{:S(2)}, u32[]{:S(2)}) collective-permute-start(bf16[256,512]{1,0:T(8,128)(2,1)S(1)} %get-tuple-element.24), channel_id=1, source_target_pairs={{0,8},{4,12},{8,0},{12,4},{16,24},{20,28},{24,16},{28,20},{1,9},{5... | collective-permute-start | bytes 786440 | tf_op jit(solution)/shard_map/ppermute | solution.py:37
  26.1 6.6 %collective-permute-start.7 = (bf16[2,256,512]{2,1,0:T(8,128)(2,1)S(1)}, bf16[2,256,512]{2,1,0:T(8,128)(2,1)S(1)}, u32[]{:S(2)}, u32[]{:S(2)}) collective-permute-start(bf16[2,256,512]{2,1,0:T(8,128)(2,1)S(1)} %get-tuple-element.22), channel_id=1, source_target_pairs={{0,4},{4,0},{8,12},{12,8},{16,20},{20,16},{24,28},{28,24},{1,5},{5... | collective-permute-start | bytes 1572872 | tf_op jit(solution)/shard_map/ppermute | solution.py:37
  29.1 5.3 %collective-permute-start.11 = (bf16[128,512]{1,0:T(8,128)(2,1)S(1)}, bf16[128,512]{1,0:T(8,128)(2,1)S(1)}, u32[]{:S(2)}, u32[]{:S(2)}) collective-permute-start(bf16[128,512]{1,0:T(8,128)(2,1)S(1)} %get-tuple-element.28), channel_id=1, source_target_pairs={{0,8},{4,12},{8,0},{12,4},{16,24},{20,28},{24,16},{28,20},{1,9},{5... | collective-permute-start | bytes 393224 | tf_op jit(solution)/shard_map/ppermute | solution.py:37
  32.1 9.3 %collective-permute-start.14 = (bf16[128,512]{1,0:T(8,128)(2,1)S(1)}, bf16[128,512]{1,0:T(8,128)(2,1)S(1)}, u32[]{:S(2)}, u32[]{:S(2)}) collective-permute-start(bf16[128,512]{1,0:T(8,128)(2,1)S(1)} %get-tuple-element.32), channel_id=1, source_target_pairs={{0,2},{1,3},{2,0},{3,1},{4,6},{5,7},{6,4},{7,5},{8,10},{9,11},{10,... | collective-permute-start | bytes 393224 | tf_op jit(solution)/shard_map/ppermute | solution.py:37
  32.8 6.7 %copy-start.3 = (bf16[1,4,256,256]{3,2,1,0:T(8,128)(2,1)S(1)}, bf16[1,4,256,256]{3,2,1,0:T(8,128)(2,1)}, u32[]{:S(2)}) copy-start(bf16[1,4,256,256]{3,2,1,0:T(8,128)(2,1)} %tiles_ref.1) | copy-start | bytes 1572868
  32.8 6.6 %copy-start.4 = (s32[1,4]{1,0:T(1,128)S(1)}, s32[1,4]{1,0:T(1,128)}, u32[]{:S(2)}) copy-start(s32[1,4]{1,0:T(1,128)} %cols_ref.1) | copy-start | bytes 52
  32.8 6.6 %collective-permute-start.10 = (bf16[256,512]{1,0:T(8,128)(2,1)S(1)}, bf16[256,512]{1,0:T(8,128)(2,1)S(1)}, u32[]{:S(2)}, u32[]{:S(2)}) collective-permute-start(bf16[256,512]{1,0:T(8,128)(2,1)S(1)} %other.1.refs_2_), channel_id=1, source_target_pairs={{0,1},{1,0},{2,3},{3,2},{4,5},{5,4},{6,7},{7,6},{8,9},{9,8},{10,11... | collective-permute-start | bytes 786440 | tf_op jit(solution)/shard_map/ppermute | solution.py:37
  34.5 9.6 %collective-permute-start.16 = (bf16[128,512]{1,0:T(8,128)(2,1)S(1)}, bf16[128,512]{1,0:T(8,128)(2,1)S(1)}, u32[]{:S(2)}, u32[]{:S(2)}) collective-permute-start(bf16[128,512]{1,0:T(8,128)(2,1)S(1)} %sum_out.1.refs_0_), channel_id=1, source_target_pairs={{0,16},{4,20},{8,24},{12,28},{16,0},{20,4},{24,8},{28,12},{1,17},{... | collective-permute-start | bytes 393224 | tf_op jit(solution)/shard_map/ppermute | solution.py:37
  41.4 7.3 %collective-permute-start.15 = (bf16[128,512]{1,0:T(8,128)(2,1)S(1)}, bf16[128,512]{1,0:T(8,128)(2,1)S(1)}, u32[]{:S(2)}, u32[]{:S(2)}) collective-permute-start(bf16[128,512]{1,0:T(8,128)(2,1)S(1)} %sum_in.1.refs_2_.refs_0_), channel_id=1, source_target_pairs={{0,16},{4,20},{8,24},{12,28},{16,0},{20,4},{24,8},{28,12},{1,17},{... | collective-permute-start | bytes 393224 | tf_op jit(solution)/shard_map/ppermute | solution.py:37
  44.1 14.5 %collective-permute-start.12 = (bf16[256,512]{1,0:T(8,128)(2,1)S(1)}, bf16[256,512]{1,0:T(8,128)(2,1)S(1)}, u32[]{:S(2)}, u32[]{:S(2)}) collective-permute-start(bf16[256,512]{1,0:T(8,128)(2,1)S(1)} %get-tuple-element.30.refs_2_), channel_id=1, source_target_pairs={{0,28},{4,0},{8,4},{12,8},{16,12},{20,16},{24,20},{28,24},{1,29},{... | collective-permute-start | bytes 786440 | tf_op jit(solution)/shard_map/ppermute | solution.py:42
  44.1 13.1 %collective-permute-start.21 = (bf16[128,512]{1,0:T(8,128)(2,1)S(1)}, bf16[128,512]{1,0:T(8,128)(2,1)S(1)}, u32[]{:S(2)}, u32[]{:S(2)}) collective-permute-start(bf16[128,512]{1,0:T(8,128)(2,1)S(1)} %add_out.1.refs_2_.refs_0_), channel_id=1, source_target_pairs={{0,8},{4,12},{8,0},{12,4},{16,24},{20,28},{24,16},{28,20},{1,9},{5... | collective-permute-start | bytes 393224 | tf_op jit(solution)/shard_map/ppermute | solution.py:37
  45.0 14.1 %collective-permute-start.13 = (bf16[256,512]{1,0:T(8,128)(2,1)S(1)}, bf16[256,512]{1,0:T(8,128)(2,1)S(1)}, u32[]{:S(2)}, u32[]{:S(2)}) collective-permute-start(bf16[256,512]{1,0:T(8,128)(2,1)S(1)} %get-tuple-element.31), channel_id=1, source_target_pairs={{0,4},{4,8},{8,12},{12,16},{16,20},{20,24},{24,28},{28,0},{1,5},{5... | collective-permute-start | bytes 786440 | tf_op jit(solution)/shard_map/ppermute | solution.py:42
  48.8 9.8 %collective-permute-start.18 = (bf16[128,512]{1,0:T(8,128)(2,1)S(1)}, bf16[128,512]{1,0:T(8,128)(2,1)S(1)}, u32[]{:S(2)}, u32[]{:S(2)}) collective-permute-start(bf16[128,512]{1,0:T(8,128)(2,1)S(1)} %add_in.1.refs_0_), channel_id=1, source_target_pairs={{0,8},{4,12},{8,0},{12,4},{16,24},{20,28},{24,16},{28,20},{1,9},{5... | collective-permute-start | bytes 393224 | tf_op jit(solution)/shard_map/ppermute | solution.py:37
  49.4 10.5 %collective-permute-start.20 = (bf16[128,512]{1,0:T(8,128)(2,1)S(1)}, bf16[128,512]{1,0:T(8,128)(2,1)S(1)}, u32[]{:S(2)}, u32[]{:S(2)}) collective-permute-start(bf16[128,512]{1,0:T(8,128)(2,1)S(1)} %add_out.1.refs_2_.refs_0_), channel_id=1, source_target_pairs={{0,4},{4,0},{8,12},{12,8},{16,20},{20,16},{24,28},{28,24},{1,5},{5... | collective-permute-start | bytes 393224 | tf_op jit(solution)/shard_map/ppermute | solution.py:37
  57.2 3.9 %collective-permute-start.17 = (bf16[128,512]{1,0:T(8,128)(2,1)S(1)}, bf16[128,512]{1,0:T(8,128)(2,1)S(1)}, u32[]{:S(2)}, u32[]{:S(2)}) collective-permute-start(bf16[128,512]{1,0:T(8,128)(2,1)S(1)} %add_in.1.refs_0_), channel_id=1, source_target_pairs={{0,4},{4,0},{8,12},{12,8},{16,20},{20,16},{24,28},{28,24},{1,5},{5... | collective-permute-start | bytes 393224 | tf_op jit(solution)/shard_map/ppermute | solution.py:37
  58.6 1.3 %collective-permute-start.22 = (bf16[128,512]{1,0:T(8,128)(2,1)S(1)}, bf16[128,512]{1,0:T(8,128)(2,1)S(1)}, u32[]{:S(2)}, u32[]{:S(2)}) collective-permute-start(bf16[128,512]{1,0:T(8,128)(2,1)S(1)} %collective-permute-done.21.refs_2_), channel_id=1, source_target_pairs={{0,4},{4,0},{8,12},{12,8},{16,20},{20,16},{24,28},{28,24},{1,5},{5... | collective-permute-start | bytes 393224 | tf_op jit(solution)/shard_map/ppermute | solution.py:37
  58.6 2.5 %collective-permute-start.19 = (bf16[128,512]{1,0:T(8,128)(2,1)S(1)}, bf16[128,512]{1,0:T(8,128)(2,1)S(1)}, u32[]{:S(2)}, u32[]{:S(2)}) collective-permute-start(bf16[128,512]{1,0:T(8,128)(2,1)S(1)} %collective-permute-done.18.refs_2_), channel_id=1, source_target_pairs={{0,4},{4,0},{8,12},{12,8},{16,20},{20,16},{24,28},{28,24},{1,5},{5... | collective-permute-start | bytes 393224 | tf_op jit(solution)/shard_map/ppermute | solution.py:37

commit v4 on v3

--- a/solution.py
+++ b/solution.py
@@ -12,8 +12,8 @@
 F32 = jnp.float32
 VMEM = pl.BlockSpec(memory_space=pltpu.VMEM)
 SMEM = pl.BlockSpec(memory_space=pltpu.SMEM)
-COST = {'in': 0.1, 'place_out': 0.1, 'out': 8, 'middle': 8, 'sum_out': 25, 'add_out': 1, 'add_in': 3, 'forward': 1, 'sum_in': 25, 'place_in': 1, 'tiles': 0.1, 'other': 0.1, 'gate_cot': 1, 'lift': 9, 'own': 3, 'split_out': 25}
-ORDER = ['gate_agg', 'need_ykin', 'gate_cot', 'forward', 'tiny', 'out', 'in', 'own', 'split_out', 'middle', 'other', 'sum_out', 'tiles', 'sum_in', 'final', 'add_out', 'place_out', 'add_in', 'place_in']
+COST = {'in': 0.1, 'place_out': 0.1, 'out': 8, 'middle': 8, 'sum_out': 25, 'add_out': 1, 'add_in': 3, 'forward': 1, 'sum_in': 25, 'place_in': 1, 'tiles': 0.1, 'other': 0.1, 'gate_cot': 8, 'lift': 9, 'own': 3, 'split_out': 25}
+ORDER = ['gate_agg', 'need_ykin', 'gate_cot', 'turn', 'forward', 'tiny', 'out', 'in', 'own', 'split_out', 'middle', 'other', 'sum_out', 'tiles', 'sum_in', 'add_out', 'add_in']
 ANY = pl.BlockSpec(memory_space=pl.ANY)
 
 
@@ -177,6 +177,11 @@
     )
 
 
+def turn_kernel(tiles_ref, *refs):
+    for slot in range(tiles_ref.shape[1]):
+        refs[-1][slot] = tiles_ref[0, slot].T
+
+
 def tiles_kernel(keep_ref, got_ref, last_ref, tiles_ref, cols_ref, count_ref, cot_ref, *refs):
     low_ref, high_ref, own_ref, sums = refs[-4:]
     grad_agg = (
@@ -185,34 +190,36 @@
     sums[0] = jnp.zeros_like(sums[0])
     sums[1] = cot_ref[...].astype(F32)
     sums[2] = jnp.zeros_like(sums[2])
-    for slot in range(tiles_ref.shape[1]):
+    for slot in range(tiles_ref.shape[0]):
 
         @pl.when(slot < count_ref[0])
         def _():
             target = cols_ref[0, slot]
-            sums[target] += product(tiles_ref[0, slot], grad_agg, 0, 0)
+            sums[target] += product(tiles_ref[slot], grad_agg, 1, 0)
 
     low_ref[...] = sums[0].astype(BF16)
     high_ref[...] = sums[2].astype(BF16)
     own_ref[...] = sums[1]
 
 
-def assemble_kernel(turn, factor, *refs):
-    out_ref = refs[-1]
-    quarter = refs[0].shape[0]
+def finish_kernel(factor, *refs):
+    (own_ref, next_ref, prev_ref), ins, outs = refs[:3], refs[3:7], refs[7:11]
+    nodes_ref, grad_in_ref, grad_out_ref = refs[-3:]
+    quarter = ins[0].shape[0]
     me = lax.rem(lax.axis_index("node"), 4)
+    nodes_ref[...] = (
+        own_ref[...] + next_ref[...].astype(F32) + prev_ref[...].astype(F32)
+    ).astype(BF16)
     for j in range(4):
-        block = refs[j][...].astype(F32) * factor
-        block = block.T if turn else block
+        out_block = outs[j][...].astype(F32) * factor
+        in_block = ins[j][...].astype(F32).T * factor
         for device in range(4):
 
             @pl.when(me == device)
-            def _(block=block, owner=device ^ j):
+            def _(in_block=in_block, out_block=out_block, owner=device ^ j):
                 first = (owner % 2 * 2 + owner // 2) * quarter
-                if turn:
-                    out_ref[:, first : first + quarter] = block
-                else:
-                    out_ref[first : first + quarter, :] = block
+                grad_out_ref[first : first + quarter, :] = out_block
+                grad_in_ref[:, first : first + quarter] = in_block
 
 
 def over_groups(piece):
@@ -270,14 +277,14 @@
         token[:] = [got]
         return got
 
-    def place(name, mine, z_piece, turn):
-        turned = v.get('turn_' + name, z_piece)
-        sources = (mine, swap(mine, "node", 1), z_piece, swap(turned, "node", 1))
-        return call("place_" + name, functools.partial(assemble_kernel, turn, factor),
-                    shape(*((width, 2 * half) if turn else (2 * half, width)), dtype=F32), sources)
+    def quarters(name):
+        z_piece = v['z_' + name]
+        return v['sum_' + name], swap(v['sum_' + name], "node", 1), z_piece, swap(z_piece, "node", 1)
 
     for step in ORDER:
-        if step == 'gate_agg':
+        if step == 'turn':
+            v['turned'] = run("turn", turn_kernel, shape(*tile_values.shape[1:]), (tile_values,))
+        elif step == 'gate_agg':
             v['agg_c'] = swap(run("gate_agg", both_kernel, shape(2, rows, width), (aggregated, agg_x)), "node", 1)
         elif step == 'gate_cot':
             v['cot_c'] = swap(run("gate_cot", both_kernel, shape(2, rows, width), (cotangent, cot_x)), "node", 1)
@@ -309,7 +316,7 @@
             v['last'] = swap(v['other'], "rep", 1)
         elif step == 'tiles':
             low, high, v['own'] = run("tiles", tiles_kernel, [shape(rows, width)] * 2 + [shape(rows, width, dtype=F32)],
-                (v['keep'], v['got'], v['last'], tile_values, tile_cols, tile_count, cotangent),
+                (v['keep'], v['got'], v['last'], v['turned'], tile_cols, tile_count, cotangent),
                 specs=[VMEM] * 4 + [SMEM] * 2 + [VMEM], scratch=[pltpu.VMEM((3, rows, width), F32)])
             v['next'] = shift(low, "node", -1)
             v['prev'] = shift(high, "node", 1)
@@ -328,24 +335,24 @@
         elif step in ('turn_out', 'turn_in'):
             n = step[5:]
             v[step] = total(step, (v['z_' + n],))
-        elif step in ('place_out', 'place_in'):
-            n = step[6:]
-            v['grad_' + n] = place(n, v['sum_' + n], v['z_' + n], n == 'in')
+        elif step == 'need_ykin':
+            token += wins
         elif step == 'halo':
             token += [v['next'], v['prev']]
+        elif step == 'need_zout':
+            token += [v['z_out']]
+        elif step == 'need_last':
+            token += [v['last']]
         elif step == 'tiny':
             token += [swap(add("lift", (w[:16],)), "node", 1) for w in wouts[:1]]
-        elif step == 'need_ykin':
-            token += wins
-        elif step == 'need_ykout':
-            token += wouts
-        elif step == 'need_last':
-            token += [v['last']]
-        elif step == 'need_zout':
-            token += [v['z_out']]
-        elif step == 'final':
-            v['nodes'] = (v['own'] + v['next'].astype(F32) + v['prev'].astype(F32)).astype(BF16)
-    return (v['nodes'], v['grad_in'], v['grad_out'])
+        elif step == 'tail':
+            token += [swap(add("lift2", (v['next'][:16], v['prev'][:16])), "node", 1)]
+    return call(
+        "finish", functools.partial(finish_kernel, factor),
+        [shape(rows, width), shape(width, 2 * half, dtype=F32), shape(2 * half, width, dtype=F32)],
+        (v['own'], v['next'], v['prev'], *quarters('in'), *quarters('out')),
+        tuple(token[1:]),
+    )
 
 
 def solution(mesh):

time: 62.8 us -> 60.8 us (0.968)
  waiting for transfers between devices: 27.9 us -> 24.6 us
  starting transfers between devices: 21.1 us -> 23.6 us
  other arithmetic: 0.81 us -> 0 us
    ppermute x21, waiting for transfers between devices: 27.8 us -> 22.8 us  [swap(): return lax.ppermute(block, axis, [(i, i ^ mask) for i in range(count)])]
    ppermute x2, starting transfers between devices: 0.23 us -> 3.01 us  [shift(): lax.ppermute(block, axis, [(i, (i + step) % count) for i in range(count)])]
    ppermute x2, waiting for transfers between devices: 0.01 us -> 1.84 us  [shift(): lax.ppermute(block, axis, [(i, (i + step) % count) for i in range(count)])]
    convert_element_type x1 -> x0, other arithmetic: 0.81 us -> none  [local(): (v['own'] + v['next'].astype(F32) + v['prev'].astype(F32)).astype(BF16)]
  transfers between devices with their start and end apart: 23 -> 23, of which waited for: 8 -> 11; matrix products, arithmetic and copies ran while one was open for 3% -> 2% of each run, Pallas kernels for 12% -> 10%
where the time goes in v4:
time: 60.8 us; the launch traced here: 60.6 us
  waiting for transfers between devices  24.6 us (40%)
  starting transfers between devices  23.6 us (39%)
  Pallas kernels  8.88 us (15%)
  local copies, waits for them, and re-layouts  1.98 us (3%)
  between operations  1.5 us (2%)
    ppermute x21, waiting for transfers between devices, swap(): return lax.ppermute(block, axis, [(i, i ^ mask) for i in range(count)])  22.8 us
    ppermute x21, starting transfers between devices, swap(): return lax.ppermute(block, axis, [(i, i ^ mask) for i in range(count)])  20.6 us
    pallas_call x17, Pallas kernels, call(): pl.pallas_call(kernel, out_shape=outs, in_specs=(specs or [VMEM] * len(ar...  8.88 us
    ppermute x2, starting transfers between devices, shift(): lax.ppermute(block, axis, [(i, (i + step) % count) for i in range(count)])  3.01 us
    ppermute x2, waiting for transfers between devices, shift(): lax.ppermute(block, axis, [(i, (i + step) % count) for i in range(count)])  1.84 us
  transfers between devices with their start and end apart: 23, of which 11 were waited for; matrix products, arithmetic and copies ran while one was open for 2% of the time, Pallas kernels for 10%

profile of v4, /device:TPU:0, one launch (start us, length us, event | category | flops | bytes accessed | tf_op | source)
XLA Modules:
  0.0 60.6 jit_solution(12080046509847876058)
XLA Ops:
  0.6 3.0 %collective-permute-start = (bf16[256,512]{1,0:T(8,128)(2,1)}, bf16[256,512]{1,0:T(8,128)(2,1)S(1)}, u32[]{:S(2)}, u32[]{:S(2)}) collective-permute-start(bf16[256,512]{1,0:T(8,128)(2,1)} %refs_1_.4), channel_id=1, source_target_pairs={{0,1},{1,0},{2,3},{3,2},{4,5},{5,4},{6,7},{7,6},{8,9},{9,8},{10,11... | collective-permute-start | bytes 786440 | tf_op jit(solution)/shard_map/ppermute | solution.py:37
  3.7 1.6 %collective-permute-start.2 = (bf16[512,256]{1,0:T(8,128)(2,1)S(1)}, bf16[512,256]{1,0:T(8,128)(2,1)S(1)}, u32[]{:S(2)}, u32[]{:S(2)}) collective-permute-start(bf16[512,256]{1,0:T(8,128)(2,1)S(1)} %constant_dynamic-slice_fusion.1.refs_3_.refs_5_), channel_id=1, source_target_pairs={{0,2},{1,3},{2,0},{3,1},{4,6},{5,7},{6,4},{7,5},{8,10},{9,11},{10,... | collective-permute-start | bytes 786440 | tf_op jit(solution)/shard_map/ppermute | solution.py:37
  5.3 1.0 %collective-permute-start.3 = (bf16[256,512]{1,0:T(8,128)(2,1)S(1)}, bf16[256,512]{1,0:T(8,128)(2,1)S(1)}, u32[]{:S(2)}, u32[]{:S(2)}) collective-permute-start(bf16[256,512]{1,0:T(8,128)(2,1)S(1)} %copy-done.2), channel_id=1, source_target_pairs={{0,1},{1,0},{2,3},{3,2},{4,5},{5,4},{6,7},{7,6},{8,9},{9,8},{10,11... | collective-permute-start | bytes 786440 | tf_op jit(solution)/shard_map/ppermute | solution.py:37
  6.2 1.0 %constant_dynamic-slice_fusion.refs_7_ = bf16[256,512]{1,0:T(8,128)(2,1)S(1)} fusion(bf16[512,512]{1,0:T(8,128)(2,1)} %param.10, s32[]{:T(128)S(6)} %select_n.4), kind=kLoop, calls=%fused_computation | loop fusion | bytes 524292 | tf_op jit(solution)/shard_map/dynamic_slice | solution.py:254
  7.2 0.9 %collective-permute-start.5 = (bf16[256,512]{1,0:T(8,128)(2,1)S(1)}, bf16[256,512]{1,0:T(8,128)(2,1)S(1)}, u32[]{:S(2)}, u32[]{:S(2)}) collective-permute-start(bf16[256,512]{1,0:T(8,128)(2,1)S(1)} %constant_dynamic-slice_fusion.refs_7_), channel_id=1, source_target_pairs={{0,2},{1,3},{2,0},{3,1},{4,6},{5,7},{6,4},{7,5},{8,10},{9,11},{10,... | collective-permute-start | bytes 786440 | tf_op jit(solution)/shard_map/ppermute | solution.py:37
  8.8 2.2 %collective-permute-done.far_ref.refs_1_.refs_2_ = bf16[256,512]{1,0:T(8,128)(2,1)S(1)} collective-permute-done((bf16[256,512]{1,0:T(8,128)(2,1)}, bf16[256,512]{1,0:T(8,128)(2,1)S(1)}, u32[]{:S(2)}, u32[]{:S(2)}) %collective-permute-start) | collective-permute-done | bytes 262176 | tf_op jit(solution)/shard_map/ppermute | solution.py:37
  11.1 1.9 %collective-permute-done.2.refs_1_.refs_4_.refs_6_ = bf16[512,256]{1,0:T(8,128)(2,1)S(1)} collective-permute-done((bf16[512,256]{1,0:T(8,128)(2,1)S(1)}, bf16[512,256]{1,0:T(8,128)(2,1)S(1)}, u32[]{:S(2)}, u32[]{:S(2)}) %collective-permute-start.2) | collective-permute-done | bytes 262176 | tf_op jit(solution)/shard_map/ppermute | solution.py:37
  13.0 2.8 %collective-permute-done.3.far_ref.refs_2_.refs_5_ = bf16[256,512]{1,0:T(8,128)(2,1)S(1)} collective-permute-done((bf16[256,512]{1,0:T(8,128)(2,1)S(1)}, bf16[256,512]{1,0:T(8,128)(2,1)S(1)}, u32[]{:S(2)}, u32[]{:S(2)}) %collective-permute-start.3) | collective-permute-done | bytes 262176 | tf_op jit(solution)/shard_map/ppermute | solution.py:37
  15.9 1.2 %collective-permute-done.5.refs_8_ = bf16[256,512]{1,0:T(8,128)(2,1)S(1)} collective-permute-done((bf16[256,512]{1,0:T(8,128)(2,1)S(1)}, bf16[256,512]{1,0:T(8,128)(2,1)S(1)}, u32[]{:S(2)}, u32[]{:S(2)}) %collective-permute-start.5) | collective-permute-done | bytes 262176 | tf_op jit(solution)/shard_map/ppermute | solution.py:37
  17.2 1.0 %copy-done.3 = bf16[1,4,256,256]{3,2,1,0:T(8,128)(2,1)S(1)} copy-done((bf16[1,4,256,256]{3,2,1,0:T(8,128)(2,1)S(1)}, bf16[1,4,256,256]{3,2,1,0:T(8,128)(2,1)}, u32[]{:S(2)}) %copy-start.3) | copy-done | bytes 524312
  18.4 1.5 %forward.1 = (bf16[4,512,256]{2,1,0:T(8,128)(2,1)S(1)}, bf16[4,512,256]{2,1,0:T(8,128)(2,1)S(1)}) custom-call(bf16[256,512]{1,0:T(8,128)(2,1)S(1)} %copy-done.1, bf16[256,512]{1,0:T(8,128)(2,1)S(1)} %collective-permute-done.far_ref.refs_1_.refs_2_, bf16[2,256,512]{2,1,0:T(8,128)(2,1)S(1)} %collective-permute-done.1.refs_2_.refs_3_, ...), custom_call_target="tpu_custom_call" | custom-call | flops 1000000000 | tf_op jit(solution)/shard_map/forward/pallas_call | solution.py:47
  19.9 0.4 out.1.refs_9_
  20.3 1.6 %collective-permute-start.9 = (bf16[256,512]{1,0:T(8,128)(2,1)S(1)}, bf16[256,512]{1,0:T(8,128)(2,1)S(1)}, u32[]{:S(2)}, u32[]{:S(2)}) collective-permute-start(bf16[256,512]{1,0:T(8,128)(2,1)S(1)} %out.1.refs_9_), channel_id=1, source_target_pairs={{0,2},{1,3},{2,0},{3,1},{4,6},{5,7},{6,4},{7,5},{8,10},{9,11},{10,... | collective-permute-start | bytes 786440 | tf_op jit(solution)/shard_map/ppermute | solution.py:37
  21.9 1.5 %in.1 = (bf16[4,512,256]{2,1,0:T(8,128)(2,1)S(1)}, f32[256,512]{1,0:T(8,128)S(1)}, bf16[256,512]{1,0:T(8,128)(2,1)S(1)}) custom-call(bf16[4,512,256]{2,1,0:T(8,128)(2,1)S(1)} %get-tuple-element.19.refs_0_, bf16[256,512]{1,0:T(8,128)(2,1)S(1)} %copy-done.1, bf16[256,512]{1,0:T(8,128)(2,1)S(1)} %collective-permute-done.far_ref.refs_1_.refs_2_, ...), custom_call_target="tpu_custom_call" | custom-call | flops 100000000 | tf_op jit(solution)/shard_map/in/pallas_call | solution.py:47
  23.4 1.6 %collective-permute-start.8 = (bf16[256,512]{1,0:T(8,128)(2,1)S(1)}, bf16[256,512]{1,0:T(8,128)(2,1)S(1)}, u32[]{:S(2)}, u32[]{:S(2)}) collective-permute-start(bf16[256,512]{1,0:T(8,128)(2,1)S(1)} %get-tuple-element.24), channel_id=1, source_target_pairs={{0,8},{4,12},{8,0},{12,4},{16,24},{20,28},{24,16},{28,20},{1,9},{5... | collective-permute-start | bytes 786440 | tf_op jit(solution)/shard_map/ppermute | solution.py:37
  25.1 1.0 %own.1 = (f32[256,512]{1,0:T(8,128)S(1)}, bf16[2,256,512]{2,1,0:T(8,128)(2,1)S(1)}, bf16[2,256,512]{2,1,0:T(8,128)(2,1)S(1)}) custom-call(bf16[4,512,256]{2,1,0:T(8,128)(2,1)S(1)} %get-tuple-element.18.refs_0_.refs_4_, bf16[256,512]{1,0:T(8,128)(2,1)S(1)} %copy-done.2, bf16[256,512]{1,0:T(8,128)(2,1)S(1)} %collective-permute-done.3.far_ref.refs_2_.refs_5_, ...), custom_call_target="tpu_custom_call" | custom-call | flops 3000000000 | tf_op jit(solution)/shard_map/own/pallas_call | solution.py:47
  26.2 2.0 %collective-permute-done.9.refs_1_ = bf16[256,512]{1,0:T(8,128)(2,1)S(1)} collective-permute-done((bf16[256,512]{1,0:T(8,128)(2,1)S(1)}, bf16[256,512]{1,0:T(8,128)(2,1)S(1)}, u32[]{:S(2)}, u32[]{:S(2)}) %collective-permute-start.9) | collective-permute-done | bytes 262176 | tf_op jit(solution)/shard_map/ppermute | solution.py:37
  28.2 1.6 %collective-permute-start.11 = (bf16[128,512]{1,0:T(8,128)(2,1)S(1)}, bf16[128,512]{1,0:T(8,128)(2,1)S(1)}, u32[]{:S(2)}, u32[]{:S(2)}) collective-permute-start(bf16[128,512]{1,0:T(8,128)(2,1)S(1)} %get-tuple-element.28), channel_id=1, source_target_pairs={{0,8},{4,12},{8,0},{12,4},{16,24},{20,28},{24,16},{28,20},{1,9},{5... | collective-permute-start | bytes 393224 | tf_op jit(solution)/shard_map/ppermute | solution.py:37
  29.8 2.5 %collective-permute-done.8.refs_1_ = bf16[256,512]{1,0:T(8,128)(2,1)S(1)} collective-permute-done((bf16[256,512]{1,0:T(8,128)(2,1)S(1)}, bf16[256,512]{1,0:T(8,128)(2,1)S(1)}, u32[]{:S(2)}, u32[]{:S(2)}) %collective-permute-start.8) | collective-permute-done | bytes 262176 | tf_op jit(solution)/shard_map/ppermute | solution.py:37
  32.6 1.3 %collective-permute-start.10 = (bf16[256,512]{1,0:T(8,128)(2,1)S(1)}, bf16[256,512]{1,0:T(8,128)(2,1)S(1)}, u32[]{:S(2)}, u32[]{:S(2)}) collective-permute-start(bf16[256,512]{1,0:T(8,128)(2,1)S(1)} %other.1.refs_2_), channel_id=1, source_target_pairs={{0,1},{1,0},{2,3},{3,2},{4,5},{5,4},{6,7},{7,6},{8,9},{9,8},{10,11... | collective-permute-start | bytes 786440 | tf_op jit(solution)/shard_map/ppermute | solution.py:37
  34.0 2.6 %collective-permute-start.16 = (bf16[128,512]{1,0:T(8,128)(2,1)S(1)}, bf16[128,512]{1,0:T(8,128)(2,1)S(1)}, u32[]{:S(2)}, u32[]{:S(2)}) collective-permute-start(bf16[128,512]{1,0:T(8,128)(2,1)S(1)} %sum_out.1.refs_0_), channel_id=1, source_target_pairs={{0,16},{4,20},{8,24},{12,28},{16,0},{20,4},{24,8},{28,12},{1,17},{... | collective-permute-start | bytes 393224 | tf_op jit(solution)/shard_map/ppermute | solution.py:37
  36.6 2.4 %collective-permute-done.10.last_ref = bf16[256,512]{1,0:T(8,128)(2,1)S(1)} collective-permute-done((bf16[256,512]{1,0:T(8,128)(2,1)S(1)}, bf16[256,512]{1,0:T(8,128)(2,1)S(1)}, u32[]{:S(2)}, u32[]{:S(2)}) %collective-permute-start.10) | collective-permute-done | bytes 262176 | tf_op jit(solution)/shard_map/ppermute | solution.py:37
  39.0 1.8 %tiles.1 = (bf16[256,512]{1,0:T(8,128)(2,1)S(1)}, bf16[256,512]{1,0:T(8,128)(2,1)S(1)}, f32[256,512]{1,0:T(8,128)S(1)}) custom-call(bf16[2,256,512]{2,1,0:T(8,128)(2,1)S(1)} %get-tuple-element.21.keep_ref, bf16[2,256,512]{2,1,0:T(8,128)(2,1)S(1)} %collective-permute-done.7.got_ref, bf16[256,512]{1,0:T(8,128)(2,1)S(1)} %collective-permute-done.10.last_ref, ...), custom_call_target="tpu_custom_call" | custom-call | flops 100000000 | tf_op jit(solution)/shard_map/tiles/pallas_call | solution.py:47
  40.9 2.2 %collective-permute-start.15 = (bf16[128,512]{1,0:T(8,128)(2,1)S(1)}, bf16[128,512]{1,0:T(8,128)(2,1)S(1)}, u32[]{:S(2)}, u32[]{:S(2)}) collective-permute-start(bf16[128,512]{1,0:T(8,128)(2,1)S(1)} %sum_in.1.refs_2_.refs_0_), channel_id=1, source_target_pairs={{0,16},{4,20},{8,24},{12,28},{16,0},{20,4},{24,8},{28,12},{1,17},{... | collective-permute-start | bytes 393224 | tf_op jit(solution)/shard_map/ppermute | solution.py:37
  43.1 0.6 %collective-permute-done.16.refs_1_ = bf16[128,512]{1,0:T(8,128)(2,1)S(1)} collective-permute-done((bf16[128,512]{1,0:T(8,128)(2,1)S(1)}, bf16[128,512]{1,0:T(8,128)(2,1)S(1)}, u32[]{:S(2)}, u32[]{:S(2)}) %collective-permute-start.16) | collective-permute-done | bytes 131104 | tf_op jit(solution)/shard_map/ppermute | solution.py:37
  43.8 1.3 %collective-permute-start.21 = (bf16[128,512]{1,0:T(8,128)(2,1)S(1)}, bf16[128,512]{1,0:T(8,128)(2,1)S(1)}, u32[]{:S(2)}, u32[]{:S(2)}) collective-permute-start(bf16[128,512]{1,0:T(8,128)(2,1)S(1)} %add_out.1.refs_2_.refs_7_), channel_id=1, source_target_pairs={{0,8},{4,12},{8,0},{12,4},{16,24},{20,28},{24,16},{28,20},{1,9},{5... | collective-permute-start | bytes 393224 | tf_op jit(solution)/shard_map/ppermute | solution.py:37
  45.0 3.0 %collective-permute-start.12 = (bf16[256,512]{1,0:T(8,128)(2,1)S(1)}, bf16[256,512]{1,0:T(8,128)(2,1)S(1)}, u32[]{:S(2)}, u32[]{:S(2)}) collective-permute-start(bf16[256,512]{1,0:T(8,128)(2,1)S(1)} %get-tuple-element.30.refs_2_), channel_id=1, source_target_pairs={{0,28},{4,0},{8,4},{12,8},{16,12},{20,16},{24,20},{28,24},{1,29},{... | collective-permute-start | bytes 786440 | tf_op jit(solution)/shard_map/ppermute | solution.py:42
  48.1 1.0 %collective-permute-start.18 = (bf16[128,512]{1,0:T(8,128)(2,1)S(1)}, bf16[128,512]{1,0:T(8,128)(2,1)S(1)}, u32[]{:S(2)}, u32[]{:S(2)}) collective-permute-start(bf16[128,512]{1,0:T(8,128)(2,1)S(1)} %add_in.1.refs_3_), channel_id=1, source_target_pairs={{0,8},{4,12},{8,0},{12,4},{16,24},{20,28},{24,16},{28,20},{1,9},{5... | collective-permute-start | bytes 393224 | tf_op jit(solution)/shard_map/ppermute | solution.py:37
  49.1 0.5 collective-permute-start.17
  49.6 7.0 %collective-permute-done.18.refs_5_ = bf16[128,512]{1,0:T(8,128)(2,1)S(1)} collective-permute-done((bf16[128,512]{1,0:T(8,128)(2,1)S(1)}, bf16[128,512]{1,0:T(8,128)(2,1)S(1)}, u32[]{:S(2)}, u32[]{:S(2)}) %collective-permute-start.18) | collective-permute-done | bytes 131104 | tf_op jit(solution)/shard_map/ppermute | solution.py:37
  56.6 1.8 %collective-permute-done.13.refs_2_ = bf16[256,512]{1,0:T(8,128)(2,1)S(1)} collective-permute-done((bf16[256,512]{1,0:T(8,128)(2,1)S(1)}, bf16[256,512]{1,0:T(8,128)(2,1)S(1)}, u32[]{:S(2)}, u32[]{:S(2)}) %collective-permute-start.13) | collective-permute-done | bytes 262176 | tf_op jit(solution)/shard_map/ppermute | solution.py:42
  58.5 2.1 %finish.1 = (bf16[256,512]{1,0:T(8,128)(2,1)}, f32[512,512]{1,0:T(8,128)}, f32[512,512]{1,0:T(8,128)}) custom-call(f32[256,512]{1,0:T(8,128)S(1)} %get-tuple-element.29.refs_0_, bf16[256,512]{1,0:T(8,128)(2,1)S(1)} %collective-permute-done.12.refs_1_, bf16[256,512]{1,0:T(8,128)(2,1)S(1)} %collective-permute-done.13.refs_2_, ...), custom_call_target="tpu_custom_call" | custom-call | flops 100000000 | tf_op jit(solution)/shard_map/finish/pallas_call | solution.py:47
  (44 shorter events, 1.1 us)
Async XLA Ops:
  0.6 3.0 %copy-start = (bf16[512,512]{1,0:T(8,128)(2,1)S(1)}, bf16[512,512]{1,0:T(8,128)(2,1)}, u32[]{:S(2)}) copy-start(bf16[512,512]{1,0:T(8,128)(2,1)} %param.9) | copy-start | bytes 1572868
  0.6 10.4 %collective-permute-start = (bf16[256,512]{1,0:T(8,128)(2,1)}, bf16[256,512]{1,0:T(8,128)(2,1)S(1)}, u32[]{:S(2)}, u32[]{:S(2)}) collective-permute-start(bf16[256,512]{1,0:T(8,128)(2,1)} %refs_1_.4), channel_id=1, source_target_pairs={{0,1},{1,0},{2,3},{3,2},{4,5},{5,4},{6,7},{7,6},{8,9},{9,8},{10,11... | collective-permute-start | bytes 786440 | tf_op jit(solution)/shard_map/ppermute | solution.py:37
  3.7 1.6 %copy-start.2 = (bf16[256,512]{1,0:T(8,128)(2,1)S(1)}, bf16[256,512]{1,0:T(8,128)(2,1)}, u32[]{:S(2)}) copy-start(bf16[256,512]{1,0:T(8,128)(2,1)} %cot_ref.1) | copy-start | bytes 786436
  3.7 7.3 %copy-start.1 = (bf16[256,512]{1,0:T(8,128)(2,1)S(1)}, bf16[256,512]{1,0:T(8,128)(2,1)}, u32[]{:S(2)}) copy-start(bf16[256,512]{1,0:T(8,128)(2,1)} %refs_1_.4) | copy-start | bytes 786436
  3.7 9.3 %collective-permute-start.2 = (bf16[512,256]{1,0:T(8,128)(2,1)S(1)}, bf16[512,256]{1,0:T(8,128)(2,1)S(1)}, u32[]{:S(2)}, u32[]{:S(2)}) collective-permute-start(bf16[512,256]{1,0:T(8,128)(2,1)S(1)} %constant_dynamic-slice_fusion.1.refs_3_.refs_5_), channel_id=1, source_target_pairs={{0,2},{1,3},{2,0},{3,1},{4,6},{5,7},{6,4},{7,5},{8,10},{9,11},{10,... | collective-permute-start | bytes 786440 | tf_op jit(solution)/shard_map/ppermute | solution.py:37
  5.3 10.5 %collective-permute-start.3 = (bf16[256,512]{1,0:T(8,128)(2,1)S(1)}, bf16[256,512]{1,0:T(8,128)(2,1)S(1)}, u32[]{:S(2)}, u32[]{:S(2)}) collective-permute-start(bf16[256,512]{1,0:T(8,128)(2,1)S(1)} %copy-done.2), channel_id=1, source_target_pairs={{0,1},{1,0},{2,3},{3,2},{4,5},{5,4},{6,7},{7,6},{8,9},{9,8},{10,11... | collective-permute-start | bytes 786440 | tf_op jit(solution)/shard_map/ppermute | solution.py:37
  7.2 9.9 %collective-permute-start.5 = (bf16[256,512]{1,0:T(8,128)(2,1)S(1)}, bf16[256,512]{1,0:T(8,128)(2,1)S(1)}, u32[]{:S(2)}, u32[]{:S(2)}) collective-permute-start(bf16[256,512]{1,0:T(8,128)(2,1)S(1)} %constant_dynamic-slice_fusion.refs_7_), channel_id=1, source_target_pairs={{0,2},{1,3},{2,0},{3,1},{4,6},{5,7},{6,4},{7,5},{8,10},{9,11},{10,... | collective-permute-start | bytes 786440 | tf_op jit(solution)/shard_map/ppermute | solution.py:37
  11.0 7.3 %collective-permute-start.1 = (bf16[2,256,512]{2,1,0:T(8,128)(2,1)S(1)}, bf16[2,256,512]{2,1,0:T(8,128)(2,1)S(1)}, u32[]{:S(2)}, u32[]{:S(2)}) collective-permute-start(bf16[2,256,512]{2,1,0:T(8,128)(2,1)S(1)} %gate_agg.1.refs_0_), channel_id=1, source_target_pairs={{0,4},{4,0},{8,12},{12,8},{16,20},{20,16},{24,28},{28,24},{1,5},{5... | collective-permute-start | bytes 1572872 | tf_op jit(solution)/shard_map/ppermute | solution.py:37
  15.8 4.0 %collective-permute-start.4 = (bf16[2,256,512]{2,1,0:T(8,128)(2,1)S(1)}, bf16[2,256,512]{2,1,0:T(8,128)(2,1)S(1)}, u32[]{:S(2)}, u32[]{:S(2)}) collective-permute-start(bf16[2,256,512]{2,1,0:T(8,128)(2,1)S(1)} %gate_cot.1.refs_0_), channel_id=1, source_target_pairs={{0,4},{4,0},{8,12},{12,8},{16,20},{20,16},{24,28},{28,24},{1,5},{5... | collective-permute-start | bytes 1572872 | tf_op jit(solution)/shard_map/ppermute | solution.py:37
  17.1 1.0 %copy-start.3 = (bf16[1,4,256,256]{3,2,1,0:T(8,128)(2,1)S(1)}, bf16[1,4,256,256]{3,2,1,0:T(8,128)(2,1)}, u32[]{:S(2)}) copy-start(bf16[1,4,256,256]{3,2,1,0:T(8,128)(2,1)} %tiles_ref.1) | copy-start | bytes 1572868
  17.1 2.7 %collective-permute-start.6 = (bf16[16,512]{1,0:T(8,128)(2,1)S(1)}, bf16[16,512]{1,0:T(8,128)(2,1)S(1)}, u32[]{:S(2)}, u32[]{:S(2)}) collective-permute-start(bf16[16,512]{1,0:T(8,128)(2,1)S(1)} %lift.1), channel_id=1, source_target_pairs={{0,4},{4,0},{8,12},{12,8},{16,20},{20,16},{24,28},{28,24},{1,5},{5... | collective-permute-start | bytes 49160 | tf_op jit(solution)/shard_map/ppermute | solution.py:37
  20.3 7.8 %collective-permute-start.9 = (bf16[256,512]{1,0:T(8,128)(2,1)S(1)}, bf16[256,512]{1,0:T(8,128)(2,1)S(1)}, u32[]{:S(2)}, u32[]{:S(2)}) collective-permute-start(bf16[256,512]{1,0:T(8,128)(2,1)S(1)} %out.1.refs_9_), channel_id=1, source_target_pairs={{0,2},{1,3},{2,0},{3,1},{4,6},{5,7},{6,4},{7,5},{8,10},{9,11},{10,... | collective-permute-start | bytes 786440 | tf_op jit(solution)/shard_map/ppermute | solution.py:37
  23.4 8.9 %collective-permute-start.8 = (bf16[256,512]{1,0:T(8,128)(2,1)S(1)}, bf16[256,512]{1,0:T(8,128)(2,1)S(1)}, u32[]{:S(2)}, u32[]{:S(2)}) collective-permute-start(bf16[256,512]{1,0:T(8,128)(2,1)S(1)} %get-tuple-element.24), channel_id=1, source_target_pairs={{0,8},{4,12},{8,0},{12,4},{16,24},{20,28},{24,16},{28,20},{1,9},{5... | collective-permute-start | bytes 786440 | tf_op jit(solution)/shard_map/ppermute | solution.py:37
  26.1 6.4 %collective-permute-start.7 = (bf16[2,256,512]{2,1,0:T(8,128)(2,1)S(1)}, bf16[2,256,512]{2,1,0:T(8,128)(2,1)S(1)}, u32[]{:S(2)}, u32[]{:S(2)}) collective-permute-start(bf16[2,256,512]{2,1,0:T(8,128)(2,1)S(1)} %get-tuple-element.22), channel_id=1, source_target_pairs={{0,4},{4,0},{8,12},{12,8},{16,20},{20,16},{24,28},{28,24},{1,5},{5... | collective-permute-start | bytes 1572872 | tf_op jit(solution)/shard_map/ppermute | solution.py:37
  28.2 5.7 %collective-permute-start.11 = (bf16[128,512]{1,0:T(8,128)(2,1)S(1)}, bf16[128,512]{1,0:T(8,128)(2,1)S(1)}, u32[]{:S(2)}, u32[]{:S(2)}) collective-permute-start(bf16[128,512]{1,0:T(8,128)(2,1)S(1)} %get-tuple-element.28), channel_id=1, source_target_pairs={{0,8},{4,12},{8,0},{12,4},{16,24},{20,28},{24,16},{28,20},{1,9},{5... | collective-permute-start | bytes 393224 | tf_op jit(solution)/shard_map/ppermute | solution.py:37
  32.4 8.4 %collective-permute-start.14 = (bf16[128,512]{1,0:T(8,128)(2,1)S(1)}, bf16[128,512]{1,0:T(8,128)(2,1)S(1)}, u32[]{:S(2)}, u32[]{:S(2)}) collective-permute-start(bf16[128,512]{1,0:T(8,128)(2,1)S(1)} %get-tuple-element.32), channel_id=1, source_target_pairs={{0,2},{1,3},{2,0},{3,1},{4,6},{5,7},{6,4},{7,5},{8,10},{9,11},{10,... | collective-permute-start | bytes 393224 | tf_op jit(solution)/shard_map/ppermute | solution.py:37
  32.6 6.5 %copy-start.4 = (s32[1,4]{1,0:T(1,128)S(1)}, s32[1,4]{1,0:T(1,128)}, u32[]{:S(2)}) copy-start(s32[1,4]{1,0:T(1,128)} %cols_ref.1) | copy-start | bytes 52
  32.6 6.4 %collective-permute-start.10 = (bf16[256,512]{1,0:T(8,128)(2,1)S(1)}, bf16[256,512]{1,0:T(8,128)(2,1)S(1)}, u32[]{:S(2)}, u32[]{:S(2)}) collective-permute-start(bf16[256,512]{1,0:T(8,128)(2,1)S(1)} %other.1.refs_2_), channel_id=1, source_target_pairs={{0,1},{1,0},{2,3},{3,2},{4,5},{5,4},{6,7},{7,6},{8,9},{9,8},{10,11... | collective-permute-start | bytes 786440 | tf_op jit(solution)/shard_map/ppermute | solution.py:37
  34.0 9.7 %collective-permute-start.16 = (bf16[128,512]{1,0:T(8,128)(2,1)S(1)}, bf16[128,512]{1,0:T(8,128)(2,1)S(1)}, u32[]{:S(2)}, u32[]{:S(2)}) collective-permute-start(bf16[128,512]{1,0:T(8,128)(2,1)S(1)} %sum_out.1.refs_0_), channel_id=1, source_target_pairs={{0,16},{4,20},{8,24},{12,28},{16,0},{20,4},{24,8},{28,12},{1,17},{... | collective-permute-start | bytes 393224 | tf_op jit(solution)/shard_map/ppermute | solution.py:37
  40.9 7.2 %collective-permute-start.15 = (bf16[128,512]{1,0:T(8,128)(2,1)S(1)}, bf16[128,512]{1,0:T(8,128)(2,1)S(1)}, u32[]{:S(2)}, u32[]{:S(2)}) collective-permute-start(bf16[128,512]{1,0:T(8,128)(2,1)S(1)} %sum_in.1.refs_2_.refs_0_), channel_id=1, source_target_pairs={{0,16},{4,20},{8,24},{12,28},{16,0},{20,4},{24,8},{28,12},{1,17},{... | collective-permute-start | bytes 393224 | tf_op jit(solution)/shard_map/ppermute | solution.py:37
  43.8 5.4 %collective-permute-start.21 = (bf16[128,512]{1,0:T(8,128)(2,1)S(1)}, bf16[128,512]{1,0:T(8,128)(2,1)S(1)}, u32[]{:S(2)}, u32[]{:S(2)}) collective-permute-start(bf16[128,512]{1,0:T(8,128)(2,1)S(1)} %add_out.1.refs_2_.refs_7_), channel_id=1, source_target_pairs={{0,8},{4,12},{8,0},{12,4},{16,24},{20,28},{24,16},{28,20},{1,9},{5... | collective-permute-start | bytes 393224 | tf_op jit(solution)/shard_map/ppermute | solution.py:37
  45.0 4.1 %collective-permute-start.20 = (bf16[128,512]{1,0:T(8,128)(2,1)S(1)}, bf16[128,512]{1,0:T(8,128)(2,1)S(1)}, u32[]{:S(2)}, u32[]{:S(2)}) collective-permute-start(bf16[128,512]{1,0:T(8,128)(2,1)S(1)} %add_out.1.refs_2_.refs_7_), channel_id=1, source_target_pairs={{0,4},{4,0},{8,12},{12,8},{16,20},{20,16},{24,28},{28,24},{1,5},{5... | collective-permute-start | bytes 393224 | tf_op jit(solution)/shard_map/ppermute | solution.py:37
  45.0 11.6 %collective-permute-start.12 = (bf16[256,512]{1,0:T(8,128)(2,1)S(1)}, bf16[256,512]{1,0:T(8,128)(2,1)S(1)}, u32[]{:S(2)}, u32[]{:S(2)}) collective-permute-start(bf16[256,512]{1,0:T(8,128)(2,1)S(1)} %get-tuple-element.30.refs_2_), channel_id=1, source_target_pairs={{0,28},{4,0},{8,4},{12,8},{16,12},{20,16},{24,20},{28,24},{1,29},{... | collective-permute-start | bytes 786440 | tf_op jit(solution)/shard_map/ppermute | solution.py:42
  48.0 10.4 %collective-permute-start.13 = (bf16[256,512]{1,0:T(8,128)(2,1)S(1)}, bf16[256,512]{1,0:T(8,128)(2,1)S(1)}, u32[]{:S(2)}, u32[]{:S(2)}) collective-permute-start(bf16[256,512]{1,0:T(8,128)(2,1)S(1)} %get-tuple-element.31), channel_id=1, source_target_pairs={{0,4},{4,8},{8,12},{12,16},{16,20},{20,24},{24,28},{28,0},{1,5},{5... | collective-permute-start | bytes 786440 | tf_op jit(solution)/shard_map/ppermute | solution.py:42
  48.1 8.5 %collective-permute-start.18 = (bf16[128,512]{1,0:T(8,128)(2,1)S(1)}, bf16[128,512]{1,0:T(8,128)(2,1)S(1)}, u32[]{:S(2)}, u32[]{:S(2)}) collective-permute-start(bf16[128,512]{1,0:T(8,128)(2,1)S(1)} %add_in.1.refs_3_), channel_id=1, source_target_pairs={{0,8},{4,12},{8,0},{12,4},{16,24},{20,28},{24,16},{28,20},{1,9},{5... | collective-permute-start | bytes 393224 | tf_op jit(solution)/shard_map/ppermute | solution.py:37
  49.1 7.5 %collective-permute-start.22 = (bf16[128,512]{1,0:T(8,128)(2,1)S(1)}, bf16[128,512]{1,0:T(8,128)(2,1)S(1)}, u32[]{:S(2)}, u32[]{:S(2)}) collective-permute-start(bf16[128,512]{1,0:T(8,128)(2,1)S(1)} %collective-permute-done.21.refs_9_), channel_id=1, source_target_pairs={{0,4},{4,0},{8,12},{12,8},{16,20},{20,16},{24,28},{28,24},{1,5},{5... | collective-permute-start | bytes 393224 | tf_op jit(solution)/shard_map/ppermute | solution.py:37
  49.1 7.5 %collective-permute-start.17 = (bf16[128,512]{1,0:T(8,128)(2,1)S(1)}, bf16[128,512]{1,0:T(8,128)(2,1)S(1)}, u32[]{:S(2)}, u32[]{:S(2)}) collective-permute-start(bf16[128,512]{1,0:T(8,128)(2,1)S(1)} %add_in.1.refs_3_), channel_id=1, source_target_pairs={{0,4},{4,0},{8,12},{12,8},{16,20},{20,16},{24,28},{28,24},{1,5},{5... | collective-permute-start | bytes 393224 | tf_op jit(solution)/shard_map/ppermute | solution.py:37
  56.6 1.9 %collective-permute-start.19 = (bf16[128,512]{1,0:T(8,128)(2,1)S(1)}, bf16[128,512]{1,0:T(8,128)(2,1)S(1)}, u32[]{:S(2)}, u32[]{:S(2)}) collective-permute-start(bf16[128,512]{1,0:T(8,128)(2,1)S(1)} %collective-permute-done.18.refs_5_), channel_id=1, source_target_pairs={{0,4},{4,0},{8,12},{12,8},{16,20},{20,16},{24,28},{28,24},{1,5},{5... | collective-permute-start | bytes 393224 | tf_op jit(solution)/shard_map/ppermute | solution.py:37

commit v5 on v4

--- a/solution.py
+++ b/solution.py
@@ -12,8 +12,10 @@
 F32 = jnp.float32
 VMEM = pl.BlockSpec(memory_space=pltpu.VMEM)
 SMEM = pl.BlockSpec(memory_space=pltpu.SMEM)
-COST = {'in': 0.1, 'place_out': 0.1, 'out': 8, 'middle': 8, 'sum_out': 25, 'add_out': 1, 'add_in': 3, 'forward': 1, 'sum_in': 25, 'place_in': 1, 'tiles': 0.1, 'other': 0.1, 'gate_cot': 8, 'lift': 9, 'own': 3, 'split_out': 25}
-ORDER = ['gate_agg', 'need_ykin', 'gate_cot', 'turn', 'forward', 'tiny', 'out', 'in', 'own', 'split_out', 'middle', 'other', 'sum_out', 'tiles', 'sum_in', 'add_out', 'add_in']
+COST = {
+    "both_cot": 8, "forward": 1, "lift": 9, "out": 8, "own": 3, "split": 25, "middle": 8,
+    "sum_out": 25, "sum_in": 25, "add_out": 1, "add_in": 3,
+}
 ANY = pl.BlockSpec(memory_space=pl.ANY)
 
 
@@ -247,111 +249,110 @@
     def shape(*dims, dtype=BF16):
         return jax.ShapeDtypeStruct(dims, dtype)
 
-    hidden = shape(4, pieces * half, rows)
+    before = []
+
+    def run(name, kernel, outs, args, **options):
+        results = call(name, kernel, outs, args, tuple(before), **options)
+        before[:] = [results[0] if isinstance(results, (list, tuple)) else results]
+        return results
+
+    def total(name, *parts):
+        before[:] = [add(name, parts, tuple(before))]
+        return before[0]
+
     agg_x = swap(aggregated, "rep", 1)
     cot_x = swap(cotangent, "rep", 1)
     win = lax.dynamic_slice_in_dim(kernel_in, core() * half, half, axis=1)
     wout = lax.dynamic_slice_in_dim(kernel_out, core() * half, half, axis=0)
     wins = [swap(win, "rep", s) for s in shards]
     wouts = [swap(wout, "rep", s) for s in shards]
-    v = {}
-    token = []
-
-    def aggs():
-        return aggregated, agg_x, v['agg_c']
-
-    def cots():
-        return cotangent, cot_x, v['cot_c']
-
-    def after(first):
-        out = (token[0],)
-        return out
-
-    def run(name, kernel, outs, args, **kw):
-        got = call(name, kernel, outs, args, tuple(token), **kw)
-        token[:] = [got[0] if isinstance(got, (list, tuple)) else got]
-        return got
-
-    def total(name, parts):
-        got = add(name, parts, tuple(token))
-        token[:] = [got]
-        return got
-
-    def quarters(name):
-        z_piece = v['z_' + name]
-        return v['sum_' + name], swap(v['sum_' + name], "node", 1), z_piece, swap(z_piece, "node", 1)
-
-    for step in ORDER:
-        if step == 'turn':
-            v['turned'] = run("turn", turn_kernel, shape(*tile_values.shape[1:]), (tile_values,))
-        elif step == 'gate_agg':
-            v['agg_c'] = swap(run("gate_agg", both_kernel, shape(2, rows, width), (aggregated, agg_x)), "node", 1)
-        elif step == 'gate_cot':
-            v['cot_c'] = swap(run("gate_cot", both_kernel, shape(2, rows, width), (cotangent, cot_x)), "node", 1)
-        elif step == 'forward':
-            v['act'], v['slope'] = run("forward", functools.partial(forward_kernel, pieces), [hidden] * 2, (*aggs(), win, *wins))
-        elif step == 'out':
-            part_out = run("out", functools.partial(out_kernel, far), [shape(half, width)] * far, (v['act'], *cots()))
-            v['got_out'] = [swap(part, "rep", s) for part, s in zip(part_out, shards)]
-        elif step == 'in':
-            v['grad_pre'], v['keep_in'], give = run("in", functools.partial(in_kernel, pieces),
-                [hidden, shape(pieces * quarter, width, dtype=F32), shape(pieces * quarter, width)],
-                (v['slope'], *aggs(), *cots(), wout, *wouts))
-            v['zgot_in'] = swap(give, "node", 2)
-        elif step == 'middle':
-            v['mine_in'], *gives = run("middle", functools.partial(middle_kernel, pieces),
-                [shape(quarter, width, dtype=F32)] + [shape(quarter, width)] * far, (v['keep_in'], v['zgot_in']))
-            v['ygot_in'] = [swap(give, "rep", s) for give, s in zip(gives, shards)]
-        elif step == 'own':
-            v['own_out'], v['keep'], send = run("own", functools.partial(own_kernel, pieces),
-                [shape(half, width, dtype=F32)] + [shape(2, rows, width)] * 2,
-                (v['act'], *cots(), v['grad_pre'], win, *wins))
-            v['got'] = swap(send, "node", 1)
-        elif step == 'split_out':
-            v['mine_out'], give = run("split_out", functools.partial(split_kernel, pieces),
-                [shape(quarter, width, dtype=F32), shape(quarter, width)], (v['own_out'], *v['got_out']))
-            v['ygot_out'] = [swap(give, "node", 2)]
-        elif step == 'other':
-            v['other'] = run("other", add_rows_kernel, shape(rows, width), (v['keep'], v['got']))
-            v['last'] = swap(v['other'], "rep", 1)
-        elif step == 'tiles':
-            low, high, v['own'] = run("tiles", tiles_kernel, [shape(rows, width)] * 2 + [shape(rows, width, dtype=F32)],
-                (v['keep'], v['got'], v['last'], v['turned'], tile_cols, tile_count, cotangent),
-                specs=[VMEM] * 4 + [SMEM] * 2 + [VMEM], scratch=[pltpu.VMEM((3, rows, width), F32)])
-            v['next'] = shift(low, "node", -1)
-            v['prev'] = shift(high, "node", 1)
-        elif step in ('sum_out', 'sum_in'):
-            n = step[4:]
-            v['t_' + n] = total("sum_" + n, (v['mine_' + n], *v['ygot_' + n]))
-            if groups == 2:
-                v['cgot_' + n] = swap(v['t_' + n], "node", 4)
-        elif step in ('add_out', 'add_in'):
-            n = step[4:]
-            if groups == 2:
-                v['sum_' + n] = total("add_" + n, (v['t_' + n], v['cgot_' + n]))
-            else:
-                v['sum_' + n] = over_groups(v['t_' + n])
-            v['z_' + n] = swap(v['sum_' + n], "node", 2)
-        elif step in ('turn_out', 'turn_in'):
-            n = step[5:]
-            v[step] = total(step, (v['z_' + n],))
-        elif step == 'need_ykin':
-            token += wins
-        elif step == 'halo':
-            token += [v['next'], v['prev']]
-        elif step == 'need_zout':
-            token += [v['z_out']]
-        elif step == 'need_last':
-            token += [v['last']]
-        elif step == 'tiny':
-            token += [swap(add("lift", (w[:16],)), "node", 1) for w in wouts[:1]]
-        elif step == 'tail':
-            token += [swap(add("lift2", (v['next'][:16], v['prev'][:16])), "node", 1)]
+    pair = shape(2, rows, width)
+    aggs = (
+        aggregated,
+        agg_x,
+        swap(run("both_agg", both_kernel, pair, (aggregated, agg_x)), "node", 1),
+    )
+    before += wins
+    cots = (
+        cotangent,
+        cot_x,
+        swap(run("both_cot", both_kernel, pair, (cotangent, cot_x)), "node", 1),
+    )
+
+    hidden = shape(4, pieces * half, rows)
+    act, slope = run(
+        "forward", functools.partial(forward_kernel, pieces), [hidden] * 2, (*aggs, win, *wins)
+    )
+    before.append(swap(add("lift", (wouts[0][:16],)), "node", 1))
+    part_out = run(
+        "out", functools.partial(out_kernel, far), [shape(half, width)] * far, (act, *cots)
+    )
+    got_out = [swap(part, "rep", s) for part, s in zip(part_out, shards)]
+    grad_pre, keep_in, give_in = run(
+        "in",
+        functools.partial(in_kernel, pieces),
+        [hidden, shape(pieces * quarter, width, dtype=F32), shape(pieces * quarter, width)],
+        (slope, *aggs, *cots, wout, *wouts),
+    )
+    got_in = swap(give_in, "node", 2)
+    own_out, keep, send = run(
+        "own",
+        functools.partial(own_kernel, pieces),
+        [shape(half, width, dtype=F32), pair, pair],
+        (act, *cots, grad_pre, win, *wins),
+    )
+    got = swap(send, "node", 1)
+    turned = run("turn", turn_kernel, shape(*tile_values.shape[1:]), (tile_values,))
+
+    mine = shape(quarter, width, dtype=F32)
+    mine_out, give_out = run(
+        "split",
+        functools.partial(split_kernel, pieces),
+        [mine, shape(quarter, width)],
+        (own_out, *got_out),
+    )
+    last_out = swap(give_out, "node", 2)
+    mine_in, *gives = run(
+        "middle",
+        functools.partial(middle_kernel, pieces),
+        [mine] + [shape(quarter, width)] * far,
+        (keep_in, got_in),
+    )
+    last_in = [swap(give, "rep", s) for give, s in zip(gives, shards)]
+
+    other = run("other", add_rows_kernel, shape(rows, width), (keep, got))
+    last = swap(other, "rep", 1)
+
+    sum_out = total("sum_out", mine_out, last_out)
+    across_out = swap(sum_out, "node", 4) if groups == 2 else None
+    low, high, own = run(
+        "tiles",
+        tiles_kernel,
+        [shape(rows, width)] * 2 + [shape(rows, width, dtype=F32)],
+        (keep, got, last, turned, tile_cols, tile_count, cotangent),
+        specs=[VMEM] * 4 + [SMEM] * 2 + [VMEM],
+        scratch=[pltpu.VMEM((3, rows, width), F32)],
+    )
+    from_next = shift(low, "node", -1)
+    from_prev = shift(high, "node", 1)
+    sum_in = total("sum_in", mine_in, *last_in)
+    across_in = swap(sum_in, "node", 4) if groups == 2 else None
+
+    def spread(name, piece, across):
+        whole = total(name, piece, across) if groups == 2 else over_groups(piece)
+        return whole, swap(whole, "node", 2)
+
+    whole_out, z_out = spread("add_out", sum_out, across_out)
+    whole_in, z_in = spread("add_in", sum_in, across_in)
+
+    def quarters(whole, z_piece):
+        return whole, swap(whole, "node", 1), z_piece, swap(z_piece, "node", 1)
+
     return call(
-        "finish", functools.partial(finish_kernel, factor),
+        "finish",
+        functools.partial(finish_kernel, factor),
         [shape(rows, width), shape(width, 2 * half, dtype=F32), shape(2 * half, width, dtype=F32)],
-        (v['own'], v['next'], v['prev'], *quarters('in'), *quarters('out')),
-        tuple(token[1:]),
+        (own, from_next, from_prev, *quarters(whole_in, z_in), *quarters(whole_out, z_out)),
     )
 
 

time: 60.8 us -> 60.4 us (level)
  waiting for transfers between devices: 24.6 us -> 26.3 us
  local copies, waits for them, and re-layouts: 1.98 us -> 1.02 us
  starting transfers between devices: 23.6 us -> 22.7 us
    ppermute x21, waiting for transfers between devices: 22.8 us -> 26.3 us  [swap(): return lax.ppermute(block, axis, [(i, i ^ mask) for i in range(count)])]
    ppermute x2, starting transfers between devices: 3.01 us -> 0.95 us  [shift(): lax.ppermute(block, axis, [(i, (i + step) % count) for i in range(count)])]
    ppermute x2, waiting for transfers between devices: 1.84 us -> 0.01 us  [shift(): lax.ppermute(block, axis, [(i, (i + step) % count) for i in range(count)])]
    ppermute x21, starting transfers between devices: 20.6 us -> 21.7 us  [swap(): return lax.ppermute(block, axis, [(i, i ^ mask) for i in range(count)])]
    unnamed x10, local copies, waits for them, and re-layouts: 0.99 us -> 0.03 us
where the time goes in v5:
time: 60.4 us; the launch traced here: 60.3 us
  waiting for transfers between devices  26.3 us (44%)
  starting transfers between devices  22.7 us (38%)
  Pallas kernels  8.86 us (15%)
  between operations  1.5 us (2%)
  local copies, waits for them, and re-layouts  1.02 us (2%)
    ppermute x21, waiting for transfers between devices, swap(): return lax.ppermute(block, axis, [(i, i ^ mask) for i in range(count)])  26.3 us
    ppermute x21, starting transfers between devices, swap(): return lax.ppermute(block, axis, [(i, i ^ mask) for i in range(count)])  21.7 us
    pallas_call x17, Pallas kernels, call(): pl.pallas_call(kernel, out_shape=outs, in_specs=(specs or [VMEM] * len(ar...  8.86 us
  transfers between devices with their start and end apart: 23, of which 11 were waited for; matrix products, arithmetic and copies ran while one was open for 2% of the time, Pallas kernels for 10%

profile of v5, /device:TPU:0, one launch (start us, length us, event | category | flops | bytes accessed | tf_op | source)
XLA Modules:
  0.0 60.3 jit_solution(6814086229153753484)
XLA Ops:
  0.6 3.0 %collective-permute-start = (bf16[256,512]{1,0:T(8,128)(2,1)}, bf16[256,512]{1,0:T(8,128)(2,1)S(1)}, u32[]{:S(2)}, u32[]{:S(2)}) collective-permute-start(bf16[256,512]{1,0:T(8,128)(2,1)} %refs_1_.4), channel_id=1, source_target_pairs={{0,1},{1,0},{2,3},{3,2},{4,5},{5,4},{6,7},{7,6},{8,9},{9,8},{10,11... | collective-permute-start | bytes 786440 | tf_op jit(solution)/shard_map/ppermute | solution.py:39
  3.7 1.6 %collective-permute-start.2 = (bf16[512,256]{1,0:T(8,128)(2,1)S(1)}, bf16[512,256]{1,0:T(8,128)(2,1)S(1)}, u32[]{:S(2)}, u32[]{:S(2)}) collective-permute-start(bf16[512,256]{1,0:T(8,128)(2,1)S(1)} %constant_dynamic-slice_fusion.1.refs_3_.refs_5_), channel_id=1, source_target_pairs={{0,2},{1,3},{2,0},{3,1},{4,6},{5,7},{6,4},{7,5},{8,10},{9,11},{10,... | collective-permute-start | bytes 786440 | tf_op jit(solution)/shard_map/ppermute | solution.py:39
  5.3 1.0 %collective-permute-start.3 = (bf16[256,512]{1,0:T(8,128)(2,1)S(1)}, bf16[256,512]{1,0:T(8,128)(2,1)S(1)}, u32[]{:S(2)}, u32[]{:S(2)}) collective-permute-start(bf16[256,512]{1,0:T(8,128)(2,1)S(1)} %copy-done.2), channel_id=1, source_target_pairs={{0,1},{1,0},{2,3},{3,2},{4,5},{5,4},{6,7},{7,6},{8,9},{9,8},{10,11... | collective-permute-start | bytes 786440 | tf_op jit(solution)/shard_map/ppermute | solution.py:39
  6.2 1.0 %constant_dynamic-slice_fusion.refs_7_ = bf16[256,512]{1,0:T(8,128)(2,1)S(1)} fusion(bf16[512,512]{1,0:T(8,128)(2,1)} %param.10, s32[]{:T(128)S(6)} %select_n.4), kind=kLoop, calls=%fused_computation | loop fusion | bytes 524292 | tf_op jit(solution)/shard_map/dynamic_slice | solution.py:266
  7.2 0.9 %collective-permute-start.5 = (bf16[256,512]{1,0:T(8,128)(2,1)S(1)}, bf16[256,512]{1,0:T(8,128)(2,1)S(1)}, u32[]{:S(2)}, u32[]{:S(2)}) collective-permute-start(bf16[256,512]{1,0:T(8,128)(2,1)S(1)} %constant_dynamic-slice_fusion.refs_7_), channel_id=1, source_target_pairs={{0,2},{1,3},{2,0},{3,1},{4,6},{5,7},{6,4},{7,5},{8,10},{9,11},{10,... | collective-permute-start | bytes 786440 | tf_op jit(solution)/shard_map/ppermute | solution.py:39
  8.8 2.2 %collective-permute-done.far_ref.refs_1_.refs_2_ = bf16[256,512]{1,0:T(8,128)(2,1)S(1)} collective-permute-done((bf16[256,512]{1,0:T(8,128)(2,1)}, bf16[256,512]{1,0:T(8,128)(2,1)S(1)}, u32[]{:S(2)}, u32[]{:S(2)}) %collective-permute-start) | collective-permute-done | bytes 262176 | tf_op jit(solution)/shard_map/ppermute | solution.py:39
  11.1 1.9 %collective-permute-done.2.refs_1_.refs_4_.refs_6_ = bf16[512,256]{1,0:T(8,128)(2,1)S(1)} collective-permute-done((bf16[512,256]{1,0:T(8,128)(2,1)S(1)}, bf16[512,256]{1,0:T(8,128)(2,1)S(1)}, u32[]{:S(2)}, u32[]{:S(2)}) %collective-permute-start.2) | collective-permute-done | bytes 262176 | tf_op jit(solution)/shard_map/ppermute | solution.py:39
  13.0 2.8 %collective-permute-done.3.far_ref.refs_2_.refs_5_ = bf16[256,512]{1,0:T(8,128)(2,1)S(1)} collective-permute-done((bf16[256,512]{1,0:T(8,128)(2,1)S(1)}, bf16[256,512]{1,0:T(8,128)(2,1)S(1)}, u32[]{:S(2)}, u32[]{:S(2)}) %collective-permute-start.3) | collective-permute-done | bytes 262176 | tf_op jit(solution)/shard_map/ppermute | solution.py:39
  15.9 1.2 %collective-permute-done.5.refs_8_ = bf16[256,512]{1,0:T(8,128)(2,1)S(1)} collective-permute-done((bf16[256,512]{1,0:T(8,128)(2,1)S(1)}, bf16[256,512]{1,0:T(8,128)(2,1)S(1)}, u32[]{:S(2)}, u32[]{:S(2)}) %collective-permute-start.5) | collective-permute-done | bytes 262176 | tf_op jit(solution)/shard_map/ppermute | solution.py:39
  17.2 1.4 %forward.1 = (bf16[4,512,256]{2,1,0:T(8,128)(2,1)S(1)}, bf16[4,512,256]{2,1,0:T(8,128)(2,1)S(1)}) custom-call(bf16[256,512]{1,0:T(8,128)(2,1)S(1)} %copy-done.1, bf16[256,512]{1,0:T(8,128)(2,1)S(1)} %collective-permute-done.far_ref.refs_1_.refs_2_, bf16[2,256,512]{2,1,0:T(8,128)(2,1)S(1)} %collective-permute-done.1.refs_2_.refs_3_, ...), custom_call_target="tpu_custom_call" | custom-call | flops 1000000000 | tf_op jit(solution)/shard_map/forward/pallas_call | solution.py:49
  18.6 0.4 out.1.refs_9_
  19.1 1.6 %collective-permute-start.9 = (bf16[256,512]{1,0:T(8,128)(2,1)S(1)}, bf16[256,512]{1,0:T(8,128)(2,1)S(1)}, u32[]{:S(2)}, u32[]{:S(2)}) collective-permute-start(bf16[256,512]{1,0:T(8,128)(2,1)S(1)} %out.1.refs_9_), channel_id=1, source_target_pairs={{0,2},{1,3},{2,0},{3,1},{4,6},{5,7},{6,4},{7,5},{8,10},{9,11},{10,... | collective-permute-start | bytes 786440 | tf_op jit(solution)/shard_map/ppermute | solution.py:39
  20.7 1.5 %in.1 = (bf16[4,512,256]{2,1,0:T(8,128)(2,1)S(1)}, f32[256,512]{1,0:T(8,128)S(1)}, bf16[256,512]{1,0:T(8,128)(2,1)S(1)}) custom-call(bf16[4,512,256]{2,1,0:T(8,128)(2,1)S(1)} %get-tuple-element.19.refs_0_, bf16[256,512]{1,0:T(8,128)(2,1)S(1)} %copy-done.1, bf16[256,512]{1,0:T(8,128)(2,1)S(1)} %collective-permute-done.far_ref.refs_1_.refs_2_, ...), custom_call_target="tpu_custom_call" | custom-call | flops 100000000 | tf_op jit(solution)/shard_map/in/pallas_call | solution.py:49
  22.2 1.6 %collective-permute-start.8 = (bf16[256,512]{1,0:T(8,128)(2,1)S(1)}, bf16[256,512]{1,0:T(8,128)(2,1)S(1)}, u32[]{:S(2)}, u32[]{:S(2)}) collective-permute-start(bf16[256,512]{1,0:T(8,128)(2,1)S(1)} %get-tuple-element.24), channel_id=1, source_target_pairs={{0,8},{4,12},{8,0},{12,4},{16,24},{20,28},{24,16},{28,20},{1,9},{5... | collective-permute-start | bytes 786440 | tf_op jit(solution)/shard_map/ppermute | solution.py:39
  23.9 1.0 %own.1 = (f32[256,512]{1,0:T(8,128)S(1)}, bf16[2,256,512]{2,1,0:T(8,128)(2,1)S(1)}, bf16[2,256,512]{2,1,0:T(8,128)(2,1)S(1)}) custom-call(bf16[4,512,256]{2,1,0:T(8,128)(2,1)S(1)} %get-tuple-element.18.refs_0_.refs_4_, bf16[256,512]{1,0:T(8,128)(2,1)S(1)} %copy-done.2, bf16[256,512]{1,0:T(8,128)(2,1)S(1)} %collective-permute-done.3.far_ref.refs_2_.refs_5_, ...), custom_call_target="tpu_custom_call" | custom-call | flops 3000000000 | tf_op jit(solution)/shard_map/own/pallas_call | solution.py:49
  25.1 2.7 %collective-permute-done.9.refs_1_ = bf16[256,512]{1,0:T(8,128)(2,1)S(1)} collective-permute-done((bf16[256,512]{1,0:T(8,128)(2,1)S(1)}, bf16[256,512]{1,0:T(8,128)(2,1)S(1)}, u32[]{:S(2)}, u32[]{:S(2)}) %collective-permute-start.9) | collective-permute-done | bytes 262176 | tf_op jit(solution)/shard_map/ppermute | solution.py:39
  27.9 1.6 %collective-permute-start.11 = (bf16[128,512]{1,0:T(8,128)(2,1)S(1)}, bf16[128,512]{1,0:T(8,128)(2,1)S(1)}, u32[]{:S(2)}, u32[]{:S(2)}) collective-permute-start(bf16[128,512]{1,0:T(8,128)(2,1)S(1)} %get-tuple-element.28), channel_id=1, source_target_pairs={{0,8},{4,12},{8,0},{12,4},{16,24},{20,28},{24,16},{28,20},{1,9},{5... | collective-permute-start | bytes 393224 | tf_op jit(solution)/shard_map/ppermute | solution.py:39
  29.6 1.5 %collective-permute-done.8.refs_1_ = bf16[256,512]{1,0:T(8,128)(2,1)S(1)} collective-permute-done((bf16[256,512]{1,0:T(8,128)(2,1)S(1)}, bf16[256,512]{1,0:T(8,128)(2,1)S(1)}, u32[]{:S(2)}, u32[]{:S(2)}) %collective-permute-start.8) | collective-permute-done | bytes 262176 | tf_op jit(solution)/shard_map/ppermute | solution.py:39
  31.4 1.3 %collective-permute-start.10 = (bf16[256,512]{1,0:T(8,128)(2,1)S(1)}, bf16[256,512]{1,0:T(8,128)(2,1)S(1)}, u32[]{:S(2)}, u32[]{:S(2)}) collective-permute-start(bf16[256,512]{1,0:T(8,128)(2,1)S(1)} %other.1.refs_2_), channel_id=1, source_target_pairs={{0,1},{1,0},{2,3},{3,2},{4,5},{5,4},{6,7},{7,6},{8,9},{9,8},{10,11... | collective-permute-start | bytes 786440 | tf_op jit(solution)/shard_map/ppermute | solution.py:39
  32.7 0.8 %collective-permute-done.11.refs_1_ = bf16[128,512]{1,0:T(8,128)(2,1)S(1)} collective-permute-done((bf16[128,512]{1,0:T(8,128)(2,1)S(1)}, bf16[128,512]{1,0:T(8,128)(2,1)S(1)}, u32[]{:S(2)}, u32[]{:S(2)}) %collective-permute-start.11) | collective-permute-done | bytes 131104 | tf_op jit(solution)/shard_map/ppermute | solution.py:39
  33.6 2.6 %collective-permute-start.16 = (bf16[128,512]{1,0:T(8,128)(2,1)S(1)}, bf16[128,512]{1,0:T(8,128)(2,1)S(1)}, u32[]{:S(2)}, u32[]{:S(2)}) collective-permute-start(bf16[128,512]{1,0:T(8,128)(2,1)S(1)} %sum_out.1.refs_0_), channel_id=1, source_target_pairs={{0,16},{4,20},{8,24},{12,28},{16,0},{20,4},{24,8},{28,12},{1,17},{... | collective-permute-start | bytes 393224 | tf_op jit(solution)/shard_map/ppermute | solution.py:39
  36.2 2.6 %collective-permute-done.10.last_ref = bf16[256,512]{1,0:T(8,128)(2,1)S(1)} collective-permute-done((bf16[256,512]{1,0:T(8,128)(2,1)S(1)}, bf16[256,512]{1,0:T(8,128)(2,1)S(1)}, u32[]{:S(2)}, u32[]{:S(2)}) %collective-permute-start.10) | collective-permute-done | bytes 262176 | tf_op jit(solution)/shard_map/ppermute | solution.py:39
  38.8 1.8 %tiles.1 = (bf16[256,512]{1,0:T(8,128)(2,1)S(1)}, bf16[256,512]{1,0:T(8,128)(2,1)S(1)}, f32[256,512]{1,0:T(8,128)S(1)}) custom-call(bf16[2,256,512]{2,1,0:T(8,128)(2,1)S(1)} %get-tuple-element.21.keep_ref, bf16[2,256,512]{2,1,0:T(8,128)(2,1)S(1)} %collective-permute-done.7.got_ref, bf16[256,512]{1,0:T(8,128)(2,1)S(1)} %collective-permute-done.10.last_ref, ...), custom_call_target="tpu_custom_call" | custom-call | flops 100000000 | tf_op jit(solution)/shard_map/tiles/pallas_call | solution.py:49
  40.6 2.0 %collective-permute-start.15 = (bf16[128,512]{1,0:T(8,128)(2,1)S(1)}, bf16[128,512]{1,0:T(8,128)(2,1)S(1)}, u32[]{:S(2)}, u32[]{:S(2)}) collective-permute-start(bf16[128,512]{1,0:T(8,128)(2,1)S(1)} %sum_in.1.refs_2_.refs_0_), channel_id=1, source_target_pairs={{0,16},{4,20},{8,24},{12,28},{16,0},{20,4},{24,8},{28,12},{1,17},{... | collective-permute-start | bytes 393224 | tf_op jit(solution)/shard_map/ppermute | solution.py:39
  42.7 2.1 %collective-permute-start.21 = (bf16[128,512]{1,0:T(8,128)(2,1)S(1)}, bf16[128,512]{1,0:T(8,128)(2,1)S(1)}, u32[]{:S(2)}, u32[]{:S(2)}) collective-permute-start(bf16[128,512]{1,0:T(8,128)(2,1)S(1)} %add_out.1.refs_2_.refs_7_), channel_id=1, source_target_pairs={{0,8},{4,12},{8,0},{12,4},{16,24},{20,28},{24,16},{28,20},{1,9},{5... | collective-permute-start | bytes 393224 | tf_op jit(solution)/shard_map/ppermute | solution.py:39
  44.8 1.0 %collective-permute-start.12 = (bf16[256,512]{1,0:T(8,128)(2,1)S(1)}, bf16[256,512]{1,0:T(8,128)(2,1)S(1)}, u32[]{:S(2)}, u32[]{:S(2)}) collective-permute-start(bf16[256,512]{1,0:T(8,128)(2,1)S(1)} %get-tuple-element.30.refs_2_), channel_id=1, source_target_pairs={{0,28},{4,0},{8,4},{12,8},{16,12},{20,16},{24,20},{28,24},{1,29},{... | collective-permute-start | bytes 786440 | tf_op jit(solution)/shard_map/ppermute | solution.py:44
  45.7 2.0 %collective-permute-done.15.refs_1_ = bf16[128,512]{1,0:T(8,128)(2,1)S(1)} collective-permute-done((bf16[128,512]{1,0:T(8,128)(2,1)S(1)}, bf16[128,512]{1,0:T(8,128)(2,1)S(1)}, u32[]{:S(2)}, u32[]{:S(2)}) %collective-permute-start.15) | collective-permute-done | bytes 131104 | tf_op jit(solution)/shard_map/ppermute | solution.py:39
  47.7 1.4 %collective-permute-start.18 = (bf16[128,512]{1,0:T(8,128)(2,1)S(1)}, bf16[128,512]{1,0:T(8,128)(2,1)S(1)}, u32[]{:S(2)}, u32[]{:S(2)}) collective-permute-start(bf16[128,512]{1,0:T(8,128)(2,1)S(1)} %add_in.1.refs_3_), channel_id=1, source_target_pairs={{0,8},{4,12},{8,0},{12,4},{16,24},{20,28},{24,16},{28,20},{1,9},{5... | collective-permute-start | bytes 393224 | tf_op jit(solution)/shard_map/ppermute | solution.py:39
  49.1 0.5 collective-permute-start.17
  49.6 7.2 %collective-permute-done.18.refs_5_ = bf16[128,512]{1,0:T(8,128)(2,1)S(1)} collective-permute-done((bf16[128,512]{1,0:T(8,128)(2,1)S(1)}, bf16[128,512]{1,0:T(8,128)(2,1)S(1)}, u32[]{:S(2)}, u32[]{:S(2)}) %collective-permute-start.18) | collective-permute-done | bytes 131104 | tf_op jit(solution)/shard_map/ppermute | solution.py:39
  56.9 1.3 %collective-permute-done.19.refs_6_ = bf16[128,512]{1,0:T(8,128)(2,1)S(1)} collective-permute-done((bf16[128,512]{1,0:T(8,128)(2,1)S(1)}, bf16[128,512]{1,0:T(8,128)(2,1)S(1)}, u32[]{:S(2)}, u32[]{:S(2)}) %collective-permute-start.19) | collective-permute-done | bytes 131104 | tf_op jit(solution)/shard_map/ppermute | solution.py:39
  58.2 2.1 %finish.1 = (bf16[256,512]{1,0:T(8,128)(2,1)}, f32[512,512]{1,0:T(8,128)}, f32[512,512]{1,0:T(8,128)}) custom-call(f32[256,512]{1,0:T(8,128)S(1)} %get-tuple-element.29.refs_0_, bf16[256,512]{1,0:T(8,128)(2,1)S(1)} %collective-permute-done.12.refs_1_, bf16[256,512]{1,0:T(8,128)(2,1)S(1)} %collective-permute-done.13.refs_2_, ...), custom_call_target="tpu_custom_call" | custom-call | flops 100000000 | tf_op jit(solution)/shard_map/finish/pallas_call | solution.py:49
  (44 shorter events, 1.1 us)
Async XLA Ops:
  0.6 3.0 %copy-start = (bf16[512,512]{1,0:T(8,128)(2,1)S(1)}, bf16[512,512]{1,0:T(8,128)(2,1)}, u32[]{:S(2)}) copy-start(bf16[512,512]{1,0:T(8,128)(2,1)} %param.9) | copy-start | bytes 1572868
  0.6 10.4 %collective-permute-start = (bf16[256,512]{1,0:T(8,128)(2,1)}, bf16[256,512]{1,0:T(8,128)(2,1)S(1)}, u32[]{:S(2)}, u32[]{:S(2)}) collective-permute-start(bf16[256,512]{1,0:T(8,128)(2,1)} %refs_1_.4), channel_id=1, source_target_pairs={{0,1},{1,0},{2,3},{3,2},{4,5},{5,4},{6,7},{7,6},{8,9},{9,8},{10,11... | collective-permute-start | bytes 786440 | tf_op jit(solution)/shard_map/ppermute | solution.py:39
  3.7 1.6 %copy-start.2 = (bf16[256,512]{1,0:T(8,128)(2,1)S(1)}, bf16[256,512]{1,0:T(8,128)(2,1)}, u32[]{:S(2)}) copy-start(bf16[256,512]{1,0:T(8,128)(2,1)} %cot_ref.1) | copy-start | bytes 786436
  3.7 7.3 %copy-start.1 = (bf16[256,512]{1,0:T(8,128)(2,1)S(1)}, bf16[256,512]{1,0:T(8,128)(2,1)}, u32[]{:S(2)}) copy-start(bf16[256,512]{1,0:T(8,128)(2,1)} %refs_1_.4) | copy-start | bytes 786436
  3.7 9.3 %collective-permute-start.2 = (bf16[512,256]{1,0:T(8,128)(2,1)S(1)}, bf16[512,256]{1,0:T(8,128)(2,1)S(1)}, u32[]{:S(2)}, u32[]{:S(2)}) collective-permute-start(bf16[512,256]{1,0:T(8,128)(2,1)S(1)} %constant_dynamic-slice_fusion.1.refs_3_.refs_5_), channel_id=1, source_target_pairs={{0,2},{1,3},{2,0},{3,1},{4,6},{5,7},{6,4},{7,5},{8,10},{9,11},{10,... | collective-permute-start | bytes 786440 | tf_op jit(solution)/shard_map/ppermute | solution.py:39
  5.3 10.5 %collective-permute-start.3 = (bf16[256,512]{1,0:T(8,128)(2,1)S(1)}, bf16[256,512]{1,0:T(8,128)(2,1)S(1)}, u32[]{:S(2)}, u32[]{:S(2)}) collective-permute-start(bf16[256,512]{1,0:T(8,128)(2,1)S(1)} %copy-done.2), channel_id=1, source_target_pairs={{0,1},{1,0},{2,3},{3,2},{4,5},{5,4},{6,7},{7,6},{8,9},{9,8},{10,11... | collective-permute-start | bytes 786440 | tf_op jit(solution)/shard_map/ppermute | solution.py:39
  7.2 9.9 %collective-permute-start.5 = (bf16[256,512]{1,0:T(8,128)(2,1)S(1)}, bf16[256,512]{1,0:T(8,128)(2,1)S(1)}, u32[]{:S(2)}, u32[]{:S(2)}) collective-permute-start(bf16[256,512]{1,0:T(8,128)(2,1)S(1)} %constant_dynamic-slice_fusion.refs_7_), channel_id=1, source_target_pairs={{0,2},{1,3},{2,0},{3,1},{4,6},{5,7},{6,4},{7,5},{8,10},{9,11},{10,... | collective-permute-start | bytes 786440 | tf_op jit(solution)/shard_map/ppermute | solution.py:39
  11.0 6.1 %collective-permute-start.1 = (bf16[2,256,512]{2,1,0:T(8,128)(2,1)S(1)}, bf16[2,256,512]{2,1,0:T(8,128)(2,1)S(1)}, u32[]{:S(2)}, u32[]{:S(2)}) collective-permute-start(bf16[2,256,512]{2,1,0:T(8,128)(2,1)S(1)} %both_agg.1.refs_0_), channel_id=1, source_target_pairs={{0,4},{4,0},{8,12},{12,8},{16,20},{20,16},{24,28},{28,24},{1,5},{5... | collective-permute-start | bytes 1572872 | tf_op jit(solution)/shard_map/ppermute | solution.py:39
  15.8 2.8 %collective-permute-start.4 = (bf16[2,256,512]{2,1,0:T(8,128)(2,1)S(1)}, bf16[2,256,512]{2,1,0:T(8,128)(2,1)S(1)}, u32[]{:S(2)}, u32[]{:S(2)}) collective-permute-start(bf16[2,256,512]{2,1,0:T(8,128)(2,1)S(1)} %both_cot.1.refs_5_), channel_id=1, source_target_pairs={{0,4},{4,0},{8,12},{12,8},{16,20},{20,16},{24,28},{28,24},{1,5},{5... | collective-permute-start | bytes 1572872 | tf_op jit(solution)/shard_map/ppermute | solution.py:39
  17.1 1.5 %collective-permute-start.6 = (bf16[16,512]{1,0:T(8,128)(2,1)S(1)}, bf16[16,512]{1,0:T(8,128)(2,1)S(1)}, u32[]{:S(2)}, u32[]{:S(2)}) collective-permute-start(bf16[16,512]{1,0:T(8,128)(2,1)S(1)} %lift.1), channel_id=1, source_target_pairs={{0,4},{4,0},{8,12},{12,8},{16,20},{20,16},{24,28},{28,24},{1,5},{5... | collective-permute-start | bytes 49160 | tf_op jit(solution)/shard_map/ppermute | solution.py:39
  19.1 8.8 %collective-permute-start.9 = (bf16[256,512]{1,0:T(8,128)(2,1)S(1)}, bf16[256,512]{1,0:T(8,128)(2,1)S(1)}, u32[]{:S(2)}, u32[]{:S(2)}) collective-permute-start(bf16[256,512]{1,0:T(8,128)(2,1)S(1)} %out.1.refs_9_), channel_id=1, source_target_pairs={{0,2},{1,3},{2,0},{3,1},{4,6},{5,7},{6,4},{7,5},{8,10},{9,11},{10,... | collective-permute-start | bytes 786440 | tf_op jit(solution)/shard_map/ppermute | solution.py:39
  22.2 8.8 %collective-permute-start.8 = (bf16[256,512]{1,0:T(8,128)(2,1)S(1)}, bf16[256,512]{1,0:T(8,128)(2,1)S(1)}, u32[]{:S(2)}, u32[]{:S(2)}) collective-permute-start(bf16[256,512]{1,0:T(8,128)(2,1)S(1)} %get-tuple-element.24), channel_id=1, source_target_pairs={{0,8},{4,12},{8,0},{12,4},{16,24},{20,28},{24,16},{28,20},{1,9},{5... | collective-permute-start | bytes 786440 | tf_op jit(solution)/shard_map/ppermute | solution.py:39
  23.9 1.1 %copy-start.3 = (bf16[1,4,256,256]{3,2,1,0:T(8,128)(2,1)S(1)}, bf16[1,4,256,256]{3,2,1,0:T(8,128)(2,1)}, u32[]{:S(2)}) copy-start(bf16[1,4,256,256]{3,2,1,0:T(8,128)(2,1)} %tiles_ref.1) | copy-start | bytes 1572868
  24.9 6.5 %collective-permute-start.7 = (bf16[2,256,512]{2,1,0:T(8,128)(2,1)S(1)}, bf16[2,256,512]{2,1,0:T(8,128)(2,1)S(1)}, u32[]{:S(2)}, u32[]{:S(2)}) collective-permute-start(bf16[2,256,512]{2,1,0:T(8,128)(2,1)S(1)} %get-tuple-element.22), channel_id=1, source_target_pairs={{0,4},{4,0},{8,12},{12,8},{16,20},{20,16},{24,28},{28,24},{1,5},{5... | collective-permute-start | bytes 1572872 | tf_op jit(solution)/shard_map/ppermute | solution.py:39
  27.9 5.6 %collective-permute-start.11 = (bf16[128,512]{1,0:T(8,128)(2,1)S(1)}, bf16[128,512]{1,0:T(8,128)(2,1)S(1)}, u32[]{:S(2)}, u32[]{:S(2)}) collective-permute-start(bf16[128,512]{1,0:T(8,128)(2,1)S(1)} %get-tuple-element.28), channel_id=1, source_target_pairs={{0,8},{4,12},{8,0},{12,4},{16,24},{20,28},{24,16},{28,20},{1,9},{5... | collective-permute-start | bytes 393224 | tf_op jit(solution)/shard_map/ppermute | solution.py:39
  31.1 9.5 %collective-permute-start.14 = (bf16[128,512]{1,0:T(8,128)(2,1)S(1)}, bf16[128,512]{1,0:T(8,128)(2,1)S(1)}, u32[]{:S(2)}, u32[]{:S(2)}) collective-permute-start(bf16[128,512]{1,0:T(8,128)(2,1)S(1)} %get-tuple-element.32), channel_id=1, source_target_pairs={{0,2},{1,3},{2,0},{3,1},{4,6},{5,7},{6,4},{7,5},{8,10},{9,11},{10,... | collective-permute-start | bytes 393224 | tf_op jit(solution)/shard_map/ppermute | solution.py:39
  31.4 7.4 %copy-start.4 = (s32[1,4]{1,0:T(1,128)S(1)}, s32[1,4]{1,0:T(1,128)}, u32[]{:S(2)}) copy-start(s32[1,4]{1,0:T(1,128)} %cols_ref.1) | copy-start | bytes 52
  31.4 7.4 %collective-permute-start.10 = (bf16[256,512]{1,0:T(8,128)(2,1)S(1)}, bf16[256,512]{1,0:T(8,128)(2,1)S(1)}, u32[]{:S(2)}, u32[]{:S(2)}) collective-permute-start(bf16[256,512]{1,0:T(8,128)(2,1)S(1)} %other.1.refs_2_), channel_id=1, source_target_pairs={{0,1},{1,0},{2,3},{3,2},{4,5},{5,4},{6,7},{7,6},{8,9},{9,8},{10,11... | collective-permute-start | bytes 786440 | tf_op jit(solution)/shard_map/ppermute | solution.py:39
  33.6 9.1 %collective-permute-start.16 = (bf16[128,512]{1,0:T(8,128)(2,1)S(1)}, bf16[128,512]{1,0:T(8,128)(2,1)S(1)}, u32[]{:S(2)}, u32[]{:S(2)}) collective-permute-start(bf16[128,512]{1,0:T(8,128)(2,1)S(1)} %sum_out.1.refs_0_), channel_id=1, source_target_pairs={{0,16},{4,20},{8,24},{12,28},{16,0},{20,4},{24,8},{28,12},{1,17},{... | collective-permute-start | bytes 393224 | tf_op jit(solution)/shard_map/ppermute | solution.py:39
  40.6 7.1 %collective-permute-start.15 = (bf16[128,512]{1,0:T(8,128)(2,1)S(1)}, bf16[128,512]{1,0:T(8,128)(2,1)S(1)}, u32[]{:S(2)}, u32[]{:S(2)}) collective-permute-start(bf16[128,512]{1,0:T(8,128)(2,1)S(1)} %sum_in.1.refs_2_.refs_0_), channel_id=1, source_target_pairs={{0,16},{4,20},{8,24},{12,28},{16,0},{20,4},{24,8},{28,12},{1,17},{... | collective-permute-start | bytes 393224 | tf_op jit(solution)/shard_map/ppermute | solution.py:39
  42.7 6.4 %collective-permute-start.21 = (bf16[128,512]{1,0:T(8,128)(2,1)S(1)}, bf16[128,512]{1,0:T(8,128)(2,1)S(1)}, u32[]{:S(2)}, u32[]{:S(2)}) collective-permute-start(bf16[128,512]{1,0:T(8,128)(2,1)S(1)} %add_out.1.refs_2_.refs_7_), channel_id=1, source_target_pairs={{0,8},{4,12},{8,0},{12,4},{16,24},{20,28},{24,16},{28,20},{1,9},{5... | collective-permute-start | bytes 393224 | tf_op jit(solution)/shard_map/ppermute | solution.py:39
  44.8 4.4 %collective-permute-start.20 = (bf16[128,512]{1,0:T(8,128)(2,1)S(1)}, bf16[128,512]{1,0:T(8,128)(2,1)S(1)}, u32[]{:S(2)}, u32[]{:S(2)}) collective-permute-start(bf16[128,512]{1,0:T(8,128)(2,1)S(1)} %add_out.1.refs_2_.refs_7_), channel_id=1, source_target_pairs={{0,4},{4,0},{8,12},{12,8},{16,20},{20,16},{24,28},{28,24},{1,5},{5... | collective-permute-start | bytes 393224 | tf_op jit(solution)/shard_map/ppermute | solution.py:39
  44.8 12.1 %collective-permute-start.12 = (bf16[256,512]{1,0:T(8,128)(2,1)S(1)}, bf16[256,512]{1,0:T(8,128)(2,1)S(1)}, u32[]{:S(2)}, u32[]{:S(2)}) collective-permute-start(bf16[256,512]{1,0:T(8,128)(2,1)S(1)} %get-tuple-element.30.refs_2_), channel_id=1, source_target_pairs={{0,28},{4,0},{8,4},{12,8},{16,12},{20,16},{24,20},{28,24},{1,29},{... | collective-permute-start | bytes 786440 | tf_op jit(solution)/shard_map/ppermute | solution.py:44
  45.7 11.2 %collective-permute-start.13 = (bf16[256,512]{1,0:T(8,128)(2,1)S(1)}, bf16[256,512]{1,0:T(8,128)(2,1)S(1)}, u32[]{:S(2)}, u32[]{:S(2)}) collective-permute-start(bf16[256,512]{1,0:T(8,128)(2,1)S(1)} %get-tuple-element.31), channel_id=1, source_target_pairs={{0,4},{4,8},{8,12},{12,16},{16,20},{20,24},{24,28},{28,0},{1,5},{5... | collective-permute-start | bytes 786440 | tf_op jit(solution)/shard_map/ppermute | solution.py:44
  47.7 9.1 %collective-permute-start.18 = (bf16[128,512]{1,0:T(8,128)(2,1)S(1)}, bf16[128,512]{1,0:T(8,128)(2,1)S(1)}, u32[]{:S(2)}, u32[]{:S(2)}) collective-permute-start(bf16[128,512]{1,0:T(8,128)(2,1)S(1)} %add_in.1.refs_3_), channel_id=1, source_target_pairs={{0,8},{4,12},{8,0},{12,4},{16,24},{20,28},{24,16},{28,20},{1,9},{5... | collective-permute-start | bytes 393224 | tf_op jit(solution)/shard_map/ppermute | solution.py:39
  49.1 7.7 %collective-permute-start.22 = (bf16[128,512]{1,0:T(8,128)(2,1)S(1)}, bf16[128,512]{1,0:T(8,128)(2,1)S(1)}, u32[]{:S(2)}, u32[]{:S(2)}) collective-permute-start(bf16[128,512]{1,0:T(8,128)(2,1)S(1)} %collective-permute-done.21.refs_9_), channel_id=1, source_target_pairs={{0,4},{4,0},{8,12},{12,8},{16,20},{20,16},{24,28},{28,24},{1,5},{5... | collective-permute-start | bytes 393224 | tf_op jit(solution)/shard_map/ppermute | solution.py:39
  49.1 7.7 %collective-permute-start.17 = (bf16[128,512]{1,0:T(8,128)(2,1)S(1)}, bf16[128,512]{1,0:T(8,128)(2,1)S(1)}, u32[]{:S(2)}, u32[]{:S(2)}) collective-permute-start(bf16[128,512]{1,0:T(8,128)(2,1)S(1)} %add_in.1.refs_3_), channel_id=1, source_target_pairs={{0,4},{4,0},{8,12},{12,8},{16,20},{20,16},{24,28},{28,24},{1,5},{5... | collective-permute-start | bytes 393224 | tf_op jit(solution)/shard_map/ppermute | solution.py:39
  56.9 1.3 %collective-permute-start.19 = (bf16[128,512]{1,0:T(8,128)(2,1)S(1)}, bf16[128,512]{1,0:T(8,128)(2,1)S(1)}, u32[]{:S(2)}, u32[]{:S(2)}) collective-permute-start(bf16[128,512]{1,0:T(8,128)(2,1)S(1)} %collective-permute-done.18.refs_5_), channel_id=1, source_target_pairs={{0,4},{4,0},{8,12},{12,8},{16,20},{20,16},{24,28},{28,24},{1,5},{5... | collective-permute-start | bytes 393224 | tf_op jit(solution)/shard_map/ppermute | solution.py:39

commit v6 on v5

--- a/solution.py
+++ b/solution.py
@@ -44,13 +44,13 @@
     return lax.ppermute(block, axis, [(i, (i + step) % count) for i in range(count)])
 
 
-def call(name, kernel, outs, args, after=(), specs=None, scratch=()):
+def call(name, kernel, outs, args, after=(), specs=None, scratch=(), space=VMEM):
     single = not isinstance(outs, (list, tuple))
     return pl.pallas_call(
         kernel,
         out_shape=outs,
         in_specs=(specs or [VMEM] * len(args)) + [ANY] * len(after),
-        out_specs=VMEM if single else [VMEM] * len(outs),
+        out_specs=space if single else [space] * len(outs),
         scratch_shapes=list(scratch),
         compiler_params=pltpu.CompilerParams(vmem_limit_bytes=40 * 1024 * 1024),
         cost_estimate=pl.CostEstimate(
@@ -206,22 +206,39 @@
 
 def finish_kernel(factor, *refs):
     (own_ref, next_ref, prev_ref), ins, outs = refs[:3], refs[3:7], refs[7:11]
-    nodes_ref, grad_in_ref, grad_out_ref = refs[-3:]
+    targets, (nodes_here, in_here, out_here), sems = refs[-7:-4], refs[-4:-1], refs[-1]
     quarter = ins[0].shape[0]
     me = lax.rem(lax.axis_index("node"), 4)
-    nodes_ref[...] = (
+    copies = [
+        pltpu.make_async_copy(source, target, sems.at[i])
+        for i, (source, target) in enumerate(zip((nodes_here, in_here, out_here), targets))
+    ]
+
+    def placed(blocks, store):
+        for j in range(4):
+            for device in range(4):
+
+                @pl.when(me == device)
+                def _(block=blocks[j], owner=device ^ j):
+                    first = (owner % 2 * 2 + owner // 2) * quarter
+                    store(slice(first, first + quarter), block)
+
+    def store_out(where, block):
+        out_here[where, :] = block
+
+    def store_in(where, block):
+        in_here[:, where] = block
+
+    placed([ref[...].astype(F32) * factor for ref in outs], store_out)
+    copies[2].start()
+    nodes_here[...] = (
         own_ref[...] + next_ref[...].astype(F32) + prev_ref[...].astype(F32)
     ).astype(BF16)
-    for j in range(4):
-        out_block = outs[j][...].astype(F32) * factor
-        in_block = ins[j][...].astype(F32).T * factor
-        for device in range(4):
-
-            @pl.when(me == device)
-            def _(in_block=in_block, out_block=out_block, owner=device ^ j):
-                first = (owner % 2 * 2 + owner // 2) * quarter
-                grad_out_ref[first : first + quarter, :] = out_block
-                grad_in_ref[:, first : first + quarter] = in_block
+    copies[0].start()
+    placed([ref[...].T.astype(F32) * factor for ref in ins], store_in)
+    copies[1].start()
+    for copy in copies:
+        copy.wait()
 
 
 def over_groups(piece):
@@ -348,11 +365,18 @@
     def quarters(whole, z_piece):
         return whole, swap(whole, "node", 1), z_piece, swap(z_piece, "node", 1)
 
+    results = (
+        shape(rows, width),
+        shape(width, 2 * half, dtype=F32),
+        shape(2 * half, width, dtype=F32),
+    )
     return call(
         "finish",
         functools.partial(finish_kernel, factor),
-        [shape(rows, width), shape(width, 2 * half, dtype=F32), shape(2 * half, width, dtype=F32)],
+        results,
         (own, from_next, from_prev, *quarters(whole_in, z_in), *quarters(whole_out, z_out)),
+        scratch=[pltpu.VMEM(r.shape, r.dtype) for r in results] + [pltpu.SemaphoreType.DMA((3,))],
+        space=ANY,
     )
 
 

time: 60.4 us -> 59.8 us (0.990)
  transfers between devices with their start and end apart: 23 -> 23, of which waited for: 11 -> 11; matrix products, arithmetic and copies ran while one was open for 2% -> 2% of each run, Pallas kernels for 10% -> 11%
where the time goes in v6:
time: 59.8 us; the launch traced here: 60 us
  waiting for transfers between devices  25.9 us (43%)
  starting transfers between devices  23.1 us (39%)
  Pallas kernels  8.39 us (14%)
  between operations  1.5 us (3%)
  local copies, waits for them, and re-layouts  1.02 us (2%)
    ppermute x21, waiting for transfers between devices, swap(): return lax.ppermute(block, axis, [(i, i ^ mask) for i in range(count)])  25.9 us
    ppermute x21, starting transfers between devices, swap(): return lax.ppermute(block, axis, [(i, i ^ mask) for i in range(count)])  22 us
    pallas_call x17, Pallas kernels, call(): pl.pallas_call(kernel, out_shape=outs, in_specs=(specs or [VMEM] * len(ar...  8.39 us
  transfers between devices with their start and end apart: 23, of which 11 were waited for; matrix products, arithmetic and copies ran while one was open for 2% of the time, Pallas kernels for 11%

profile of v6, /device:TPU:0, one launch (start us, length us, event | category | flops | bytes accessed | tf_op | source)
XLA Modules:
  0.0 60.0 jit_solution(11059801802452772142)
XLA Ops:
  0.6 3.0 %collective-permute-start = (bf16[256,512]{1,0:T(8,128)(2,1)}, bf16[256,512]{1,0:T(8,128)(2,1)S(1)}, u32[]{:S(2)}, u32[]{:S(2)}) collective-permute-start(bf16[256,512]{1,0:T(8,128)(2,1)} %refs_1_.4), channel_id=1, source_target_pairs={{0,1},{1,0},{2,3},{3,2},{4,5},{5,4},{6,7},{7,6},{8,9},{9,8},{10,11... | collective-permute-start | bytes 786440 | tf_op jit(solution)/shard_map/ppermute | solution.py:39
  3.7 1.6 %collective-permute-start.2 = (bf16[512,256]{1,0:T(8,128)(2,1)S(1)}, bf16[512,256]{1,0:T(8,128)(2,1)S(1)}, u32[]{:S(2)}, u32[]{:S(2)}) collective-permute-start(bf16[512,256]{1,0:T(8,128)(2,1)S(1)} %constant_dynamic-slice_fusion.1.refs_3_.refs_5_), channel_id=1, source_target_pairs={{0,2},{1,3},{2,0},{3,1},{4,6},{5,7},{6,4},{7,5},{8,10},{9,11},{10,... | collective-permute-start | bytes 786440 | tf_op jit(solution)/shard_map/ppermute | solution.py:39
  5.3 1.0 %collective-permute-start.3 = (bf16[256,512]{1,0:T(8,128)(2,1)S(1)}, bf16[256,512]{1,0:T(8,128)(2,1)S(1)}, u32[]{:S(2)}, u32[]{:S(2)}) collective-permute-start(bf16[256,512]{1,0:T(8,128)(2,1)S(1)} %copy-done.2), channel_id=1, source_target_pairs={{0,1},{1,0},{2,3},{3,2},{4,5},{5,4},{6,7},{7,6},{8,9},{9,8},{10,11... | collective-permute-start | bytes 786440 | tf_op jit(solution)/shard_map/ppermute | solution.py:39
  6.2 1.0 %constant_dynamic-slice_fusion.refs_7_ = bf16[256,512]{1,0:T(8,128)(2,1)S(1)} fusion(bf16[512,512]{1,0:T(8,128)(2,1)} %param.10, s32[]{:T(128)S(6)} %select_n.4), kind=kLoop, calls=%fused_computation | loop fusion | bytes 524292 | tf_op jit(solution)/shard_map/dynamic_slice | solution.py:283
  7.2 0.9 %collective-permute-start.5 = (bf16[256,512]{1,0:T(8,128)(2,1)S(1)}, bf16[256,512]{1,0:T(8,128)(2,1)S(1)}, u32[]{:S(2)}, u32[]{:S(2)}) collective-permute-start(bf16[256,512]{1,0:T(8,128)(2,1)S(1)} %constant_dynamic-slice_fusion.refs_7_), channel_id=1, source_target_pairs={{0,2},{1,3},{2,0},{3,1},{4,6},{5,7},{6,4},{7,5},{8,10},{9,11},{10,... | collective-permute-start | bytes 786440 | tf_op jit(solution)/shard_map/ppermute | solution.py:39
  8.8 2.2 %collective-permute-done.far_ref.refs_1_.refs_2_ = bf16[256,512]{1,0:T(8,128)(2,1)S(1)} collective-permute-done((bf16[256,512]{1,0:T(8,128)(2,1)}, bf16[256,512]{1,0:T(8,128)(2,1)S(1)}, u32[]{:S(2)}, u32[]{:S(2)}) %collective-permute-start) | collective-permute-done | bytes 262176 | tf_op jit(solution)/shard_map/ppermute | solution.py:39
  11.1 1.9 %collective-permute-done.2.refs_1_.refs_4_.refs_6_ = bf16[512,256]{1,0:T(8,128)(2,1)S(1)} collective-permute-done((bf16[512,256]{1,0:T(8,128)(2,1)S(1)}, bf16[512,256]{1,0:T(8,128)(2,1)S(1)}, u32[]{:S(2)}, u32[]{:S(2)}) %collective-permute-start.2) | collective-permute-done | bytes 262176 | tf_op jit(solution)/shard_map/ppermute | solution.py:39
  13.0 2.8 %collective-permute-done.3.far_ref.refs_2_.refs_5_ = bf16[256,512]{1,0:T(8,128)(2,1)S(1)} collective-permute-done((bf16[256,512]{1,0:T(8,128)(2,1)S(1)}, bf16[256,512]{1,0:T(8,128)(2,1)S(1)}, u32[]{:S(2)}, u32[]{:S(2)}) %collective-permute-start.3) | collective-permute-done | bytes 262176 | tf_op jit(solution)/shard_map/ppermute | solution.py:39
  15.9 1.2 %collective-permute-done.5.refs_8_ = bf16[256,512]{1,0:T(8,128)(2,1)S(1)} collective-permute-done((bf16[256,512]{1,0:T(8,128)(2,1)S(1)}, bf16[256,512]{1,0:T(8,128)(2,1)S(1)}, u32[]{:S(2)}, u32[]{:S(2)}) %collective-permute-start.5) | collective-permute-done | bytes 262176 | tf_op jit(solution)/shard_map/ppermute | solution.py:39
  17.2 1.4 %forward.1 = (bf16[4,512,256]{2,1,0:T(8,128)(2,1)S(1)}, bf16[4,512,256]{2,1,0:T(8,128)(2,1)S(1)}) custom-call(bf16[256,512]{1,0:T(8,128)(2,1)S(1)} %copy-done.1, bf16[256,512]{1,0:T(8,128)(2,1)S(1)} %collective-permute-done.far_ref.refs_1_.refs_2_, bf16[2,256,512]{2,1,0:T(8,128)(2,1)S(1)} %collective-permute-done.1.refs_2_.refs_3_, ...), custom_call_target="tpu_custom_call" | custom-call | flops 1000000000 | tf_op jit(solution)/shard_map/forward/pallas_call | solution.py:49
  18.6 0.4 out.1.refs_9_
  19.1 1.6 %collective-permute-start.9 = (bf16[256,512]{1,0:T(8,128)(2,1)S(1)}, bf16[256,512]{1,0:T(8,128)(2,1)S(1)}, u32[]{:S(2)}, u32[]{:S(2)}) collective-permute-start(bf16[256,512]{1,0:T(8,128)(2,1)S(1)} %out.1.refs_9_), channel_id=1, source_target_pairs={{0,2},{1,3},{2,0},{3,1},{4,6},{5,7},{6,4},{7,5},{8,10},{9,11},{10,... | collective-permute-start | bytes 786440 | tf_op jit(solution)/shard_map/ppermute | solution.py:39
  20.7 1.5 %in.1 = (bf16[4,512,256]{2,1,0:T(8,128)(2,1)S(1)}, f32[256,512]{1,0:T(8,128)S(1)}, bf16[256,512]{1,0:T(8,128)(2,1)S(1)}) custom-call(bf16[4,512,256]{2,1,0:T(8,128)(2,1)S(1)} %get-tuple-element.19.refs_0_, bf16[256,512]{1,0:T(8,128)(2,1)S(1)} %copy-done.1, bf16[256,512]{1,0:T(8,128)(2,1)S(1)} %collective-permute-done.far_ref.refs_1_.refs_2_, ...), custom_call_target="tpu_custom_call" | custom-call | flops 100000000 | tf_op jit(solution)/shard_map/in/pallas_call | solution.py:49
  22.2 1.6 %collective-permute-start.8 = (bf16[256,512]{1,0:T(8,128)(2,1)S(1)}, bf16[256,512]{1,0:T(8,128)(2,1)S(1)}, u32[]{:S(2)}, u32[]{:S(2)}) collective-permute-start(bf16[256,512]{1,0:T(8,128)(2,1)S(1)} %get-tuple-element.24), channel_id=1, source_target_pairs={{0,8},{4,12},{8,0},{12,4},{16,24},{20,28},{24,16},{28,20},{1,9},{5... | collective-permute-start | bytes 786440 | tf_op jit(solution)/shard_map/ppermute | solution.py:39
  23.9 1.0 %own.1 = (f32[256,512]{1,0:T(8,128)S(1)}, bf16[2,256,512]{2,1,0:T(8,128)(2,1)S(1)}, bf16[2,256,512]{2,1,0:T(8,128)(2,1)S(1)}) custom-call(bf16[4,512,256]{2,1,0:T(8,128)(2,1)S(1)} %get-tuple-element.18.refs_0_.refs_4_, bf16[256,512]{1,0:T(8,128)(2,1)S(1)} %copy-done.2, bf16[256,512]{1,0:T(8,128)(2,1)S(1)} %collective-permute-done.3.far_ref.refs_2_.refs_5_, ...), custom_call_target="tpu_custom_call" | custom-call | flops 3000000000 | tf_op jit(solution)/shard_map/own/pallas_call | solution.py:49
  25.1 2.7 %collective-permute-done.9.refs_1_ = bf16[256,512]{1,0:T(8,128)(2,1)S(1)} collective-permute-done((bf16[256,512]{1,0:T(8,128)(2,1)S(1)}, bf16[256,512]{1,0:T(8,128)(2,1)S(1)}, u32[]{:S(2)}, u32[]{:S(2)}) %collective-permute-start.9) | collective-permute-done | bytes 262176 | tf_op jit(solution)/shard_map/ppermute | solution.py:39
  27.9 1.6 %collective-permute-start.11 = (bf16[128,512]{1,0:T(8,128)(2,1)S(1)}, bf16[128,512]{1,0:T(8,128)(2,1)S(1)}, u32[]{:S(2)}, u32[]{:S(2)}) collective-permute-start(bf16[128,512]{1,0:T(8,128)(2,1)S(1)} %get-tuple-element.28), channel_id=1, source_target_pairs={{0,8},{4,12},{8,0},{12,4},{16,24},{20,28},{24,16},{28,20},{1,9},{5... | collective-permute-start | bytes 393224 | tf_op jit(solution)/shard_map/ppermute | solution.py:39
  29.6 1.5 %collective-permute-done.8.refs_1_ = bf16[256,512]{1,0:T(8,128)(2,1)S(1)} collective-permute-done((bf16[256,512]{1,0:T(8,128)(2,1)S(1)}, bf16[256,512]{1,0:T(8,128)(2,1)S(1)}, u32[]{:S(2)}, u32[]{:S(2)}) %collective-permute-start.8) | collective-permute-done | bytes 262176 | tf_op jit(solution)/shard_map/ppermute | solution.py:39
  31.4 1.3 %collective-permute-start.10 = (bf16[256,512]{1,0:T(8,128)(2,1)S(1)}, bf16[256,512]{1,0:T(8,128)(2,1)S(1)}, u32[]{:S(2)}, u32[]{:S(2)}) collective-permute-start(bf16[256,512]{1,0:T(8,128)(2,1)S(1)} %other.1.refs_2_), channel_id=1, source_target_pairs={{0,1},{1,0},{2,3},{3,2},{4,5},{5,4},{6,7},{7,6},{8,9},{9,8},{10,11... | collective-permute-start | bytes 786440 | tf_op jit(solution)/shard_map/ppermute | solution.py:39
  32.7 0.8 %collective-permute-done.11.refs_1_ = bf16[128,512]{1,0:T(8,128)(2,1)S(1)} collective-permute-done((bf16[128,512]{1,0:T(8,128)(2,1)S(1)}, bf16[128,512]{1,0:T(8,128)(2,1)S(1)}, u32[]{:S(2)}, u32[]{:S(2)}) %collective-permute-start.11) | collective-permute-done | bytes 131104 | tf_op jit(solution)/shard_map/ppermute | solution.py:39
  33.6 2.6 %collective-permute-start.16 = (bf16[128,512]{1,0:T(8,128)(2,1)S(1)}, bf16[128,512]{1,0:T(8,128)(2,1)S(1)}, u32[]{:S(2)}, u32[]{:S(2)}) collective-permute-start(bf16[128,512]{1,0:T(8,128)(2,1)S(1)} %sum_out.1.refs_0_), channel_id=1, source_target_pairs={{0,16},{4,20},{8,24},{12,28},{16,0},{20,4},{24,8},{28,12},{1,17},{... | collective-permute-start | bytes 393224 | tf_op jit(solution)/shard_map/ppermute | solution.py:39
  36.2 2.6 %collective-permute-done.10.last_ref = bf16[256,512]{1,0:T(8,128)(2,1)S(1)} collective-permute-done((bf16[256,512]{1,0:T(8,128)(2,1)S(1)}, bf16[256,512]{1,0:T(8,128)(2,1)S(1)}, u32[]{:S(2)}, u32[]{:S(2)}) %collective-permute-start.10) | collective-permute-done | bytes 262176 | tf_op jit(solution)/shard_map/ppermute | solution.py:39
  38.8 1.8 %tiles.1 = (bf16[256,512]{1,0:T(8,128)(2,1)S(1)}, bf16[256,512]{1,0:T(8,128)(2,1)S(1)}, f32[256,512]{1,0:T(8,128)S(1)}) custom-call(bf16[2,256,512]{2,1,0:T(8,128)(2,1)S(1)} %get-tuple-element.21.keep_ref, bf16[2,256,512]{2,1,0:T(8,128)(2,1)S(1)} %collective-permute-done.7.got_ref, bf16[256,512]{1,0:T(8,128)(2,1)S(1)} %collective-permute-done.10.last_ref, ...), custom_call_target="tpu_custom_call" | custom-call | flops 100000000 | tf_op jit(solution)/shard_map/tiles/pallas_call | solution.py:49
  40.6 2.7 %collective-permute-start.15 = (bf16[128,512]{1,0:T(8,128)(2,1)S(1)}, bf16[128,512]{1,0:T(8,128)(2,1)S(1)}, u32[]{:S(2)}, u32[]{:S(2)}) collective-permute-start(bf16[128,512]{1,0:T(8,128)(2,1)S(1)} %sum_in.1.refs_2_.refs_0_), channel_id=1, source_target_pairs={{0,16},{4,20},{8,24},{12,28},{16,0},{20,4},{24,8},{28,12},{1,17},{... | collective-permute-start | bytes 393224 | tf_op jit(solution)/shard_map/ppermute | solution.py:39
  43.4 1.2 %collective-permute-start.21 = (bf16[128,512]{1,0:T(8,128)(2,1)S(1)}, bf16[128,512]{1,0:T(8,128)(2,1)S(1)}, u32[]{:S(2)}, u32[]{:S(2)}) collective-permute-start(bf16[128,512]{1,0:T(8,128)(2,1)S(1)} %add_out.1.refs_2_.refs_7_), channel_id=1, source_target_pairs={{0,8},{4,12},{8,0},{12,4},{16,24},{20,28},{24,16},{28,20},{1,9},{5... | collective-permute-start | bytes 393224 | tf_op jit(solution)/shard_map/ppermute | solution.py:39
  44.6 1.2 %collective-permute-start.12 = (bf16[256,512]{1,0:T(8,128)(2,1)S(1)}, bf16[256,512]{1,0:T(8,128)(2,1)S(1)}, u32[]{:S(2)}, u32[]{:S(2)}) collective-permute-start(bf16[256,512]{1,0:T(8,128)(2,1)S(1)} %get-tuple-element.30.refs_2_), channel_id=1, source_target_pairs={{0,28},{4,0},{8,4},{12,8},{16,12},{20,16},{24,20},{28,24},{1,29},{... | collective-permute-start | bytes 786440 | tf_op jit(solution)/shard_map/ppermute | solution.py:44
  45.7 1.6 %collective-permute-done.15.refs_1_ = bf16[128,512]{1,0:T(8,128)(2,1)S(1)} collective-permute-done((bf16[128,512]{1,0:T(8,128)(2,1)S(1)}, bf16[128,512]{1,0:T(8,128)(2,1)S(1)}, u32[]{:S(2)}, u32[]{:S(2)}) %collective-permute-start.15) | collective-permute-done | bytes 131104 | tf_op jit(solution)/shard_map/ppermute | solution.py:39
  47.4 1.8 %collective-permute-start.18 = (bf16[128,512]{1,0:T(8,128)(2,1)S(1)}, bf16[128,512]{1,0:T(8,128)(2,1)S(1)}, u32[]{:S(2)}, u32[]{:S(2)}) collective-permute-start(bf16[128,512]{1,0:T(8,128)(2,1)S(1)} %add_in.1.refs_3_), channel_id=1, source_target_pairs={{0,8},{4,12},{8,0},{12,4},{16,24},{20,28},{24,16},{28,20},{1,9},{5... | collective-permute-start | bytes 393224 | tf_op jit(solution)/shard_map/ppermute | solution.py:39
  49.3 0.5 collective-permute-start.17
  49.8 7.2 %collective-permute-done.18.refs_5_ = bf16[128,512]{1,0:T(8,128)(2,1)S(1)} collective-permute-done((bf16[128,512]{1,0:T(8,128)(2,1)S(1)}, bf16[128,512]{1,0:T(8,128)(2,1)S(1)}, u32[]{:S(2)}, u32[]{:S(2)}) %collective-permute-start.18) | collective-permute-done | bytes 131104 | tf_op jit(solution)/shard_map/ppermute | solution.py:39
  57.0 1.3 %collective-permute-done.19.refs_6_ = bf16[128,512]{1,0:T(8,128)(2,1)S(1)} collective-permute-done((bf16[128,512]{1,0:T(8,128)(2,1)S(1)}, bf16[128,512]{1,0:T(8,128)(2,1)S(1)}, u32[]{:S(2)}, u32[]{:S(2)}) %collective-permute-start.19) | collective-permute-done | bytes 131104 | tf_op jit(solution)/shard_map/ppermute | solution.py:39
  58.4 1.6 %finish.1 = (bf16[256,512]{1,0:T(8,128)(2,1)}, f32[512,512]{1,0:T(8,128)}, f32[512,512]{1,0:T(8,128)}) custom-call(f32[256,512]{1,0:T(8,128)S(1)} %get-tuple-element.29.refs_0_, bf16[256,512]{1,0:T(8,128)(2,1)S(1)} %collective-permute-done.12.refs_1_, bf16[256,512]{1,0:T(8,128)(2,1)S(1)} %collective-permute-done.13.refs_2_, ...), custom_call_target="tpu_custom_call" | custom-call | flops 100000000 | tf_op jit(solution)/shard_map/finish/pallas_call | solution.py:49
  (44 shorter events, 1.1 us)
Async XLA Ops:
  0.6 3.0 %copy-start = (bf16[512,512]{1,0:T(8,128)(2,1)S(1)}, bf16[512,512]{1,0:T(8,128)(2,1)}, u32[]{:S(2)}) copy-start(bf16[512,512]{1,0:T(8,128)(2,1)} %param.9) | copy-start | bytes 1572868
  0.6 10.4 %collective-permute-start = (bf16[256,512]{1,0:T(8,128)(2,1)}, bf16[256,512]{1,0:T(8,128)(2,1)S(1)}, u32[]{:S(2)}, u32[]{:S(2)}) collective-permute-start(bf16[256,512]{1,0:T(8,128)(2,1)} %refs_1_.4), channel_id=1, source_target_pairs={{0,1},{1,0},{2,3},{3,2},{4,5},{5,4},{6,7},{7,6},{8,9},{9,8},{10,11... | collective-permute-start | bytes 786440 | tf_op jit(solution)/shard_map/ppermute | solution.py:39
  3.7 1.6 %copy-start.2 = (bf16[256,512]{1,0:T(8,128)(2,1)S(1)}, bf16[256,512]{1,0:T(8,128)(2,1)}, u32[]{:S(2)}) copy-start(bf16[256,512]{1,0:T(8,128)(2,1)} %cot_ref.1) | copy-start | bytes 786436
  3.7 7.3 %copy-start.1 = (bf16[256,512]{1,0:T(8,128)(2,1)S(1)}, bf16[256,512]{1,0:T(8,128)(2,1)}, u32[]{:S(2)}) copy-start(bf16[256,512]{1,0:T(8,128)(2,1)} %refs_1_.4) | copy-start | bytes 786436
  3.7 9.3 %collective-permute-start.2 = (bf16[512,256]{1,0:T(8,128)(2,1)S(1)}, bf16[512,256]{1,0:T(8,128)(2,1)S(1)}, u32[]{:S(2)}, u32[]{:S(2)}) collective-permute-start(bf16[512,256]{1,0:T(8,128)(2,1)S(1)} %constant_dynamic-slice_fusion.1.refs_3_.refs_5_), channel_id=1, source_target_pairs={{0,2},{1,3},{2,0},{3,1},{4,6},{5,7},{6,4},{7,5},{8,10},{9,11},{10,... | collective-permute-start | bytes 786440 | tf_op jit(solution)/shard_map/ppermute | solution.py:39
  5.3 10.5 %collective-permute-start.3 = (bf16[256,512]{1,0:T(8,128)(2,1)S(1)}, bf16[256,512]{1,0:T(8,128)(2,1)S(1)}, u32[]{:S(2)}, u32[]{:S(2)}) collective-permute-start(bf16[256,512]{1,0:T(8,128)(2,1)S(1)} %copy-done.2), channel_id=1, source_target_pairs={{0,1},{1,0},{2,3},{3,2},{4,5},{5,4},{6,7},{7,6},{8,9},{9,8},{10,11... | collective-permute-start | bytes 786440 | tf_op jit(solution)/shard_map/ppermute | solution.py:39
  7.2 9.9 %collective-permute-start.5 = (bf16[256,512]{1,0:T(8,128)(2,1)S(1)}, bf16[256,512]{1,0:T(8,128)(2,1)S(1)}, u32[]{:S(2)}, u32[]{:S(2)}) collective-permute-start(bf16[256,512]{1,0:T(8,128)(2,1)S(1)} %constant_dynamic-slice_fusion.refs_7_), channel_id=1, source_target_pairs={{0,2},{1,3},{2,0},{3,1},{4,6},{5,7},{6,4},{7,5},{8,10},{9,11},{10,... | collective-permute-start | bytes 786440 | tf_op jit(solution)/shard_map/ppermute | solution.py:39
  11.0 6.1 %collective-permute-start.1 = (bf16[2,256,512]{2,1,0:T(8,128)(2,1)S(1)}, bf16[2,256,512]{2,1,0:T(8,128)(2,1)S(1)}, u32[]{:S(2)}, u32[]{:S(2)}) collective-permute-start(bf16[2,256,512]{2,1,0:T(8,128)(2,1)S(1)} %both_agg.1.refs_0_), channel_id=1, source_target_pairs={{0,4},{4,0},{8,12},{12,8},{16,20},{20,16},{24,28},{28,24},{1,5},{5... | collective-permute-start | bytes 1572872 | tf_op jit(solution)/shard_map/ppermute | solution.py:39
  15.8 2.8 %collective-permute-start.4 = (bf16[2,256,512]{2,1,0:T(8,128)(2,1)S(1)}, bf16[2,256,512]{2,1,0:T(8,128)(2,1)S(1)}, u32[]{:S(2)}, u32[]{:S(2)}) collective-permute-start(bf16[2,256,512]{2,1,0:T(8,128)(2,1)S(1)} %both_cot.1.refs_5_), channel_id=1, source_target_pairs={{0,4},{4,0},{8,12},{12,8},{16,20},{20,16},{24,28},{28,24},{1,5},{5... | collective-permute-start | bytes 1572872 | tf_op jit(solution)/shard_map/ppermute | solution.py:39
  17.1 1.5 %collective-permute-start.6 = (bf16[16,512]{1,0:T(8,128)(2,1)S(1)}, bf16[16,512]{1,0:T(8,128)(2,1)S(1)}, u32[]{:S(2)}, u32[]{:S(2)}) collective-permute-start(bf16[16,512]{1,0:T(8,128)(2,1)S(1)} %lift.1), channel_id=1, source_target_pairs={{0,4},{4,0},{8,12},{12,8},{16,20},{20,16},{24,28},{28,24},{1,5},{5... | collective-permute-start | bytes 49160 | tf_op jit(solution)/shard_map/ppermute | solution.py:39
  19.1 8.8 %collective-permute-start.9 = (bf16[256,512]{1,0:T(8,128)(2,1)S(1)}, bf16[256,512]{1,0:T(8,128)(2,1)S(1)}, u32[]{:S(2)}, u32[]{:S(2)}) collective-permute-start(bf16[256,512]{1,0:T(8,128)(2,1)S(1)} %out.1.refs_9_), channel_id=1, source_target_pairs={{0,2},{1,3},{2,0},{3,1},{4,6},{5,7},{6,4},{7,5},{8,10},{9,11},{10,... | collective-permute-start | bytes 786440 | tf_op jit(solution)/shard_map/ppermute | solution.py:39
  22.2 8.8 %collective-permute-start.8 = (bf16[256,512]{1,0:T(8,128)(2,1)S(1)}, bf16[256,512]{1,0:T(8,128)(2,1)S(1)}, u32[]{:S(2)}, u32[]{:S(2)}) collective-permute-start(bf16[256,512]{1,0:T(8,128)(2,1)S(1)} %get-tuple-element.24), channel_id=1, source_target_pairs={{0,8},{4,12},{8,0},{12,4},{16,24},{20,28},{24,16},{28,20},{1,9},{5... | collective-permute-start | bytes 786440 | tf_op jit(solution)/shard_map/ppermute | solution.py:39
  23.9 1.1 %copy-start.3 = (bf16[1,4,256,256]{3,2,1,0:T(8,128)(2,1)S(1)}, bf16[1,4,256,256]{3,2,1,0:T(8,128)(2,1)}, u32[]{:S(2)}) copy-start(bf16[1,4,256,256]{3,2,1,0:T(8,128)(2,1)} %tiles_ref.1) | copy-start | bytes 1572868
  24.9 6.5 %collective-permute-start.7 = (bf16[2,256,512]{2,1,0:T(8,128)(2,1)S(1)}, bf16[2,256,512]{2,1,0:T(8,128)(2,1)S(1)}, u32[]{:S(2)}, u32[]{:S(2)}) collective-permute-start(bf16[2,256,512]{2,1,0:T(8,128)(2,1)S(1)} %get-tuple-element.22), channel_id=1, source_target_pairs={{0,4},{4,0},{8,12},{12,8},{16,20},{20,16},{24,28},{28,24},{1,5},{5... | collective-permute-start | bytes 1572872 | tf_op jit(solution)/shard_map/ppermute | solution.py:39
  27.9 5.6 %collective-permute-start.11 = (bf16[128,512]{1,0:T(8,128)(2,1)S(1)}, bf16[128,512]{1,0:T(8,128)(2,1)S(1)}, u32[]{:S(2)}, u32[]{:S(2)}) collective-permute-start(bf16[128,512]{1,0:T(8,128)(2,1)S(1)} %get-tuple-element.28), channel_id=1, source_target_pairs={{0,8},{4,12},{8,0},{12,4},{16,24},{20,28},{24,16},{28,20},{1,9},{5... | collective-permute-start | bytes 393224 | tf_op jit(solution)/shard_map/ppermute | solution.py:39
  31.1 9.5 %collective-permute-start.14 = (bf16[128,512]{1,0:T(8,128)(2,1)S(1)}, bf16[128,512]{1,0:T(8,128)(2,1)S(1)}, u32[]{:S(2)}, u32[]{:S(2)}) collective-permute-start(bf16[128,512]{1,0:T(8,128)(2,1)S(1)} %get-tuple-element.32), channel_id=1, source_target_pairs={{0,2},{1,3},{2,0},{3,1},{4,6},{5,7},{6,4},{7,5},{8,10},{9,11},{10,... | collective-permute-start | bytes 393224 | tf_op jit(solution)/shard_map/ppermute | solution.py:39
  31.4 7.4 %copy-start.4 = (s32[1,4]{1,0:T(1,128)S(1)}, s32[1,4]{1,0:T(1,128)}, u32[]{:S(2)}) copy-start(s32[1,4]{1,0:T(1,128)} %cols_ref.1) | copy-start | bytes 52
  31.4 7.4 %collective-permute-start.10 = (bf16[256,512]{1,0:T(8,128)(2,1)S(1)}, bf16[256,512]{1,0:T(8,128)(2,1)S(1)}, u32[]{:S(2)}, u32[]{:S(2)}) collective-permute-start(bf16[256,512]{1,0:T(8,128)(2,1)S(1)} %other.1.refs_2_), channel_id=1, source_target_pairs={{0,1},{1,0},{2,3},{3,2},{4,5},{5,4},{6,7},{7,6},{8,9},{9,8},{10,11... | collective-permute-start | bytes 786440 | tf_op jit(solution)/shard_map/ppermute | solution.py:39
  33.6 9.8 %collective-permute-start.16 = (bf16[128,512]{1,0:T(8,128)(2,1)S(1)}, bf16[128,512]{1,0:T(8,128)(2,1)S(1)}, u32[]{:S(2)}, u32[]{:S(2)}) collective-permute-start(bf16[128,512]{1,0:T(8,128)(2,1)S(1)} %sum_out.1.refs_0_), channel_id=1, source_target_pairs={{0,16},{4,20},{8,24},{12,28},{16,0},{20,4},{24,8},{28,12},{1,17},{... | collective-permute-start | bytes 393224 | tf_op jit(solution)/shard_map/ppermute | solution.py:39
  40.6 6.7 %collective-permute-start.15 = (bf16[128,512]{1,0:T(8,128)(2,1)S(1)}, bf16[128,512]{1,0:T(8,128)(2,1)S(1)}, u32[]{:S(2)}, u32[]{:S(2)}) collective-permute-start(bf16[128,512]{1,0:T(8,128)(2,1)S(1)} %sum_in.1.refs_2_.refs_0_), channel_id=1, source_target_pairs={{0,16},{4,20},{8,24},{12,28},{16,0},{20,4},{24,8},{28,12},{1,17},{... | collective-permute-start | bytes 393224 | tf_op jit(solution)/shard_map/ppermute | solution.py:39
  43.4 5.9 %collective-permute-start.21 = (bf16[128,512]{1,0:T(8,128)(2,1)S(1)}, bf16[128,512]{1,0:T(8,128)(2,1)S(1)}, u32[]{:S(2)}, u32[]{:S(2)}) collective-permute-start(bf16[128,512]{1,0:T(8,128)(2,1)S(1)} %add_out.1.refs_2_.refs_7_), channel_id=1, source_target_pairs={{0,8},{4,12},{8,0},{12,4},{16,24},{20,28},{24,16},{28,20},{1,9},{5... | collective-permute-start | bytes 393224 | tf_op jit(solution)/shard_map/ppermute | solution.py:39
  44.5 4.7 %collective-permute-start.20 = (bf16[128,512]{1,0:T(8,128)(2,1)S(1)}, bf16[128,512]{1,0:T(8,128)(2,1)S(1)}, u32[]{:S(2)}, u32[]{:S(2)}) collective-permute-start(bf16[128,512]{1,0:T(8,128)(2,1)S(1)} %add_out.1.refs_2_.refs_7_), channel_id=1, source_target_pairs={{0,4},{4,0},{8,12},{12,8},{16,20},{20,16},{24,28},{28,24},{1,5},{5... | collective-permute-start | bytes 393224 | tf_op jit(solution)/shard_map/ppermute | solution.py:39
  44.6 12.5 %collective-permute-start.12 = (bf16[256,512]{1,0:T(8,128)(2,1)S(1)}, bf16[256,512]{1,0:T(8,128)(2,1)S(1)}, u32[]{:S(2)}, u32[]{:S(2)}) collective-permute-start(bf16[256,512]{1,0:T(8,128)(2,1)S(1)} %get-tuple-element.30.refs_2_), channel_id=1, source_target_pairs={{0,28},{4,0},{8,4},{12,8},{16,12},{20,16},{24,20},{28,24},{1,29},{... | collective-permute-start | bytes 786440 | tf_op jit(solution)/shard_map/ppermute | solution.py:44
  45.7 11.3 %collective-permute-start.13 = (bf16[256,512]{1,0:T(8,128)(2,1)S(1)}, bf16[256,512]{1,0:T(8,128)(2,1)S(1)}, u32[]{:S(2)}, u32[]{:S(2)}) collective-permute-start(bf16[256,512]{1,0:T(8,128)(2,1)S(1)} %get-tuple-element.31), channel_id=1, source_target_pairs={{0,4},{4,8},{8,12},{12,16},{16,20},{20,24},{24,28},{28,0},{1,5},{5... | collective-permute-start | bytes 786440 | tf_op jit(solution)/shard_map/ppermute | solution.py:44
  47.4 9.6 %collective-permute-start.18 = (bf16[128,512]{1,0:T(8,128)(2,1)S(1)}, bf16[128,512]{1,0:T(8,128)(2,1)S(1)}, u32[]{:S(2)}, u32[]{:S(2)}) collective-permute-start(bf16[128,512]{1,0:T(8,128)(2,1)S(1)} %add_in.1.refs_3_), channel_id=1, source_target_pairs={{0,8},{4,12},{8,0},{12,4},{16,24},{20,28},{24,16},{28,20},{1,9},{5... | collective-permute-start | bytes 393224 | tf_op jit(solution)/shard_map/ppermute | solution.py:39
  49.3 7.8 %collective-permute-start.22 = (bf16[128,512]{1,0:T(8,128)(2,1)S(1)}, bf16[128,512]{1,0:T(8,128)(2,1)S(1)}, u32[]{:S(2)}, u32[]{:S(2)}) collective-permute-start(bf16[128,512]{1,0:T(8,128)(2,1)S(1)} %collective-permute-done.21.refs_9_), channel_id=1, source_target_pairs={{0,4},{4,0},{8,12},{12,8},{16,20},{20,16},{24,28},{28,24},{1,5},{5... | collective-permute-start | bytes 393224 | tf_op jit(solution)/shard_map/ppermute | solution.py:39
  49.3 7.8 %collective-permute-start.17 = (bf16[128,512]{1,0:T(8,128)(2,1)S(1)}, bf16[128,512]{1,0:T(8,128)(2,1)S(1)}, u32[]{:S(2)}, u32[]{:S(2)}) collective-permute-start(bf16[128,512]{1,0:T(8,128)(2,1)S(1)} %add_in.1.refs_3_), channel_id=1, source_target_pairs={{0,4},{4,0},{8,12},{12,8},{16,20},{20,16},{24,28},{28,24},{1,5},{5... | collective-permute-start | bytes 393224 | tf_op jit(solution)/shard_map/ppermute | solution.py:39
  57.0 1.3 %collective-permute-start.19 = (bf16[128,512]{1,0:T(8,128)(2,1)S(1)}, bf16[128,512]{1,0:T(8,128)(2,1)S(1)}, u32[]{:S(2)}, u32[]{:S(2)}) collective-permute-start(bf16[128,512]{1,0:T(8,128)(2,1)S(1)} %collective-permute-done.18.refs_5_), channel_id=1, source_target_pairs={{0,4},{4,0},{8,12},{12,8},{16,20},{20,16},{24,28},{28,24},{1,5},{5... | collective-permute-start | bytes 393224 | tf_op jit(solution)/shard_map/ppermute | solution.py:39

commit v7 on v6

--- a/solution.py
+++ b/solution.py
@@ -13,7 +13,7 @@
 VMEM = pl.BlockSpec(memory_space=pltpu.VMEM)
 SMEM = pl.BlockSpec(memory_space=pltpu.SMEM)
 COST = {
-    "both_cot": 8, "forward": 1, "lift": 9, "out": 8, "own": 3, "split": 25, "middle": 8,
+    "both_cot": 8, "forward": 4, "lift": 9, "out": 8, "own": 3, "split": 25, "middle": 8,
     "sum_out": 25, "sum_in": 25, "add_out": 1, "add_in": 3,
 }
 ANY = pl.BlockSpec(memory_space=pl.ANY)
@@ -300,11 +300,11 @@
     act, slope = run(
         "forward", functools.partial(forward_kernel, pieces), [hidden] * 2, (*aggs, win, *wins)
     )
-    before.append(swap(add("lift", (wouts[0][:16],)), "node", 1))
     part_out = run(
         "out", functools.partial(out_kernel, far), [shape(half, width)] * far, (act, *cots)
     )
     got_out = [swap(part, "rep", s) for part, s in zip(part_out, shards)]
+    before.append(swap(add("lift", (wouts[0][:16],)), "node", 1))
     grad_pre, keep_in, give_in = run(
         "in",
         functools.partial(in_kernel, pieces),

time: 59.8 us -> 59.9 us (level); the launches traced: 60 us -> 59.2 us
  waiting for transfers between devices: 25.9 us -> 23.2 us
  starting transfers between devices: 23.1 us -> 25.1 us
    ppermute x21, waiting for transfers between devices: 25.9 us -> 21.6 us  [swap(): return lax.ppermute(block, axis, [(i, i ^ mask) for i in range(count)])]
    ppermute x2, starting transfers between devices: 1.18 us -> 2.84 us  [shift(): lax.ppermute(block, axis, [(i, (i + step) % count) for i in range(count)])]
    ppermute x2, waiting for transfers between devices: 0.01 us -> 1.57 us  [shift(): lax.ppermute(block, axis, [(i, (i + step) % count) for i in range(count)])]
  transfers between devices with their start and end apart: 23 -> 23, of which waited for: 11 -> 10; matrix products, arithmetic and copies ran while one was open for 2% -> 2% of each run, Pallas kernels for 11% -> 11%
where the time goes in v7:
time: 59.9 us; the launch traced here: 59.2 us
  starting transfers between devices  25.1 us (42%)
  waiting for transfers between devices  23.2 us (39%)
  Pallas kernels  8.39 us (14%)
  between operations  1.49 us (2%)
  local copies, waits for them, and re-layouts  1.02 us (2%)
    ppermute x21, starting transfers between devices, swap(): return lax.ppermute(block, axis, [(i, i ^ mask) for i in range(count)])  22.3 us
    ppermute x21, waiting for transfers between devices, swap(): return lax.ppermute(block, axis, [(i, i ^ mask) for i in range(count)])  21.6 us
    pallas_call x17, Pallas kernels, call(): pl.pallas_call(kernel, out_shape=outs, in_specs=(specs or [VMEM] * len(ar...  8.39 us
    ppermute x2, starting transfers between devices, shift(): lax.ppermute(block, axis, [(i, (i + step) % count) for i in range(count)])  2.84 us
    ppermute x2, waiting for transfers between devices, shift(): lax.ppermute(block, axis, [(i, (i + step) % count) for i in range(count)])  1.57 us
  transfers between devices with their start and end apart: 23, of which 10 were waited for; matrix products, arithmetic and copies ran while one was open for 2% of the time, Pallas kernels for 11%

profile of v7, /device:TPU:0, one launch (start us, length us, event | category | flops | bytes accessed | tf_op | source)
XLA Modules:
  0.0 59.2 jit_solution(18281996880031530372)
XLA Ops:
  0.6 3.0 %collective-permute-start = (bf16[256,512]{1,0:T(8,128)(2,1)}, bf16[256,512]{1,0:T(8,128)(2,1)S(1)}, u32[]{:S(2)}, u32[]{:S(2)}) collective-permute-start(bf16[256,512]{1,0:T(8,128)(2,1)} %refs_1_.4), channel_id=1, source_target_pairs={{0,1},{1,0},{2,3},{3,2},{4,5},{5,4},{6,7},{7,6},{8,9},{9,8},{10,11... | collective-permute-start | bytes 786440 | tf_op jit(solution)/shard_map/ppermute | solution.py:39
  3.7 1.6 %collective-permute-start.2 = (bf16[512,256]{1,0:T(8,128)(2,1)S(1)}, bf16[512,256]{1,0:T(8,128)(2,1)S(1)}, u32[]{:S(2)}, u32[]{:S(2)}) collective-permute-start(bf16[512,256]{1,0:T(8,128)(2,1)S(1)} %constant_dynamic-slice_fusion.1.refs_3_.refs_5_), channel_id=1, source_target_pairs={{0,2},{1,3},{2,0},{3,1},{4,6},{5,7},{6,4},{7,5},{8,10},{9,11},{10,... | collective-permute-start | bytes 786440 | tf_op jit(solution)/shard_map/ppermute | solution.py:39
  5.3 1.0 %collective-permute-start.3 = (bf16[256,512]{1,0:T(8,128)(2,1)S(1)}, bf16[256,512]{1,0:T(8,128)(2,1)S(1)}, u32[]{:S(2)}, u32[]{:S(2)}) collective-permute-start(bf16[256,512]{1,0:T(8,128)(2,1)S(1)} %copy-done.2), channel_id=1, source_target_pairs={{0,1},{1,0},{2,3},{3,2},{4,5},{5,4},{6,7},{7,6},{8,9},{9,8},{10,11... | collective-permute-start | bytes 786440 | tf_op jit(solution)/shard_map/ppermute | solution.py:39
  6.2 1.0 %constant_dynamic-slice_fusion.refs_7_ = bf16[256,512]{1,0:T(8,128)(2,1)S(1)} fusion(bf16[512,512]{1,0:T(8,128)(2,1)} %param.10, s32[]{:T(128)S(6)} %select_n.4), kind=kLoop, calls=%fused_computation | loop fusion | bytes 524292 | tf_op jit(solution)/shard_map/dynamic_slice | solution.py:283
  7.2 0.9 %collective-permute-start.5 = (bf16[256,512]{1,0:T(8,128)(2,1)S(1)}, bf16[256,512]{1,0:T(8,128)(2,1)S(1)}, u32[]{:S(2)}, u32[]{:S(2)}) collective-permute-start(bf16[256,512]{1,0:T(8,128)(2,1)S(1)} %constant_dynamic-slice_fusion.refs_7_), channel_id=1, source_target_pairs={{0,2},{1,3},{2,0},{3,1},{4,6},{5,7},{6,4},{7,5},{8,10},{9,11},{10,... | collective-permute-start | bytes 786440 | tf_op jit(solution)/shard_map/ppermute | solution.py:39
  8.8 2.2 %collective-permute-done.far_ref.refs_1_.refs_2_ = bf16[256,512]{1,0:T(8,128)(2,1)S(1)} collective-permute-done((bf16[256,512]{1,0:T(8,128)(2,1)}, bf16[256,512]{1,0:T(8,128)(2,1)S(1)}, u32[]{:S(2)}, u32[]{:S(2)}) %collective-permute-start) | collective-permute-done | bytes 262176 | tf_op jit(solution)/shard_map/ppermute | solution.py:39
  11.1 1.9 %collective-permute-done.2.refs_1_.refs_4_.refs_6_ = bf16[512,256]{1,0:T(8,128)(2,1)S(1)} collective-permute-done((bf16[512,256]{1,0:T(8,128)(2,1)S(1)}, bf16[512,256]{1,0:T(8,128)(2,1)S(1)}, u32[]{:S(2)}, u32[]{:S(2)}) %collective-permute-start.2) | collective-permute-done | bytes 262176 | tf_op jit(solution)/shard_map/ppermute | solution.py:39
  13.0 2.8 %collective-permute-done.3.far_ref.refs_2_.refs_5_ = bf16[256,512]{1,0:T(8,128)(2,1)S(1)} collective-permute-done((bf16[256,512]{1,0:T(8,128)(2,1)S(1)}, bf16[256,512]{1,0:T(8,128)(2,1)S(1)}, u32[]{:S(2)}, u32[]{:S(2)}) %collective-permute-start.3) | collective-permute-done | bytes 262176 | tf_op jit(solution)/shard_map/ppermute | solution.py:39
  15.9 1.2 %collective-permute-done.5.refs_8_ = bf16[256,512]{1,0:T(8,128)(2,1)S(1)} collective-permute-done((bf16[256,512]{1,0:T(8,128)(2,1)S(1)}, bf16[256,512]{1,0:T(8,128)(2,1)S(1)}, u32[]{:S(2)}, u32[]{:S(2)}) %collective-permute-start.5) | collective-permute-done | bytes 262176 | tf_op jit(solution)/shard_map/ppermute | solution.py:39
  17.2 1.4 %forward.1 = (bf16[4,512,256]{2,1,0:T(8,128)(2,1)S(1)}, bf16[4,512,256]{2,1,0:T(8,128)(2,1)S(1)}) custom-call(bf16[256,512]{1,0:T(8,128)(2,1)S(1)} %copy-done.1, bf16[256,512]{1,0:T(8,128)(2,1)S(1)} %collective-permute-done.far_ref.refs_1_.refs_2_, bf16[2,256,512]{2,1,0:T(8,128)(2,1)S(1)} %collective-permute-done.1.refs_2_.refs_3_, ...), custom_call_target="tpu_custom_call" | custom-call | flops 4000000000 | tf_op jit(solution)/shard_map/forward/pallas_call | solution.py:49
  18.6 0.4 out.1.refs_9_
  19.1 1.6 %collective-permute-start.9 = (bf16[256,512]{1,0:T(8,128)(2,1)S(1)}, bf16[256,512]{1,0:T(8,128)(2,1)S(1)}, u32[]{:S(2)}, u32[]{:S(2)}) collective-permute-start(bf16[256,512]{1,0:T(8,128)(2,1)S(1)} %out.1.refs_9_), channel_id=1, source_target_pairs={{0,2},{1,3},{2,0},{3,1},{4,6},{5,7},{6,4},{7,5},{8,10},{9,11},{10,... | collective-permute-start | bytes 786440 | tf_op jit(solution)/shard_map/ppermute | solution.py:39
  20.7 1.5 %in.1 = (bf16[4,512,256]{2,1,0:T(8,128)(2,1)S(1)}, f32[256,512]{1,0:T(8,128)S(1)}, bf16[256,512]{1,0:T(8,128)(2,1)S(1)}) custom-call(bf16[4,512,256]{2,1,0:T(8,128)(2,1)S(1)} %get-tuple-element.19.refs_0_, bf16[256,512]{1,0:T(8,128)(2,1)S(1)} %copy-done.1, bf16[256,512]{1,0:T(8,128)(2,1)S(1)} %collective-permute-done.far_ref.refs_1_.refs_2_, ...), custom_call_target="tpu_custom_call" | custom-call | flops 100000000 | tf_op jit(solution)/shard_map/in/pallas_call | solution.py:49
  22.2 1.6 %collective-permute-start.8 = (bf16[256,512]{1,0:T(8,128)(2,1)S(1)}, bf16[256,512]{1,0:T(8,128)(2,1)S(1)}, u32[]{:S(2)}, u32[]{:S(2)}) collective-permute-start(bf16[256,512]{1,0:T(8,128)(2,1)S(1)} %get-tuple-element.24), channel_id=1, source_target_pairs={{0,8},{4,12},{8,0},{12,4},{16,24},{20,28},{24,16},{28,20},{1,9},{5... | collective-permute-start | bytes 786440 | tf_op jit(solution)/shard_map/ppermute | solution.py:39
  23.8 1.0 %own.1 = (f32[256,512]{1,0:T(8,128)S(1)}, bf16[2,256,512]{2,1,0:T(8,128)(2,1)S(1)}, bf16[2,256,512]{2,1,0:T(8,128)(2,1)S(1)}) custom-call(bf16[4,512,256]{2,1,0:T(8,128)(2,1)S(1)} %get-tuple-element.18.refs_0_.refs_4_, bf16[256,512]{1,0:T(8,128)(2,1)S(1)} %copy-done.2, bf16[256,512]{1,0:T(8,128)(2,1)S(1)} %collective-permute-done.3.far_ref.refs_2_.refs_5_, ...), custom_call_target="tpu_custom_call" | custom-call | flops 3000000000 | tf_op jit(solution)/shard_map/own/pallas_call | solution.py:49
  25.1 2.7 %collective-permute-done.9.refs_1_ = bf16[256,512]{1,0:T(8,128)(2,1)S(1)} collective-permute-done((bf16[256,512]{1,0:T(8,128)(2,1)S(1)}, bf16[256,512]{1,0:T(8,128)(2,1)S(1)}, u32[]{:S(2)}, u32[]{:S(2)}) %collective-permute-start.9) | collective-permute-done | bytes 262176 | tf_op jit(solution)/shard_map/ppermute | solution.py:39
  27.9 1.6 %collective-permute-start.11 = (bf16[128,512]{1,0:T(8,128)(2,1)S(1)}, bf16[128,512]{1,0:T(8,128)(2,1)S(1)}, u32[]{:S(2)}, u32[]{:S(2)}) collective-permute-start(bf16[128,512]{1,0:T(8,128)(2,1)S(1)} %get-tuple-element.28), channel_id=1, source_target_pairs={{0,8},{4,12},{8,0},{12,4},{16,24},{20,28},{24,16},{28,20},{1,9},{5... | collective-permute-start | bytes 393224 | tf_op jit(solution)/shard_map/ppermute | solution.py:39
  29.6 1.5 %collective-permute-done.8.refs_1_ = bf16[256,512]{1,0:T(8,128)(2,1)S(1)} collective-permute-done((bf16[256,512]{1,0:T(8,128)(2,1)S(1)}, bf16[256,512]{1,0:T(8,128)(2,1)S(1)}, u32[]{:S(2)}, u32[]{:S(2)}) %collective-permute-start.8) | collective-permute-done | bytes 262176 | tf_op jit(solution)/shard_map/ppermute | solution.py:39
  31.1 0.2 collective-permute-start.14
  31.4 1.3 %collective-permute-start.10 = (bf16[256,512]{1,0:T(8,128)(2,1)S(1)}, bf16[256,512]{1,0:T(8,128)(2,1)S(1)}, u32[]{:S(2)}, u32[]{:S(2)}) collective-permute-start(bf16[256,512]{1,0:T(8,128)(2,1)S(1)} %other.1.refs_2_), channel_id=1, source_target_pairs={{0,1},{1,0},{2,3},{3,2},{4,5},{5,4},{6,7},{7,6},{8,9},{9,8},{10,11... | collective-permute-start | bytes 786440 | tf_op jit(solution)/shard_map/ppermute | solution.py:39
  32.7 0.8 %collective-permute-done.11.refs_1_ = bf16[128,512]{1,0:T(8,128)(2,1)S(1)} collective-permute-done((bf16[128,512]{1,0:T(8,128)(2,1)S(1)}, bf16[128,512]{1,0:T(8,128)(2,1)S(1)}, u32[]{:S(2)}, u32[]{:S(2)}) %collective-permute-start.11) | collective-permute-done | bytes 131104 | tf_op jit(solution)/shard_map/ppermute | solution.py:39
  33.6 2.6 %collective-permute-start.16 = (bf16[128,512]{1,0:T(8,128)(2,1)S(1)}, bf16[128,512]{1,0:T(8,128)(2,1)S(1)}, u32[]{:S(2)}, u32[]{:S(2)}) collective-permute-start(bf16[128,512]{1,0:T(8,128)(2,1)S(1)} %sum_out.1.refs_0_), channel_id=1, source_target_pairs={{0,16},{4,20},{8,24},{12,28},{16,0},{20,4},{24,8},{28,12},{1,17},{... | collective-permute-start | bytes 393224 | tf_op jit(solution)/shard_map/ppermute | solution.py:39
  36.2 2.6 %collective-permute-done.10.last_ref = bf16[256,512]{1,0:T(8,128)(2,1)S(1)} collective-permute-done((bf16[256,512]{1,0:T(8,128)(2,1)S(1)}, bf16[256,512]{1,0:T(8,128)(2,1)S(1)}, u32[]{:S(2)}, u32[]{:S(2)}) %collective-permute-start.10) | collective-permute-done | bytes 262176 | tf_op jit(solution)/shard_map/ppermute | solution.py:39
  38.8 1.8 %tiles.1 = (bf16[256,512]{1,0:T(8,128)(2,1)S(1)}, bf16[256,512]{1,0:T(8,128)(2,1)S(1)}, f32[256,512]{1,0:T(8,128)S(1)}) custom-call(bf16[2,256,512]{2,1,0:T(8,128)(2,1)S(1)} %get-tuple-element.21.keep_ref, bf16[2,256,512]{2,1,0:T(8,128)(2,1)S(1)} %collective-permute-done.7.got_ref, bf16[256,512]{1,0:T(8,128)(2,1)S(1)} %collective-permute-done.10.last_ref, ...), custom_call_target="tpu_custom_call" | custom-call | flops 100000000 | tf_op jit(solution)/shard_map/tiles/pallas_call | solution.py:49
  40.6 2.7 %collective-permute-start.15 = (bf16[128,512]{1,0:T(8,128)(2,1)S(1)}, bf16[128,512]{1,0:T(8,128)(2,1)S(1)}, u32[]{:S(2)}, u32[]{:S(2)}) collective-permute-start(bf16[128,512]{1,0:T(8,128)(2,1)S(1)} %sum_in.1.refs_2_.refs_0_), channel_id=1, source_target_pairs={{0,16},{4,20},{8,24},{12,28},{16,0},{20,4},{24,8},{28,12},{1,17},{... | collective-permute-start | bytes 393224 | tf_op jit(solution)/shard_map/ppermute | solution.py:39
  43.3 1.0 %collective-permute-start.21 = (bf16[128,512]{1,0:T(8,128)(2,1)S(1)}, bf16[128,512]{1,0:T(8,128)(2,1)S(1)}, u32[]{:S(2)}, u32[]{:S(2)}) collective-permute-start(bf16[128,512]{1,0:T(8,128)(2,1)S(1)} %add_out.1.refs_2_.refs_7_), channel_id=1, source_target_pairs={{0,8},{4,12},{8,0},{12,4},{16,24},{20,28},{24,16},{28,20},{1,9},{5... | collective-permute-start | bytes 393224 | tf_op jit(solution)/shard_map/ppermute | solution.py:39
  44.3 2.8 %collective-permute-start.12 = (bf16[256,512]{1,0:T(8,128)(2,1)S(1)}, bf16[256,512]{1,0:T(8,128)(2,1)S(1)}, u32[]{:S(2)}, u32[]{:S(2)}) collective-permute-start(bf16[256,512]{1,0:T(8,128)(2,1)S(1)} %get-tuple-element.30.refs_2_), channel_id=1, source_target_pairs={{0,28},{4,0},{8,4},{12,8},{16,12},{20,16},{24,20},{28,24},{1,29},{... | collective-permute-start | bytes 786440 | tf_op jit(solution)/shard_map/ppermute | solution.py:44
  47.2 2.4 %collective-permute-start.18 = (bf16[128,512]{1,0:T(8,128)(2,1)S(1)}, bf16[128,512]{1,0:T(8,128)(2,1)S(1)}, u32[]{:S(2)}, u32[]{:S(2)}) collective-permute-start(bf16[128,512]{1,0:T(8,128)(2,1)S(1)} %add_in.1.refs_3_), channel_id=1, source_target_pairs={{0,8},{4,12},{8,0},{12,4},{16,24},{20,28},{24,16},{28,20},{1,9},{5... | collective-permute-start | bytes 393224 | tf_op jit(solution)/shard_map/ppermute | solution.py:39
  49.6 0.5 collective-permute-start.17
  50.1 5.8 %collective-permute-done.18.refs_5_ = bf16[128,512]{1,0:T(8,128)(2,1)S(1)} collective-permute-done((bf16[128,512]{1,0:T(8,128)(2,1)S(1)}, bf16[128,512]{1,0:T(8,128)(2,1)S(1)}, u32[]{:S(2)}, u32[]{:S(2)}) %collective-permute-start.18) | collective-permute-done | bytes 131104 | tf_op jit(solution)/shard_map/ppermute | solution.py:39
  56.0 1.6 %collective-permute-done.13.refs_2_ = bf16[256,512]{1,0:T(8,128)(2,1)S(1)} collective-permute-done((bf16[256,512]{1,0:T(8,128)(2,1)S(1)}, bf16[256,512]{1,0:T(8,128)(2,1)S(1)}, u32[]{:S(2)}, u32[]{:S(2)}) %collective-permute-start.13) | collective-permute-done | bytes 262176 | tf_op jit(solution)/shard_map/ppermute | solution.py:44
  57.6 1.6 %finish.1 = (bf16[256,512]{1,0:T(8,128)(2,1)}, f32[512,512]{1,0:T(8,128)}, f32[512,512]{1,0:T(8,128)}) custom-call(f32[256,512]{1,0:T(8,128)S(1)} %get-tuple-element.29.refs_0_, bf16[256,512]{1,0:T(8,128)(2,1)S(1)} %collective-permute-done.12.refs_1_, bf16[256,512]{1,0:T(8,128)(2,1)S(1)} %collective-permute-done.13.refs_2_, ...), custom_call_target="tpu_custom_call" | custom-call | flops 100000000 | tf_op jit(solution)/shard_map/finish/pallas_call | solution.py:49
  (44 shorter events, 0.9 us)
Async XLA Ops:
  0.6 3.0 %copy-start = (bf16[512,512]{1,0:T(8,128)(2,1)S(1)}, bf16[512,512]{1,0:T(8,128)(2,1)}, u32[]{:S(2)}) copy-start(bf16[512,512]{1,0:T(8,128)(2,1)} %param.9) | copy-start | bytes 1572868
  0.6 10.4 %collective-permute-start = (bf16[256,512]{1,0:T(8,128)(2,1)}, bf16[256,512]{1,0:T(8,128)(2,1)S(1)}, u32[]{:S(2)}, u32[]{:S(2)}) collective-permute-start(bf16[256,512]{1,0:T(8,128)(2,1)} %refs_1_.4), channel_id=1, source_target_pairs={{0,1},{1,0},{2,3},{3,2},{4,5},{5,4},{6,7},{7,6},{8,9},{9,8},{10,11... | collective-permute-start | bytes 786440 | tf_op jit(solution)/shard_map/ppermute | solution.py:39
  3.7 1.6 %copy-start.2 = (bf16[256,512]{1,0:T(8,128)(2,1)S(1)}, bf16[256,512]{1,0:T(8,128)(2,1)}, u32[]{:S(2)}) copy-start(bf16[256,512]{1,0:T(8,128)(2,1)} %cot_ref.1) | copy-start | bytes 786436
  3.7 7.3 %copy-start.1 = (bf16[256,512]{1,0:T(8,128)(2,1)S(1)}, bf16[256,512]{1,0:T(8,128)(2,1)}, u32[]{:S(2)}) copy-start(bf16[256,512]{1,0:T(8,128)(2,1)} %refs_1_.4) | copy-start | bytes 786436
  3.7 9.3 %collective-permute-start.2 = (bf16[512,256]{1,0:T(8,128)(2,1)S(1)}, bf16[512,256]{1,0:T(8,128)(2,1)S(1)}, u32[]{:S(2)}, u32[]{:S(2)}) collective-permute-start(bf16[512,256]{1,0:T(8,128)(2,1)S(1)} %constant_dynamic-slice_fusion.1.refs_3_.refs_5_), channel_id=1, source_target_pairs={{0,2},{1,3},{2,0},{3,1},{4,6},{5,7},{6,4},{7,5},{8,10},{9,11},{10,... | collective-permute-start | bytes 786440 | tf_op jit(solution)/shard_map/ppermute | solution.py:39
  5.3 10.5 %collective-permute-start.3 = (bf16[256,512]{1,0:T(8,128)(2,1)S(1)}, bf16[256,512]{1,0:T(8,128)(2,1)S(1)}, u32[]{:S(2)}, u32[]{:S(2)}) collective-permute-start(bf16[256,512]{1,0:T(8,128)(2,1)S(1)} %copy-done.2), channel_id=1, source_target_pairs={{0,1},{1,0},{2,3},{3,2},{4,5},{5,4},{6,7},{7,6},{8,9},{9,8},{10,11... | collective-permute-start | bytes 786440 | tf_op jit(solution)/shard_map/ppermute | solution.py:39
  7.2 9.9 %collective-permute-start.5 = (bf16[256,512]{1,0:T(8,128)(2,1)S(1)}, bf16[256,512]{1,0:T(8,128)(2,1)S(1)}, u32[]{:S(2)}, u32[]{:S(2)}) collective-permute-start(bf16[256,512]{1,0:T(8,128)(2,1)S(1)} %constant_dynamic-slice_fusion.refs_7_), channel_id=1, source_target_pairs={{0,2},{1,3},{2,0},{3,1},{4,6},{5,7},{6,4},{7,5},{8,10},{9,11},{10,... | collective-permute-start | bytes 786440 | tf_op jit(solution)/shard_map/ppermute | solution.py:39
  11.0 6.1 %collective-permute-start.1 = (bf16[2,256,512]{2,1,0:T(8,128)(2,1)S(1)}, bf16[2,256,512]{2,1,0:T(8,128)(2,1)S(1)}, u32[]{:S(2)}, u32[]{:S(2)}) collective-permute-start(bf16[2,256,512]{2,1,0:T(8,128)(2,1)S(1)} %both_agg.1.refs_0_), channel_id=1, source_target_pairs={{0,4},{4,0},{8,12},{12,8},{16,20},{20,16},{24,28},{28,24},{1,5},{5... | collective-permute-start | bytes 1572872 | tf_op jit(solution)/shard_map/ppermute | solution.py:39
  15.8 2.8 %collective-permute-start.4 = (bf16[2,256,512]{2,1,0:T(8,128)(2,1)S(1)}, bf16[2,256,512]{2,1,0:T(8,128)(2,1)S(1)}, u32[]{:S(2)}, u32[]{:S(2)}) collective-permute-start(bf16[2,256,512]{2,1,0:T(8,128)(2,1)S(1)} %both_cot.1.refs_5_), channel_id=1, source_target_pairs={{0,4},{4,0},{8,12},{12,8},{16,20},{20,16},{24,28},{28,24},{1,5},{5... | collective-permute-start | bytes 1572872 | tf_op jit(solution)/shard_map/ppermute | solution.py:39
  17.1 3.5 %collective-permute-start.6 = (bf16[16,512]{1,0:T(8,128)(2,1)S(1)}, bf16[16,512]{1,0:T(8,128)(2,1)S(1)}, u32[]{:S(2)}, u32[]{:S(2)}) collective-permute-start(bf16[16,512]{1,0:T(8,128)(2,1)S(1)} %lift.1), channel_id=1, source_target_pairs={{0,4},{4,0},{8,12},{12,8},{16,20},{20,16},{24,28},{28,24},{1,5},{5... | collective-permute-start | bytes 49160 | tf_op jit(solution)/shard_map/ppermute | solution.py:39
  19.1 8.8 %collective-permute-start.9 = (bf16[256,512]{1,0:T(8,128)(2,1)S(1)}, bf16[256,512]{1,0:T(8,128)(2,1)S(1)}, u32[]{:S(2)}, u32[]{:S(2)}) collective-permute-start(bf16[256,512]{1,0:T(8,128)(2,1)S(1)} %out.1.refs_9_), channel_id=1, source_target_pairs={{0,2},{1,3},{2,0},{3,1},{4,6},{5,7},{6,4},{7,5},{8,10},{9,11},{10,... | collective-permute-start | bytes 786440 | tf_op jit(solution)/shard_map/ppermute | solution.py:39
  22.2 8.9 %collective-permute-start.8 = (bf16[256,512]{1,0:T(8,128)(2,1)S(1)}, bf16[256,512]{1,0:T(8,128)(2,1)S(1)}, u32[]{:S(2)}, u32[]{:S(2)}) collective-permute-start(bf16[256,512]{1,0:T(8,128)(2,1)S(1)} %get-tuple-element.24), channel_id=1, source_target_pairs={{0,8},{4,12},{8,0},{12,4},{16,24},{20,28},{24,16},{28,20},{1,9},{5... | collective-permute-start | bytes 786440 | tf_op jit(solution)/shard_map/ppermute | solution.py:39
  23.8 1.1 %copy-start.3 = (bf16[1,4,256,256]{3,2,1,0:T(8,128)(2,1)S(1)}, bf16[1,4,256,256]{3,2,1,0:T(8,128)(2,1)}, u32[]{:S(2)}) copy-start(bf16[1,4,256,256]{3,2,1,0:T(8,128)(2,1)} %tiles_ref.1) | copy-start | bytes 1572868
  24.8 6.5 %collective-permute-start.7 = (bf16[2,256,512]{2,1,0:T(8,128)(2,1)S(1)}, bf16[2,256,512]{2,1,0:T(8,128)(2,1)S(1)}, u32[]{:S(2)}, u32[]{:S(2)}) collective-permute-start(bf16[2,256,512]{2,1,0:T(8,128)(2,1)S(1)} %get-tuple-element.22), channel_id=1, source_target_pairs={{0,4},{4,0},{8,12},{12,8},{16,20},{20,16},{24,28},{28,24},{1,5},{5... | collective-permute-start | bytes 1572872 | tf_op jit(solution)/shard_map/ppermute | solution.py:39
  27.9 5.6 %collective-permute-start.11 = (bf16[128,512]{1,0:T(8,128)(2,1)S(1)}, bf16[128,512]{1,0:T(8,128)(2,1)S(1)}, u32[]{:S(2)}, u32[]{:S(2)}) collective-permute-start(bf16[128,512]{1,0:T(8,128)(2,1)S(1)} %get-tuple-element.28), channel_id=1, source_target_pairs={{0,8},{4,12},{8,0},{12,4},{16,24},{20,28},{24,16},{28,20},{1,9},{5... | collective-permute-start | bytes 393224 | tf_op jit(solution)/shard_map/ppermute | solution.py:39
  31.1 9.5 %collective-permute-start.14 = (bf16[128,512]{1,0:T(8,128)(2,1)S(1)}, bf16[128,512]{1,0:T(8,128)(2,1)S(1)}, u32[]{:S(2)}, u32[]{:S(2)}) collective-permute-start(bf16[128,512]{1,0:T(8,128)(2,1)S(1)} %get-tuple-element.32), channel_id=1, source_target_pairs={{0,2},{1,3},{2,0},{3,1},{4,6},{5,7},{6,4},{7,5},{8,10},{9,11},{10,... | collective-permute-start | bytes 393224 | tf_op jit(solution)/shard_map/ppermute | solution.py:39
  31.4 7.4 %copy-start.4 = (s32[1,4]{1,0:T(1,128)S(1)}, s32[1,4]{1,0:T(1,128)}, u32[]{:S(2)}) copy-start(s32[1,4]{1,0:T(1,128)} %cols_ref.1) | copy-start | bytes 52
  31.4 7.4 %collective-permute-start.10 = (bf16[256,512]{1,0:T(8,128)(2,1)S(1)}, bf16[256,512]{1,0:T(8,128)(2,1)S(1)}, u32[]{:S(2)}, u32[]{:S(2)}) collective-permute-start(bf16[256,512]{1,0:T(8,128)(2,1)S(1)} %other.1.refs_2_), channel_id=1, source_target_pairs={{0,1},{1,0},{2,3},{3,2},{4,5},{5,4},{6,7},{7,6},{8,9},{9,8},{10,11... | collective-permute-start | bytes 786440 | tf_op jit(solution)/shard_map/ppermute | solution.py:39
  33.6 9.8 %collective-permute-start.16 = (bf16[128,512]{1,0:T(8,128)(2,1)S(1)}, bf16[128,512]{1,0:T(8,128)(2,1)S(1)}, u32[]{:S(2)}, u32[]{:S(2)}) collective-permute-start(bf16[128,512]{1,0:T(8,128)(2,1)S(1)} %sum_out.1.refs_0_), channel_id=1, source_target_pairs={{0,16},{4,20},{8,24},{12,28},{16,0},{20,4},{24,8},{28,12},{1,17},{... | collective-permute-start | bytes 393224 | tf_op jit(solution)/shard_map/ppermute | solution.py:39
  40.6 6.5 %collective-permute-start.15 = (bf16[128,512]{1,0:T(8,128)(2,1)S(1)}, bf16[128,512]{1,0:T(8,128)(2,1)S(1)}, u32[]{:S(2)}, u32[]{:S(2)}) collective-permute-start(bf16[128,512]{1,0:T(8,128)(2,1)S(1)} %sum_in.1.refs_2_.refs_0_), channel_id=1, source_target_pairs={{0,16},{4,20},{8,24},{12,28},{16,0},{20,4},{24,8},{28,12},{1,17},{... | collective-permute-start | bytes 393224 | tf_op jit(solution)/shard_map/ppermute | solution.py:39
  43.3 6.3 %collective-permute-start.21 = (bf16[128,512]{1,0:T(8,128)(2,1)S(1)}, bf16[128,512]{1,0:T(8,128)(2,1)S(1)}, u32[]{:S(2)}, u32[]{:S(2)}) collective-permute-start(bf16[128,512]{1,0:T(8,128)(2,1)S(1)} %add_out.1.refs_2_.refs_7_), channel_id=1, source_target_pairs={{0,8},{4,12},{8,0},{12,4},{16,24},{20,28},{24,16},{28,20},{1,9},{5... | collective-permute-start | bytes 393224 | tf_op jit(solution)/shard_map/ppermute | solution.py:39
  44.3 5.3 %collective-permute-start.20 = (bf16[128,512]{1,0:T(8,128)(2,1)S(1)}, bf16[128,512]{1,0:T(8,128)(2,1)S(1)}, u32[]{:S(2)}, u32[]{:S(2)}) collective-permute-start(bf16[128,512]{1,0:T(8,128)(2,1)S(1)} %add_out.1.refs_2_.refs_7_), channel_id=1, source_target_pairs={{0,4},{4,0},{8,12},{12,8},{16,20},{20,16},{24,28},{28,24},{1,5},{5... | collective-permute-start | bytes 393224 | tf_op jit(solution)/shard_map/ppermute | solution.py:39
  44.3 11.7 %collective-permute-start.12 = (bf16[256,512]{1,0:T(8,128)(2,1)S(1)}, bf16[256,512]{1,0:T(8,128)(2,1)S(1)}, u32[]{:S(2)}, u32[]{:S(2)}) collective-permute-start(bf16[256,512]{1,0:T(8,128)(2,1)S(1)} %get-tuple-element.30.refs_2_), channel_id=1, source_target_pairs={{0,28},{4,0},{8,4},{12,8},{16,12},{20,16},{24,20},{28,24},{1,29},{... | collective-permute-start | bytes 786440 | tf_op jit(solution)/shard_map/ppermute | solution.py:44
  47.2 10.4 %collective-permute-start.13 = (bf16[256,512]{1,0:T(8,128)(2,1)S(1)}, bf16[256,512]{1,0:T(8,128)(2,1)S(1)}, u32[]{:S(2)}, u32[]{:S(2)}) collective-permute-start(bf16[256,512]{1,0:T(8,128)(2,1)S(1)} %get-tuple-element.31), channel_id=1, source_target_pairs={{0,4},{4,8},{8,12},{12,16},{16,20},{20,24},{24,28},{28,0},{1,5},{5... | collective-permute-start | bytes 786440 | tf_op jit(solution)/shard_map/ppermute | solution.py:44
  47.2 8.8 %collective-permute-start.18 = (bf16[128,512]{1,0:T(8,128)(2,1)S(1)}, bf16[128,512]{1,0:T(8,128)(2,1)S(1)}, u32[]{:S(2)}, u32[]{:S(2)}) collective-permute-start(bf16[128,512]{1,0:T(8,128)(2,1)S(1)} %add_in.1.refs_3_), channel_id=1, source_target_pairs={{0,8},{4,12},{8,0},{12,4},{16,24},{20,28},{24,16},{28,20},{1,9},{5... | collective-permute-start | bytes 393224 | tf_op jit(solution)/shard_map/ppermute | solution.py:39
  49.6 6.4 %collective-permute-start.22 = (bf16[128,512]{1,0:T(8,128)(2,1)S(1)}, bf16[128,512]{1,0:T(8,128)(2,1)S(1)}, u32[]{:S(2)}, u32[]{:S(2)}) collective-permute-start(bf16[128,512]{1,0:T(8,128)(2,1)S(1)} %collective-permute-done.21.refs_9_), channel_id=1, source_target_pairs={{0,4},{4,0},{8,12},{12,8},{16,20},{20,16},{24,28},{28,24},{1,5},{5... | collective-permute-start | bytes 393224 | tf_op jit(solution)/shard_map/ppermute | solution.py:39
  49.6 6.4 %collective-permute-start.17 = (bf16[128,512]{1,0:T(8,128)(2,1)S(1)}, bf16[128,512]{1,0:T(8,128)(2,1)S(1)}, u32[]{:S(2)}, u32[]{:S(2)}) collective-permute-start(bf16[128,512]{1,0:T(8,128)(2,1)S(1)} %add_in.1.refs_3_), channel_id=1, source_target_pairs={{0,4},{4,0},{8,12},{12,8},{16,20},{20,16},{24,28},{28,24},{1,5},{5... | collective-permute-start | bytes 393224 | tf_op jit(solution)/shard_map/ppermute | solution.py:39
  56.0 1.6 %collective-permute-start.19 = (bf16[128,512]{1,0:T(8,128)(2,1)S(1)}, bf16[128,512]{1,0:T(8,128)(2,1)S(1)}, u32[]{:S(2)}, u32[]{:S(2)}) collective-permute-start(bf16[128,512]{1,0:T(8,128)(2,1)S(1)} %collective-permute-done.18.refs_5_), channel_id=1, source_target_pairs={{0,4},{4,0},{8,12},{12,8},{16,20},{20,16},{24,28},{28,24},{1,5},{5... | collective-permute-start | bytes 393224 | tf_op jit(solution)/shard_map/ppermute | solution.py:39

commit v8 on v7

--- a/solution.py
+++ b/solution.py
@@ -13,7 +13,7 @@
 VMEM = pl.BlockSpec(memory_space=pltpu.VMEM)
 SMEM = pl.BlockSpec(memory_space=pltpu.SMEM)
 COST = {
-    "both_cot": 8, "forward": 4, "lift": 9, "out": 8, "own": 3, "split": 25, "middle": 8,
+    "both_cot": 3, "forward": 1, "lift": 9, "out": 8, "own": 3, "split": 25, "middle": 8,
     "sum_out": 25, "sum_in": 25, "add_out": 1, "add_in": 3,
 }
 ANY = pl.BlockSpec(memory_space=pl.ANY)

time: 59.9 us -> 59.9 us (level); the launches traced: 59.2 us -> 59.8 us
  waiting for transfers between devices: 23.2 us -> 24.9 us
  starting transfers between devices: 25.1 us -> 24 us
    ppermute x21, waiting for transfers between devices: 21.6 us -> 24.9 us  [swap(): return lax.ppermute(block, axis, [(i, i ^ mask) for i in range(count)])]
    ppermute x2, starting transfers between devices: 2.84 us -> 0.97 us  [shift(): lax.ppermute(block, axis, [(i, (i + step) % count) for i in range(count)])]
    ppermute x2, waiting for transfers between devices: 1.57 us -> 0.01 us  [shift(): lax.ppermute(block, axis, [(i, (i + step) % count) for i in range(count)])]
    ppermute x21, starting transfers between devices: 22.3 us -> 23 us  [swap(): return lax.ppermute(block, axis, [(i, i ^ mask) for i in range(count)])]
  transfers between devices with their start and end apart: 23 -> 23, of which waited for: 10 -> 11; matrix products, arithmetic and copies ran while one was open for 2% -> 2% of each run, Pallas kernels for 11% -> 11%
where the time goes in v8:
time: 59.9 us; the launch traced here: 59.8 us
  waiting for transfers between devices  24.9 us (42%)
  starting transfers between devices  24 us (40%)
  Pallas kernels  8.39 us (14%)
  between operations  1.49 us (2%)
  local copies, waits for them, and re-layouts  1.02 us (2%)
    ppermute x21, waiting for transfers between devices, swap(): return lax.ppermute(block, axis, [(i, i ^ mask) for i in range(count)])  24.9 us
    ppermute x21, starting transfers between devices, swap(): return lax.ppermute(block, axis, [(i, i ^ mask) for i in range(count)])  23 us
    pallas_call x17, Pallas kernels, call(): pl.pallas_call(kernel, out_shape=outs, in_specs=(specs or [VMEM] * len(ar...  8.39 us
  transfers between devices with their start and end apart: 23, of which 11 were waited for; matrix products, arithmetic and copies ran while one was open for 2% of the time, Pallas kernels for 11%

profile of v8, /device:TPU:0, one launch (start us, length us, event | category | flops | bytes accessed | tf_op | source)
XLA Modules:
  0.0 59.8 jit_solution(18281996880031530372)
XLA Ops:
  0.6 3.0 %collective-permute-start = (bf16[256,512]{1,0:T(8,128)(2,1)}, bf16[256,512]{1,0:T(8,128)(2,1)S(1)}, u32[]{:S(2)}, u32[]{:S(2)}) collective-permute-start(bf16[256,512]{1,0:T(8,128)(2,1)} %refs_1_.4), channel_id=1, source_target_pairs={{0,1},{1,0},{2,3},{3,2},{4,5},{5,4},{6,7},{7,6},{8,9},{9,8},{10,11... | collective-permute-start | bytes 786440 | tf_op jit(solution)/shard_map/ppermute | solution.py:39
  3.7 1.6 %collective-permute-start.2 = (bf16[512,256]{1,0:T(8,128)(2,1)S(1)}, bf16[512,256]{1,0:T(8,128)(2,1)S(1)}, u32[]{:S(2)}, u32[]{:S(2)}) collective-permute-start(bf16[512,256]{1,0:T(8,128)(2,1)S(1)} %constant_dynamic-slice_fusion.1.refs_3_.refs_5_), channel_id=1, source_target_pairs={{0,2},{1,3},{2,0},{3,1},{4,6},{5,7},{6,4},{7,5},{8,10},{9,11},{10,... | collective-permute-start | bytes 786440 | tf_op jit(solution)/shard_map/ppermute | solution.py:39
  5.3 1.0 %collective-permute-start.3 = (bf16[256,512]{1,0:T(8,128)(2,1)S(1)}, bf16[256,512]{1,0:T(8,128)(2,1)S(1)}, u32[]{:S(2)}, u32[]{:S(2)}) collective-permute-start(bf16[256,512]{1,0:T(8,128)(2,1)S(1)} %copy-done.2), channel_id=1, source_target_pairs={{0,1},{1,0},{2,3},{3,2},{4,5},{5,4},{6,7},{7,6},{8,9},{9,8},{10,11... | collective-permute-start | bytes 786440 | tf_op jit(solution)/shard_map/ppermute | solution.py:39
  6.2 1.0 %constant_dynamic-slice_fusion.refs_7_ = bf16[256,512]{1,0:T(8,128)(2,1)S(1)} fusion(bf16[512,512]{1,0:T(8,128)(2,1)} %param.10, s32[]{:T(128)S(6)} %select_n.4), kind=kLoop, calls=%fused_computation | loop fusion | bytes 524292 | tf_op jit(solution)/shard_map/dynamic_slice | solution.py:283
  7.2 0.9 %collective-permute-start.5 = (bf16[256,512]{1,0:T(8,128)(2,1)S(1)}, bf16[256,512]{1,0:T(8,128)(2,1)S(1)}, u32[]{:S(2)}, u32[]{:S(2)}) collective-permute-start(bf16[256,512]{1,0:T(8,128)(2,1)S(1)} %constant_dynamic-slice_fusion.refs_7_), channel_id=1, source_target_pairs={{0,2},{1,3},{2,0},{3,1},{4,6},{5,7},{6,4},{7,5},{8,10},{9,11},{10,... | collective-permute-start | bytes 786440 | tf_op jit(solution)/shard_map/ppermute | solution.py:39
  8.8 2.2 %collective-permute-done.far_ref.refs_1_.refs_2_ = bf16[256,512]{1,0:T(8,128)(2,1)S(1)} collective-permute-done((bf16[256,512]{1,0:T(8,128)(2,1)}, bf16[256,512]{1,0:T(8,128)(2,1)S(1)}, u32[]{:S(2)}, u32[]{:S(2)}) %collective-permute-start) | collective-permute-done | bytes 262176 | tf_op jit(solution)/shard_map/ppermute | solution.py:39
  11.1 1.9 %collective-permute-done.2.refs_1_.refs_4_.refs_6_ = bf16[512,256]{1,0:T(8,128)(2,1)S(1)} collective-permute-done((bf16[512,256]{1,0:T(8,128)(2,1)S(1)}, bf16[512,256]{1,0:T(8,128)(2,1)S(1)}, u32[]{:S(2)}, u32[]{:S(2)}) %collective-permute-start.2) | collective-permute-done | bytes 262176 | tf_op jit(solution)/shard_map/ppermute | solution.py:39
  13.0 2.8 %collective-permute-done.3.far_ref.refs_2_.refs_5_ = bf16[256,512]{1,0:T(8,128)(2,1)S(1)} collective-permute-done((bf16[256,512]{1,0:T(8,128)(2,1)S(1)}, bf16[256,512]{1,0:T(8,128)(2,1)S(1)}, u32[]{:S(2)}, u32[]{:S(2)}) %collective-permute-start.3) | collective-permute-done | bytes 262176 | tf_op jit(solution)/shard_map/ppermute | solution.py:39
  15.9 1.2 %collective-permute-done.5.refs_8_ = bf16[256,512]{1,0:T(8,128)(2,1)S(1)} collective-permute-done((bf16[256,512]{1,0:T(8,128)(2,1)S(1)}, bf16[256,512]{1,0:T(8,128)(2,1)S(1)}, u32[]{:S(2)}, u32[]{:S(2)}) %collective-permute-start.5) | collective-permute-done | bytes 262176 | tf_op jit(solution)/shard_map/ppermute | solution.py:39
  17.2 1.4 %forward.1 = (bf16[4,512,256]{2,1,0:T(8,128)(2,1)S(1)}, bf16[4,512,256]{2,1,0:T(8,128)(2,1)S(1)}) custom-call(bf16[256,512]{1,0:T(8,128)(2,1)S(1)} %copy-done.1, bf16[256,512]{1,0:T(8,128)(2,1)S(1)} %collective-permute-done.far_ref.refs_1_.refs_2_, bf16[2,256,512]{2,1,0:T(8,128)(2,1)S(1)} %collective-permute-done.1.refs_2_.refs_3_, ...), custom_call_target="tpu_custom_call" | custom-call | flops 1000000000 | tf_op jit(solution)/shard_map/forward/pallas_call | solution.py:49
  18.6 0.4 out.1.refs_9_
  19.1 1.6 %collective-permute-start.9 = (bf16[256,512]{1,0:T(8,128)(2,1)S(1)}, bf16[256,512]{1,0:T(8,128)(2,1)S(1)}, u32[]{:S(2)}, u32[]{:S(2)}) collective-permute-start(bf16[256,512]{1,0:T(8,128)(2,1)S(1)} %out.1.refs_9_), channel_id=1, source_target_pairs={{0,2},{1,3},{2,0},{3,1},{4,6},{5,7},{6,4},{7,5},{8,10},{9,11},{10,... | collective-permute-start | bytes 786440 | tf_op jit(solution)/shard_map/ppermute | solution.py:39
  20.7 1.5 %in.1 = (bf16[4,512,256]{2,1,0:T(8,128)(2,1)S(1)}, f32[256,512]{1,0:T(8,128)S(1)}, bf16[256,512]{1,0:T(8,128)(2,1)S(1)}) custom-call(bf16[4,512,256]{2,1,0:T(8,128)(2,1)S(1)} %get-tuple-element.19.refs_0_, bf16[256,512]{1,0:T(8,128)(2,1)S(1)} %copy-done.1, bf16[256,512]{1,0:T(8,128)(2,1)S(1)} %collective-permute-done.far_ref.refs_1_.refs_2_, ...), custom_call_target="tpu_custom_call" | custom-call | flops 100000000 | tf_op jit(solution)/shard_map/in/pallas_call | solution.py:49
  22.2 1.6 %collective-permute-start.8 = (bf16[256,512]{1,0:T(8,128)(2,1)S(1)}, bf16[256,512]{1,0:T(8,128)(2,1)S(1)}, u32[]{:S(2)}, u32[]{:S(2)}) collective-permute-start(bf16[256,512]{1,0:T(8,128)(2,1)S(1)} %get-tuple-element.24), channel_id=1, source_target_pairs={{0,8},{4,12},{8,0},{12,4},{16,24},{20,28},{24,16},{28,20},{1,9},{5... | collective-permute-start | bytes 786440 | tf_op jit(solution)/shard_map/ppermute | solution.py:39
  23.8 1.0 %own.1 = (f32[256,512]{1,0:T(8,128)S(1)}, bf16[2,256,512]{2,1,0:T(8,128)(2,1)S(1)}, bf16[2,256,512]{2,1,0:T(8,128)(2,1)S(1)}) custom-call(bf16[4,512,256]{2,1,0:T(8,128)(2,1)S(1)} %get-tuple-element.18.refs_0_.refs_4_, bf16[256,512]{1,0:T(8,128)(2,1)S(1)} %copy-done.2, bf16[256,512]{1,0:T(8,128)(2,1)S(1)} %collective-permute-done.3.far_ref.refs_2_.refs_5_, ...), custom_call_target="tpu_custom_call" | custom-call | flops 3000000000 | tf_op jit(solution)/shard_map/own/pallas_call | solution.py:49
  25.1 2.7 %collective-permute-done.9.refs_1_ = bf16[256,512]{1,0:T(8,128)(2,1)S(1)} collective-permute-done((bf16[256,512]{1,0:T(8,128)(2,1)S(1)}, bf16[256,512]{1,0:T(8,128)(2,1)S(1)}, u32[]{:S(2)}, u32[]{:S(2)}) %collective-permute-start.9) | collective-permute-done | bytes 262176 | tf_op jit(solution)/shard_map/ppermute | solution.py:39
  27.9 1.6 %collective-permute-start.11 = (bf16[128,512]{1,0:T(8,128)(2,1)S(1)}, bf16[128,512]{1,0:T(8,128)(2,1)S(1)}, u32[]{:S(2)}, u32[]{:S(2)}) collective-permute-start(bf16[128,512]{1,0:T(8,128)(2,1)S(1)} %get-tuple-element.28), channel_id=1, source_target_pairs={{0,8},{4,12},{8,0},{12,4},{16,24},{20,28},{24,16},{28,20},{1,9},{5... | collective-permute-start | bytes 393224 | tf_op jit(solution)/shard_map/ppermute | solution.py:39
  29.6 1.5 %collective-permute-done.8.refs_1_ = bf16[256,512]{1,0:T(8,128)(2,1)S(1)} collective-permute-done((bf16[256,512]{1,0:T(8,128)(2,1)S(1)}, bf16[256,512]{1,0:T(8,128)(2,1)S(1)}, u32[]{:S(2)}, u32[]{:S(2)}) %collective-permute-start.8) | collective-permute-done | bytes 262176 | tf_op jit(solution)/shard_map/ppermute | solution.py:39
  31.4 1.3 %collective-permute-start.10 = (bf16[256,512]{1,0:T(8,128)(2,1)S(1)}, bf16[256,512]{1,0:T(8,128)(2,1)S(1)}, u32[]{:S(2)}, u32[]{:S(2)}) collective-permute-start(bf16[256,512]{1,0:T(8,128)(2,1)S(1)} %other.1.refs_2_), channel_id=1, source_target_pairs={{0,1},{1,0},{2,3},{3,2},{4,5},{5,4},{6,7},{7,6},{8,9},{9,8},{10,11... | collective-permute-start | bytes 786440 | tf_op jit(solution)/shard_map/ppermute | solution.py:39
  32.7 0.8 %collective-permute-done.11.refs_1_ = bf16[128,512]{1,0:T(8,128)(2,1)S(1)} collective-permute-done((bf16[128,512]{1,0:T(8,128)(2,1)S(1)}, bf16[128,512]{1,0:T(8,128)(2,1)S(1)}, u32[]{:S(2)}, u32[]{:S(2)}) %collective-permute-start.11) | collective-permute-done | bytes 131104 | tf_op jit(solution)/shard_map/ppermute | solution.py:39
  33.6 2.6 %collective-permute-start.16 = (bf16[128,512]{1,0:T(8,128)(2,1)S(1)}, bf16[128,512]{1,0:T(8,128)(2,1)S(1)}, u32[]{:S(2)}, u32[]{:S(2)}) collective-permute-start(bf16[128,512]{1,0:T(8,128)(2,1)S(1)} %sum_out.1.refs_0_), channel_id=1, source_target_pairs={{0,16},{4,20},{8,24},{12,28},{16,0},{20,4},{24,8},{28,12},{1,17},{... | collective-permute-start | bytes 393224 | tf_op jit(solution)/shard_map/ppermute | solution.py:39
  36.2 2.6 %collective-permute-done.10.last_ref = bf16[256,512]{1,0:T(8,128)(2,1)S(1)} collective-permute-done((bf16[256,512]{1,0:T(8,128)(2,1)S(1)}, bf16[256,512]{1,0:T(8,128)(2,1)S(1)}, u32[]{:S(2)}, u32[]{:S(2)}) %collective-permute-start.10) | collective-permute-done | bytes 262176 | tf_op jit(solution)/shard_map/ppermute | solution.py:39
  38.8 1.8 %tiles.1 = (bf16[256,512]{1,0:T(8,128)(2,1)S(1)}, bf16[256,512]{1,0:T(8,128)(2,1)S(1)}, f32[256,512]{1,0:T(8,128)S(1)}) custom-call(bf16[2,256,512]{2,1,0:T(8,128)(2,1)S(1)} %get-tuple-element.21.keep_ref, bf16[2,256,512]{2,1,0:T(8,128)(2,1)S(1)} %collective-permute-done.7.got_ref, bf16[256,512]{1,0:T(8,128)(2,1)S(1)} %collective-permute-done.10.last_ref, ...), custom_call_target="tpu_custom_call" | custom-call | flops 100000000 | tf_op jit(solution)/shard_map/tiles/pallas_call | solution.py:49
  40.6 2.2 %collective-permute-start.15 = (bf16[128,512]{1,0:T(8,128)(2,1)S(1)}, bf16[128,512]{1,0:T(8,128)(2,1)S(1)}, u32[]{:S(2)}, u32[]{:S(2)}) collective-permute-start(bf16[128,512]{1,0:T(8,128)(2,1)S(1)} %sum_in.1.refs_2_.refs_0_), channel_id=1, source_target_pairs={{0,16},{4,20},{8,24},{12,28},{16,0},{20,4},{24,8},{28,12},{1,17},{... | collective-permute-start | bytes 393224 | tf_op jit(solution)/shard_map/ppermute | solution.py:39
  42.9 1.9 %collective-permute-start.21 = (bf16[128,512]{1,0:T(8,128)(2,1)S(1)}, bf16[128,512]{1,0:T(8,128)(2,1)S(1)}, u32[]{:S(2)}, u32[]{:S(2)}) collective-permute-start(bf16[128,512]{1,0:T(8,128)(2,1)S(1)} %add_out.1.refs_2_.refs_7_), channel_id=1, source_target_pairs={{0,8},{4,12},{8,0},{12,4},{16,24},{20,28},{24,16},{28,20},{1,9},{5... | collective-permute-start | bytes 393224 | tf_op jit(solution)/shard_map/ppermute | solution.py:39
  44.8 1.0 %collective-permute-start.12 = (bf16[256,512]{1,0:T(8,128)(2,1)S(1)}, bf16[256,512]{1,0:T(8,128)(2,1)S(1)}, u32[]{:S(2)}, u32[]{:S(2)}) collective-permute-start(bf16[256,512]{1,0:T(8,128)(2,1)S(1)} %get-tuple-element.30.refs_2_), channel_id=1, source_target_pairs={{0,28},{4,0},{8,4},{12,8},{16,12},{20,16},{24,20},{28,24},{1,29},{... | collective-permute-start | bytes 786440 | tf_op jit(solution)/shard_map/ppermute | solution.py:44
  45.7 1.2 %collective-permute-done.15.refs_1_ = bf16[128,512]{1,0:T(8,128)(2,1)S(1)} collective-permute-done((bf16[128,512]{1,0:T(8,128)(2,1)S(1)}, bf16[128,512]{1,0:T(8,128)(2,1)S(1)}, u32[]{:S(2)}, u32[]{:S(2)}) %collective-permute-start.15) | collective-permute-done | bytes 131104 | tf_op jit(solution)/shard_map/ppermute | solution.py:39
  47.0 2.7 %collective-permute-start.18 = (bf16[128,512]{1,0:T(8,128)(2,1)S(1)}, bf16[128,512]{1,0:T(8,128)(2,1)S(1)}, u32[]{:S(2)}, u32[]{:S(2)}) collective-permute-start(bf16[128,512]{1,0:T(8,128)(2,1)S(1)} %add_in.1.refs_3_), channel_id=1, source_target_pairs={{0,8},{4,12},{8,0},{12,4},{16,24},{20,28},{24,16},{28,20},{1,9},{5... | collective-permute-start | bytes 393224 | tf_op jit(solution)/shard_map/ppermute | solution.py:39
  49.7 0.5 collective-permute-start.17
  50.2 6.6 %collective-permute-done.18.refs_5_ = bf16[128,512]{1,0:T(8,128)(2,1)S(1)} collective-permute-done((bf16[128,512]{1,0:T(8,128)(2,1)S(1)}, bf16[128,512]{1,0:T(8,128)(2,1)S(1)}, u32[]{:S(2)}, u32[]{:S(2)}) %collective-permute-start.18) | collective-permute-done | bytes 131104 | tf_op jit(solution)/shard_map/ppermute | solution.py:39
  56.9 1.3 %collective-permute-done.19.refs_6_ = bf16[128,512]{1,0:T(8,128)(2,1)S(1)} collective-permute-done((bf16[128,512]{1,0:T(8,128)(2,1)S(1)}, bf16[128,512]{1,0:T(8,128)(2,1)S(1)}, u32[]{:S(2)}, u32[]{:S(2)}) %collective-permute-start.19) | collective-permute-done | bytes 131104 | tf_op jit(solution)/shard_map/ppermute | solution.py:39
  58.2 1.6 %finish.1 = (bf16[256,512]{1,0:T(8,128)(2,1)}, f32[512,512]{1,0:T(8,128)}, f32[512,512]{1,0:T(8,128)}) custom-call(f32[256,512]{1,0:T(8,128)S(1)} %get-tuple-element.29.refs_0_, bf16[256,512]{1,0:T(8,128)(2,1)S(1)} %collective-permute-done.12.refs_1_, bf16[256,512]{1,0:T(8,128)(2,1)S(1)} %collective-permute-done.13.refs_2_, ...), custom_call_target="tpu_custom_call" | custom-call | flops 100000000 | tf_op jit(solution)/shard_map/finish/pallas_call | solution.py:49
  (44 shorter events, 1.1 us)
Async XLA Ops:
  0.6 3.0 %copy-start = (bf16[512,512]{1,0:T(8,128)(2,1)S(1)}, bf16[512,512]{1,0:T(8,128)(2,1)}, u32[]{:S(2)}) copy-start(bf16[512,512]{1,0:T(8,128)(2,1)} %param.9) | copy-start | bytes 1572868
  0.6 10.4 %collective-permute-start = (bf16[256,512]{1,0:T(8,128)(2,1)}, bf16[256,512]{1,0:T(8,128)(2,1)S(1)}, u32[]{:S(2)}, u32[]{:S(2)}) collective-permute-start(bf16[256,512]{1,0:T(8,128)(2,1)} %refs_1_.4), channel_id=1, source_target_pairs={{0,1},{1,0},{2,3},{3,2},{4,5},{5,4},{6,7},{7,6},{8,9},{9,8},{10,11... | collective-permute-start | bytes 786440 | tf_op jit(solution)/shard_map/ppermute | solution.py:39
  3.7 1.6 %copy-start.2 = (bf16[256,512]{1,0:T(8,128)(2,1)S(1)}, bf16[256,512]{1,0:T(8,128)(2,1)}, u32[]{:S(2)}) copy-start(bf16[256,512]{1,0:T(8,128)(2,1)} %cot_ref.1) | copy-start | bytes 786436
  3.7 7.3 %copy-start.1 = (bf16[256,512]{1,0:T(8,128)(2,1)S(1)}, bf16[256,512]{1,0:T(8,128)(2,1)}, u32[]{:S(2)}) copy-start(bf16[256,512]{1,0:T(8,128)(2,1)} %refs_1_.4) | copy-start | bytes 786436
  3.7 9.3 %collective-permute-start.2 = (bf16[512,256]{1,0:T(8,128)(2,1)S(1)}, bf16[512,256]{1,0:T(8,128)(2,1)S(1)}, u32[]{:S(2)}, u32[]{:S(2)}) collective-permute-start(bf16[512,256]{1,0:T(8,128)(2,1)S(1)} %constant_dynamic-slice_fusion.1.refs_3_.refs_5_), channel_id=1, source_target_pairs={{0,2},{1,3},{2,0},{3,1},{4,6},{5,7},{6,4},{7,5},{8,10},{9,11},{10,... | collective-permute-start | bytes 786440 | tf_op jit(solution)/shard_map/ppermute | solution.py:39
  5.3 10.5 %collective-permute-start.3 = (bf16[256,512]{1,0:T(8,128)(2,1)S(1)}, bf16[256,512]{1,0:T(8,128)(2,1)S(1)}, u32[]{:S(2)}, u32[]{:S(2)}) collective-permute-start(bf16[256,512]{1,0:T(8,128)(2,1)S(1)} %copy-done.2), channel_id=1, source_target_pairs={{0,1},{1,0},{2,3},{3,2},{4,5},{5,4},{6,7},{7,6},{8,9},{9,8},{10,11... | collective-permute-start | bytes 786440 | tf_op jit(solution)/shard_map/ppermute | solution.py:39
  7.2 9.9 %collective-permute-start.5 = (bf16[256,512]{1,0:T(8,128)(2,1)S(1)}, bf16[256,512]{1,0:T(8,128)(2,1)S(1)}, u32[]{:S(2)}, u32[]{:S(2)}) collective-permute-start(bf16[256,512]{1,0:T(8,128)(2,1)S(1)} %constant_dynamic-slice_fusion.refs_7_), channel_id=1, source_target_pairs={{0,2},{1,3},{2,0},{3,1},{4,6},{5,7},{6,4},{7,5},{8,10},{9,11},{10,... | collective-permute-start | bytes 786440 | tf_op jit(solution)/shard_map/ppermute | solution.py:39
  11.0 6.1 %collective-permute-start.1 = (bf16[2,256,512]{2,1,0:T(8,128)(2,1)S(1)}, bf16[2,256,512]{2,1,0:T(8,128)(2,1)S(1)}, u32[]{:S(2)}, u32[]{:S(2)}) collective-permute-start(bf16[2,256,512]{2,1,0:T(8,128)(2,1)S(1)} %both_agg.1.refs_0_), channel_id=1, source_target_pairs={{0,4},{4,0},{8,12},{12,8},{16,20},{20,16},{24,28},{28,24},{1,5},{5... | collective-permute-start | bytes 1572872 | tf_op jit(solution)/shard_map/ppermute | solution.py:39
  15.8 2.8 %collective-permute-start.4 = (bf16[2,256,512]{2,1,0:T(8,128)(2,1)S(1)}, bf16[2,256,512]{2,1,0:T(8,128)(2,1)S(1)}, u32[]{:S(2)}, u32[]{:S(2)}) collective-permute-start(bf16[2,256,512]{2,1,0:T(8,128)(2,1)S(1)} %both_cot.1.refs_5_), channel_id=1, source_target_pairs={{0,4},{4,0},{8,12},{12,8},{16,20},{20,16},{24,28},{28,24},{1,5},{5... | collective-permute-start | bytes 1572872 | tf_op jit(solution)/shard_map/ppermute | solution.py:39
  17.1 3.5 %collective-permute-start.6 = (bf16[16,512]{1,0:T(8,128)(2,1)S(1)}, bf16[16,512]{1,0:T(8,128)(2,1)S(1)}, u32[]{:S(2)}, u32[]{:S(2)}) collective-permute-start(bf16[16,512]{1,0:T(8,128)(2,1)S(1)} %lift.1), channel_id=1, source_target_pairs={{0,4},{4,0},{8,12},{12,8},{16,20},{20,16},{24,28},{28,24},{1,5},{5... | collective-permute-start | bytes 49160 | tf_op jit(solution)/shard_map/ppermute | solution.py:39
  19.1 8.8 %collective-permute-start.9 = (bf16[256,512]{1,0:T(8,128)(2,1)S(1)}, bf16[256,512]{1,0:T(8,128)(2,1)S(1)}, u32[]{:S(2)}, u32[]{:S(2)}) collective-permute-start(bf16[256,512]{1,0:T(8,128)(2,1)S(1)} %out.1.refs_9_), channel_id=1, source_target_pairs={{0,2},{1,3},{2,0},{3,1},{4,6},{5,7},{6,4},{7,5},{8,10},{9,11},{10,... | collective-permute-start | bytes 786440 | tf_op jit(solution)/shard_map/ppermute | solution.py:39
  22.2 8.9 %collective-permute-start.8 = (bf16[256,512]{1,0:T(8,128)(2,1)S(1)}, bf16[256,512]{1,0:T(8,128)(2,1)S(1)}, u32[]{:S(2)}, u32[]{:S(2)}) collective-permute-start(bf16[256,512]{1,0:T(8,128)(2,1)S(1)} %get-tuple-element.24), channel_id=1, source_target_pairs={{0,8},{4,12},{8,0},{12,4},{16,24},{20,28},{24,16},{28,20},{1,9},{5... | collective-permute-start | bytes 786440 | tf_op jit(solution)/shard_map/ppermute | solution.py:39
  23.8 1.1 %copy-start.3 = (bf16[1,4,256,256]{3,2,1,0:T(8,128)(2,1)S(1)}, bf16[1,4,256,256]{3,2,1,0:T(8,128)(2,1)}, u32[]{:S(2)}) copy-start(bf16[1,4,256,256]{3,2,1,0:T(8,128)(2,1)} %tiles_ref.1) | copy-start | bytes 1572868
  24.8 6.5 %collective-permute-start.7 = (bf16[2,256,512]{2,1,0:T(8,128)(2,1)S(1)}, bf16[2,256,512]{2,1,0:T(8,128)(2,1)S(1)}, u32[]{:S(2)}, u32[]{:S(2)}) collective-permute-start(bf16[2,256,512]{2,1,0:T(8,128)(2,1)S(1)} %get-tuple-element.22), channel_id=1, source_target_pairs={{0,4},{4,0},{8,12},{12,8},{16,20},{20,16},{24,28},{28,24},{1,5},{5... | collective-permute-start | bytes 1572872 | tf_op jit(solution)/shard_map/ppermute | solution.py:39
  27.9 5.6 %collective-permute-start.11 = (bf16[128,512]{1,0:T(8,128)(2,1)S(1)}, bf16[128,512]{1,0:T(8,128)(2,1)S(1)}, u32[]{:S(2)}, u32[]{:S(2)}) collective-permute-start(bf16[128,512]{1,0:T(8,128)(2,1)S(1)} %get-tuple-element.28), channel_id=1, source_target_pairs={{0,8},{4,12},{8,0},{12,4},{16,24},{20,28},{24,16},{28,20},{1,9},{5... | collective-permute-start | bytes 393224 | tf_op jit(solution)/shard_map/ppermute | solution.py:39
  31.1 9.5 %collective-permute-start.14 = (bf16[128,512]{1,0:T(8,128)(2,1)S(1)}, bf16[128,512]{1,0:T(8,128)(2,1)S(1)}, u32[]{:S(2)}, u32[]{:S(2)}) collective-permute-start(bf16[128,512]{1,0:T(8,128)(2,1)S(1)} %get-tuple-element.32), channel_id=1, source_target_pairs={{0,2},{1,3},{2,0},{3,1},{4,6},{5,7},{6,4},{7,5},{8,10},{9,11},{10,... | collective-permute-start | bytes 393224 | tf_op jit(solution)/shard_map/ppermute | solution.py:39
  31.4 7.4 %copy-start.4 = (s32[1,4]{1,0:T(1,128)S(1)}, s32[1,4]{1,0:T(1,128)}, u32[]{:S(2)}) copy-start(s32[1,4]{1,0:T(1,128)} %cols_ref.1) | copy-start | bytes 52
  31.4 7.4 %collective-permute-start.10 = (bf16[256,512]{1,0:T(8,128)(2,1)S(1)}, bf16[256,512]{1,0:T(8,128)(2,1)S(1)}, u32[]{:S(2)}, u32[]{:S(2)}) collective-permute-start(bf16[256,512]{1,0:T(8,128)(2,1)S(1)} %other.1.refs_2_), channel_id=1, source_target_pairs={{0,1},{1,0},{2,3},{3,2},{4,5},{5,4},{6,7},{7,6},{8,9},{9,8},{10,11... | collective-permute-start | bytes 786440 | tf_op jit(solution)/shard_map/ppermute | solution.py:39
  33.6 9.3 %collective-permute-start.16 = (bf16[128,512]{1,0:T(8,128)(2,1)S(1)}, bf16[128,512]{1,0:T(8,128)(2,1)S(1)}, u32[]{:S(2)}, u32[]{:S(2)}) collective-permute-start(bf16[128,512]{1,0:T(8,128)(2,1)S(1)} %sum_out.1.refs_0_), channel_id=1, source_target_pairs={{0,16},{4,20},{8,24},{12,28},{16,0},{20,4},{24,8},{28,12},{1,17},{... | collective-permute-start | bytes 393224 | tf_op jit(solution)/shard_map/ppermute | solution.py:39
  40.6 6.3 %collective-permute-start.15 = (bf16[128,512]{1,0:T(8,128)(2,1)S(1)}, bf16[128,512]{1,0:T(8,128)(2,1)S(1)}, u32[]{:S(2)}, u32[]{:S(2)}) collective-permute-start(bf16[128,512]{1,0:T(8,128)(2,1)S(1)} %sum_in.1.refs_2_.refs_0_), channel_id=1, source_target_pairs={{0,16},{4,20},{8,24},{12,28},{16,0},{20,4},{24,8},{28,12},{1,17},{... | collective-permute-start | bytes 393224 | tf_op jit(solution)/shard_map/ppermute | solution.py:39
  42.9 6.8 %collective-permute-start.21 = (bf16[128,512]{1,0:T(8,128)(2,1)S(1)}, bf16[128,512]{1,0:T(8,128)(2,1)S(1)}, u32[]{:S(2)}, u32[]{:S(2)}) collective-permute-start(bf16[128,512]{1,0:T(8,128)(2,1)S(1)} %add_out.1.refs_2_.refs_7_), channel_id=1, source_target_pairs={{0,8},{4,12},{8,0},{12,4},{16,24},{20,28},{24,16},{28,20},{1,9},{5... | collective-permute-start | bytes 393224 | tf_op jit(solution)/shard_map/ppermute | solution.py:39
  44.7 5.0 %collective-permute-start.20 = (bf16[128,512]{1,0:T(8,128)(2,1)S(1)}, bf16[128,512]{1,0:T(8,128)(2,1)S(1)}, u32[]{:S(2)}, u32[]{:S(2)}) collective-permute-start(bf16[128,512]{1,0:T(8,128)(2,1)S(1)} %add_out.1.refs_2_.refs_7_), channel_id=1, source_target_pairs={{0,4},{4,0},{8,12},{12,8},{16,20},{20,16},{24,28},{28,24},{1,5},{5... | collective-permute-start | bytes 393224 | tf_op jit(solution)/shard_map/ppermute | solution.py:39
  44.8 12.1 %collective-permute-start.12 = (bf16[256,512]{1,0:T(8,128)(2,1)S(1)}, bf16[256,512]{1,0:T(8,128)(2,1)S(1)}, u32[]{:S(2)}, u32[]{:S(2)}) collective-permute-start(bf16[256,512]{1,0:T(8,128)(2,1)S(1)} %get-tuple-element.30.refs_2_), channel_id=1, source_target_pairs={{0,28},{4,0},{8,4},{12,8},{16,12},{20,16},{24,20},{28,24},{1,29},{... | collective-permute-start | bytes 786440 | tf_op jit(solution)/shard_map/ppermute | solution.py:44
  45.7 11.2 %collective-permute-start.13 = (bf16[256,512]{1,0:T(8,128)(2,1)S(1)}, bf16[256,512]{1,0:T(8,128)(2,1)S(1)}, u32[]{:S(2)}, u32[]{:S(2)}) collective-permute-start(bf16[256,512]{1,0:T(8,128)(2,1)S(1)} %get-tuple-element.31), channel_id=1, source_target_pairs={{0,4},{4,8},{8,12},{12,16},{16,20},{20,24},{24,28},{28,0},{1,5},{5... | collective-permute-start | bytes 786440 | tf_op jit(solution)/shard_map/ppermute | solution.py:44
  47.0 9.8 %collective-permute-start.18 = (bf16[128,512]{1,0:T(8,128)(2,1)S(1)}, bf16[128,512]{1,0:T(8,128)(2,1)S(1)}, u32[]{:S(2)}, u32[]{:S(2)}) collective-permute-start(bf16[128,512]{1,0:T(8,128)(2,1)S(1)} %add_in.1.refs_3_), channel_id=1, source_target_pairs={{0,8},{4,12},{8,0},{12,4},{16,24},{20,28},{24,16},{28,20},{1,9},{5... | collective-permute-start | bytes 393224 | tf_op jit(solution)/shard_map/ppermute | solution.py:39
  49.7 7.1 %collective-permute-start.22 = (bf16[128,512]{1,0:T(8,128)(2,1)S(1)}, bf16[128,512]{1,0:T(8,128)(2,1)S(1)}, u32[]{:S(2)}, u32[]{:S(2)}) collective-permute-start(bf16[128,512]{1,0:T(8,128)(2,1)S(1)} %collective-permute-done.21.refs_9_), channel_id=1, source_target_pairs={{0,4},{4,0},{8,12},{12,8},{16,20},{20,16},{24,28},{28,24},{1,5},{5... | collective-permute-start | bytes 393224 | tf_op jit(solution)/shard_map/ppermute | solution.py:39
  49.7 7.1 %collective-permute-start.17 = (bf16[128,512]{1,0:T(8,128)(2,1)S(1)}, bf16[128,512]{1,0:T(8,128)(2,1)S(1)}, u32[]{:S(2)}, u32[]{:S(2)}) collective-permute-start(bf16[128,512]{1,0:T(8,128)(2,1)S(1)} %add_in.1.refs_3_), channel_id=1, source_target_pairs={{0,4},{4,0},{8,12},{12,8},{16,20},{20,16},{24,28},{28,24},{1,5},{5... | collective-permute-start | bytes 393224 | tf_op jit(solution)/shard_map/ppermute | solution.py:39
  56.9 1.3 %collective-permute-start.19 = (bf16[128,512]{1,0:T(8,128)(2,1)S(1)}, bf16[128,512]{1,0:T(8,128)(2,1)S(1)}, u32[]{:S(2)}, u32[]{:S(2)}) collective-permute-start(bf16[128,512]{1,0:T(8,128)(2,1)S(1)} %collective-permute-done.18.refs_5_), channel_id=1, source_target_pairs={{0,4},{4,0},{8,12},{12,8},{16,20},{20,16},{24,28},{28,24},{1,5},{5... | collective-permute-start | bytes 393224 | tf_op jit(solution)/shard_map/ppermute | solution.py:39
